TPU v7x, 32 devices: a whole 2x2x4 slice. The times are simulated.
32 devices in a mesh: dp: 8 (over y, x, core), mp: 4 (over z).
Axes of the slice: x: 2, y: 2, z: 4, core: 2. Of those that a mesh axis runs over, the one named last changes fastest.
Arguments:
- tokens: bfloat16 [256, 40, 768], P(('dp', 'mp')), may hold values from -6 to 6
- images: bfloat16 [256, 145, 1024], P(('dp', 'mp')), may hold values from -6 to 6
- segment_of_token: int32 [256, 40], P('dp'), may hold values from 0 to 3, never falling along the last dimension, each value on 1 to 20 neighbouring positions
- image_of_row: int32 [256], P('dp'), may hold values from 0 to 255, as said below
- attention_in: bfloat16 [3, 3, 768, 768], P(None, None, None, 'mp'), may hold values from -0.21875 to 0.21875
- query_value_bias: bfloat16 [3, 2, 768], P(None, None, 'mp'), may hold values from -3 to 3
- attention_out: bfloat16 [3, 768, 768], P(None, 'mp'), may hold values from -0.625 to 0.625
- output_bias: bfloat16 [5, 768], replicated, may hold values from -2 to 2
- feed_in: bfloat16 [2, 768, 3072], P(None, None, 'mp'), may hold values from -0.21875 to 0.21875
- feed_bias: bfloat16 [2, 3072], P(None, 'mp'), may hold values from -3 to 3
- feed_out: bfloat16 [2, 3072, 768], P(None, 'mp'), may hold values from -0.109375 to 0.109375
- image_weight: bfloat16 [1024, 768], P(None, 'mp'), may hold values from -0.1875 to 0.1875
- image_bias: bfloat16 [768], P('mp'), may hold values from -2 to 2
- norm_gain: bfloat16 [5, 768], replicated, may hold values from 0.5 to 1.5
- norm_bias: bfloat16 [5, 768], replicated, may hold values from -2 to 2
- cotangent: bfloat16 [256, 40, 768], P(('dp', 'mp')), may hold values from -6 to 6
Outputs:
- mixed_out: float32 [256, 40, 768], P(('dp', 'mp'))
- grad_tokens: float32 [256, 40, 768], P(('dp', 'mp'))
- grad_images: float32 [256, 145, 1024], P(('dp', 'mp'))
- grad_attention_in: float32 [3, 3, 768, 768], P(None, None, None, 'mp')
- grad_query_value_bias: float32 [3, 2, 768], P(None, None, 'mp')
- grad_attention_out: float32 [3, 768, 768], P(None, 'mp')
- grad_output_bias: float32 [5, 768], replicated
- grad_feed_in: float32 [2, 768, 3072], P(None, None, 'mp')
- grad_feed_bias: float32 [2, 3072], P(None, 'mp')
- grad_feed_out: float32 [2, 3072, 768], P(None, 'mp')
- grad_image_weight: float32 [1024, 768], P(None, 'mp')
- grad_image_bias: float32 [768], P('mp')
- grad_norm_gain: float32 [5, 768], replicated
- grad_norm_bias: float32 [5, 768], replicated
Inputs may be any that keep to these rules, and one draw needn't show every extreme that they name: `image_of_row`: within each aligned block of 32 rows the entries are a permutation of that block's row numbers: each row uses one image of its own block. `segment_of_token`: along a row the numbers never fall; a token attends to the tokens of its row with the same number.
All inputs are finite; a program needn't handle non-finite values.
Results may differ from a plain program's by a relative error of at most 0.03.
Values may be sent and summed in bfloat16 or wider, within the bound.
No kernel may reach another device: no remote copies, remote signals or barrier semaphores. Data moves between devices by JAX's collectives and lax.ppermute only.
A program may use at most 256 MiB of HBM per device.

v0:
```python
from functools import partial

import jax
import jax.numpy as jnp
from jax import lax
from jax.sharding import PartitionSpec as P

HEAD_DIM = 64


epsilon = 1e-06
blocked = -1000000000.0


def norm_rows(values, gain_row, shift_row):
    center = values - jnp.mean(values, axis=-1, keepdims=True)
    moment = jnp.mean(center * center, axis=-1, keepdims=True)
    return center * lax.rsqrt(moment + epsilon) * gain_row + shift_row


def norm_back(pre_norm, gain_row, shift_row, grad_out):
    _, norm_pull = jax.vjp(
        norm_rows, pre_norm, gain_row.astype(jnp.float32), shift_row.astype(jnp.float32)
    )
    return norm_pull(grad_out)


def split_heads(values):
    return values.reshape(values.shape[:-1] + (values.shape[-1] // HEAD_DIM, HEAD_DIM))


def merge_heads(values):
    return values.reshape(values.shape[:-2] + (values.shape[-2] * values.shape[-1],))


def product(values, weight):
    return jnp.dot(values, weight, preferred_element_type=jnp.float32)


def product_back(values, weight):
    return jnp.einsum("...n,kn->...k", values, weight, preferred_element_type=jnp.float32)


def outer_sum(left_rows, right_rows):
    left_flat = left_rows.reshape(-1, left_rows.shape[-1])
    right_flat = right_rows.reshape(-1, right_rows.shape[-1])
    return lax.dot_general(
        left_flat, right_flat, (((0,), (0,)), ((), ())), preferred_element_type=jnp.float32
    )


def column_total(values):
    return jnp.sum(values.astype(jnp.float32).reshape(-1, values.shape[-1]), axis=0)


def spread(values):
    return lax.all_gather(values, "mp", axis=0, tiled=True)


def spread_grad(values):
    return lax.all_gather(values, "mp", axis=0, tiled=True)


def settle(row_fn, own_rows):
    return lax.psum_scatter(
        row_fn(jnp.int32(0), lax.axis_size("mp") * own_rows), "mp", scatter_dimension=0, tiled=True
    )


def settle_grad(row_fn, own_rows):
    return lax.psum_scatter(
        row_fn(jnp.int32(0), lax.axis_size("mp") * own_rows), "mp", scatter_dimension=0, tiled=True
    )


def attention_scores(query_rows, key_rows, allowed):
    scores = jnp.einsum(
        "rqhe,rkhe->rhqk", query_rows, key_rows, preferred_element_type=jnp.float32
    ) * HEAD_DIM ** (-0.5)
    if allowed is not None:
        scores = jnp.where(allowed[:, None], scores, blocked)
    return scores


def attend_forward(query_rows, key_rows, value_rows, allowed):
    scores = attention_scores(query_rows, key_rows, allowed)
    row_top = jnp.max(scores, axis=-1, keepdims=True)
    log_total = jnp.log(jnp.sum(jnp.exp(scores - row_top), axis=-1, keepdims=True)) + row_top
    weights = jnp.exp(scores - log_total).astype(jnp.bfloat16)
    context = jnp.einsum("rhqk,rkhe->rqhe", weights, value_rows, preferred_element_type=jnp.float32)
    return (context.astype(jnp.bfloat16), log_total)


def attend_backward(query_rows, key_rows, value_rows, allowed, log_total, grad_context):
    scores = attention_scores(query_rows, key_rows, allowed)
    weights = jnp.exp(scores - log_total)
    grad_weights = jnp.einsum(
        "rqhe,rkhe->rhqk", grad_context, value_rows, preferred_element_type=jnp.float32
    )
    grad_scores = (
        weights * (grad_weights - jnp.sum(weights * grad_weights, axis=-1, keepdims=True))
    ).astype(jnp.bfloat16)
    score_scale = HEAD_DIM ** (-0.5)
    grad_query = (
        jnp.einsum("rhqk,rkhe->rqhe", grad_scores, key_rows, preferred_element_type=jnp.float32)
        * score_scale
    ).astype(jnp.bfloat16)
    grad_keys = (
        jnp.einsum("rhqk,rqhe->rkhe", grad_scores, query_rows, preferred_element_type=jnp.float32)
        * score_scale
    ).astype(jnp.bfloat16)
    grad_values = jnp.einsum(
        "rhqk,rqhe->rkhe",
        weights.astype(jnp.bfloat16),
        grad_context,
        preferred_element_type=jnp.float32,
    ).astype(jnp.bfloat16)
    return (merge_heads(grad_query), merge_heads(grad_keys), merge_heads(grad_values))


def attention_forward(
    stream, source, weight_in, bias_pair, weight_out, bias_out, gain_row, shift_row, allowed
):
    gathered = spread(stream.astype(jnp.bfloat16))
    source_rows = gathered if source is None else source
    query_rows = (product(gathered, weight_in[0]) + bias_pair[0]).astype(jnp.bfloat16)
    key_rows = product(source_rows, weight_in[1]).astype(jnp.bfloat16)
    value_rows = (product(source_rows, weight_in[2]) + bias_pair[1]).astype(jnp.bfloat16)
    context, log_total = attend_forward(
        split_heads(query_rows), split_heads(key_rows), split_heads(value_rows), allowed
    )
    context = merge_heads(context)

    def attention_out_rows(first_row, row_count):
        return product(context, weight_out)

    pre_norm = settle(attention_out_rows, stream.shape[0]) + bias_out + stream
    kept_state = (
        gathered,
        source_rows,
        query_rows,
        key_rows,
        value_rows,
        log_total,
        context,
        pre_norm,
    )
    return (norm_rows(pre_norm, gain_row, shift_row), kept_state)


def attention_backward(
    kept_state, grad_out, weight_in, weight_out, gain_row, shift_row, allowed, cross
):
    gathered, source_rows, query_rows, key_rows, value_rows, log_total, context, pre_norm = (
        kept_state
    )
    grad_pre, grad_gain, grad_shift = norm_back(pre_norm, gain_row, shift_row, grad_out)
    grad_branch = spread_grad(grad_pre.astype(jnp.bfloat16))
    grad_weight_out = outer_sum(context, grad_branch)
    grad_context = product_back(grad_branch, weight_out).astype(jnp.bfloat16)
    grad_query, grad_keys, grad_values = attend_backward(
        split_heads(query_rows),
        split_heads(key_rows),
        split_heads(value_rows),
        allowed,
        log_total,
        split_heads(grad_context),
    )
    grad_weight_in = jnp.stack(
        [
            outer_sum(gathered, grad_query),
            outer_sum(source_rows, grad_keys),
            outer_sum(source_rows, grad_values),
        ]
    )
    grad_bias_pair = jnp.stack([column_total(grad_query), column_total(grad_values)])

    def attention_back_rows(first_row, row_count):
        row_term = product_back(grad_query, weight_in[0])
        if not cross:
            row_term = row_term + product_back(grad_keys, weight_in[1])
            row_term = row_term + product_back(grad_values, weight_in[2])
        return row_term

    grad_stream = settle_grad(attention_back_rows, grad_out.shape[0]) + grad_pre
    grad_list = (
        grad_weight_in,
        grad_bias_pair,
        grad_weight_out,
        column_total(grad_pre),
        grad_gain,
        grad_shift,
    )
    return (grad_stream, grad_list, (grad_keys, grad_values))


def feed_forward(stream, weight_in, bias_in, weight_out, bias_out, gain_row, shift_row):
    gathered = spread(stream.astype(jnp.bfloat16))
    inner_rows = product(gathered, weight_in) + bias_in
    active = jax.nn.gelu(inner_rows, approximate=False).astype(jnp.bfloat16)

    def feed_out_rows(first_row, row_count):
        return product(active, weight_out)

    pre_norm = settle(feed_out_rows, stream.shape[0]) + bias_out + stream
    return (norm_rows(pre_norm, gain_row, shift_row), (gathered, inner_rows, active, pre_norm))


def feed_backward(kept_state, grad_out, weight_in, weight_out, gain_row, shift_row):
    gathered, inner_rows, active, pre_norm = kept_state
    grad_pre, grad_gain, grad_shift = norm_back(pre_norm, gain_row, shift_row, grad_out)
    grad_branch = spread_grad(grad_pre.astype(jnp.bfloat16))
    grad_weight_out = outer_sum(active, grad_branch)
    grad_active = product_back(grad_branch, weight_out)
    _, gelu_pull = jax.vjp(partial(jax.nn.gelu, approximate=False), inner_rows)
    grad_inner = gelu_pull(grad_active)[0].astype(jnp.bfloat16)

    def feed_back_rows(first_row, row_count):
        return product_back(grad_inner, weight_in)

    grad_stream = settle_grad(feed_back_rows, grad_out.shape[0]) + grad_pre
    grad_list = (
        outer_sum(gathered, grad_inner),
        column_total(grad_inner),
        grad_weight_out,
        column_total(grad_pre),
        grad_gain,
        grad_shift,
    )
    return (grad_stream, grad_list)


def on_device(
    tokens,
    images,
    segment_of_token,
    image_of_row,
    attention_in,
    query_value_bias,
    attention_out,
    output_bias,
    feed_in,
    feed_bias,
    feed_out,
    image_weight,
    image_bias,
    norm_gain,
    norm_bias,
    cotangent,
):
    group_rows = segment_of_token.shape[0]
    allowed = segment_of_token[:, :, None] == segment_of_token[:, None, :]
    local_order = image_of_row % group_rows
    stream, text_attention = attention_forward(
        tokens.astype(jnp.float32),
        None,
        attention_in[0],
        query_value_bias[0],
        attention_out[0],
        output_bias[0],
        norm_gain[0],
        norm_bias[0],
        allowed,
    )
    stream, text_feed = feed_forward(
        stream, feed_in[0], feed_bias[0], feed_out[0], output_bias[1], norm_gain[1], norm_bias[1]
    )
    stream, joining_attention = attention_forward(
        stream,
        None,
        attention_in[1],
        query_value_bias[1],
        attention_out[1],
        output_bias[2],
        norm_gain[2],
        norm_bias[2],
        allowed,
    )
    group_images = lax.all_gather(images, "mp", axis=0, tiled=True)
    columns = (product(group_images, image_weight) + image_bias).astype(jnp.bfloat16)
    group_projected = lax.all_gather(columns, "mp", axis=2, tiled=True)
    picked = jnp.take(group_projected, local_order, axis=0)
    stream, cross_attention = attention_forward(
        stream,
        picked,
        attention_in[2],
        query_value_bias[2],
        attention_out[2],
        output_bias[3],
        norm_gain[3],
        norm_bias[3],
        None,
    )
    stream, joining_feed = feed_forward(
        stream, feed_in[1], feed_bias[1], feed_out[1], output_bias[4], norm_gain[4], norm_bias[4]
    )
    grad_stream = cotangent.astype(jnp.float32)
    grad_stream, joining_feed_grads = feed_backward(
        joining_feed, grad_stream, feed_in[1], feed_out[1], norm_gain[4], norm_bias[4]
    )
    grad_stream, cross_grads, source_grads = attention_backward(
        cross_attention,
        grad_stream,
        attention_in[2],
        attention_out[2],
        norm_gain[3],
        norm_bias[3],
        None,
        True,
    )
    positions = jnp.arange(group_rows, dtype=jnp.int32)
    inverse = jnp.zeros((group_rows,), jnp.int32).at[local_order].set(positions)
    key_image = jnp.take(source_grads[0], inverse, axis=0)
    value_image = jnp.take(source_grads[1], inverse, axis=0)
    full_grad = product_back(key_image, attention_in[2][1]) + product_back(
        value_image, attention_in[2][2]
    )
    grad_columns = lax.psum_scatter(full_grad, "mp", scatter_dimension=2, tiled=True).astype(
        jnp.bfloat16
    )
    grad_image_weight = outer_sum(group_images, grad_columns)
    grad_image_bias = column_total(grad_columns)
    grad_images = lax.psum_scatter(
        product_back(grad_columns, image_weight), "mp", scatter_dimension=0, tiled=True
    )
    grad_stream, joining_attention_grads, unused_source = attention_backward(
        joining_attention,
        grad_stream,
        attention_in[1],
        attention_out[1],
        norm_gain[2],
        norm_bias[2],
        allowed,
        False,
    )
    grad_stream, text_feed_grads = feed_backward(
        text_feed, grad_stream, feed_in[0], feed_out[0], norm_gain[1], norm_bias[1]
    )
    grad_stream, text_attention_grads, unused_text = attention_backward(
        text_attention,
        grad_stream,
        attention_in[0],
        attention_out[0],
        norm_gain[0],
        norm_bias[0],
        allowed,
        False,
    )
    attention_grads = (text_attention_grads, joining_attention_grads, cross_grads)
    feed_grads = (text_feed_grads, joining_feed_grads)
    grad_attention_in = jnp.stack([entry[0] for entry in attention_grads])
    grad_query_value_bias = jnp.stack([entry[1] for entry in attention_grads])
    grad_attention_out = jnp.stack([entry[2] for entry in attention_grads])
    grad_feed_in = jnp.stack([entry[0] for entry in feed_grads])
    grad_feed_bias = jnp.stack([entry[1] for entry in feed_grads])
    grad_feed_out = jnp.stack([entry[2] for entry in feed_grads])
    layer_order = (
        text_attention_grads,
        text_feed_grads,
        joining_attention_grads,
        cross_grads,
        joining_feed_grads,
    )
    grad_output_bias = jnp.stack([entry[3] for entry in layer_order])
    grad_norm_gain = jnp.stack([entry[4] for entry in layer_order])
    grad_norm_bias = jnp.stack([entry[5] for entry in layer_order])
    sharded = lax.psum(
        (
            grad_attention_in,
            grad_query_value_bias,
            grad_attention_out,
            grad_feed_in,
            grad_feed_bias,
            grad_feed_out,
            grad_image_weight,
            grad_image_bias,
        ),
        "dp",
    )
    shared = lax.psum((grad_output_bias, grad_norm_gain, grad_norm_bias), ("dp", "mp"))
    return (
        stream,
        grad_stream,
        grad_images,
        sharded[0],
        sharded[1],
        sharded[2],
        shared[0],
        sharded[3],
        sharded[4],
        sharded[5],
        sharded[6],
        sharded[7],
        shared[1],
        shared[2],
    )


def solution(mesh):
    return jax.shard_map(
        on_device,
        mesh=mesh,
        in_specs=(
            P(("dp", "mp"), None, None),
            P(("dp", "mp"), None, None),
            P("dp", None),
            P("dp"),
            P(None, None, None, "mp"),
            P(None, None, "mp"),
            P(None, "mp", None),
            P(),
            P(None, None, "mp"),
            P(None, "mp"),
            P(None, "mp", None),
            P(None, "mp"),
            P("mp"),
            P(),
            P(),
            P(("dp", "mp"), None, None),
        ),
        out_specs=(
            P(("dp", "mp"), None, None),
            P(("dp", "mp"), None, None),
            P(("dp", "mp"), None, None),
            P(None, None, None, "mp"),
            P(None, None, "mp"),
            P(None, "mp", None),
            P(),
            P(None, None, "mp"),
            P(None, "mp"),
            P(None, "mp", None),
            P(None, "mp"),
            P("mp"),
            P(),
            P(),
        ),
        check_vma=False,
    )
```

profile of v0, /device:TPU:0, one launch (start us, length us, event | category | flops | bytes accessed | tf_op | source)
XLA Modules:
  0.0 2642.6 jit_solution(5430359881609607527)
XLA Ops:
  10.4 45.5 %all-gather.17.cloned.1.call-done = bf16[32,40,768]{2,1,0:T(8,128)(2,1)} async-done(((bf16[8,40,768]{2,1,0:T(8,128)(2,1)}), bf16[32,40,768]{2,1,0:T(8,128)(2,1)}) %all-gather.17.cloned.1.call-update) | async-done | bytes 1966096 | tf_op jit(solution)/shard_map/all_gather | solution.py:57
  74.9 70.3 %reduce-scatter.15.cloned.1.call-done = f32[8,40,768]{2,1,0:T(8,128)} async-done(((f32[32,40,768]{2,1,0:T(8,128)}), f32[8,40,768]{2,1,0:T(8,128)}) %reduce-scatter.15.cloned.1.call-update) | async-done | bytes 983056 | tf_op jit(solution)/shard_map/reduce_scatter | solution.py:65
  148.2 43.7 %all-gather.19.cloned.1.call-done = bf16[32,40,768]{2,1,0:T(8,128)(2,1)} async-done(((bf16[8,40,768]{2,1,0:T(8,128)(2,1)}), bf16[32,40,768]{2,1,0:T(8,128)(2,1)}) %all-gather.19.cloned.1.call-update) | async-done | bytes 1966096 | tf_op jit(solution)/shard_map/all_gather | solution.py:57
  211.3 71.6 %reduce-scatter.17.cloned.1.call-done = f32[8,40,768]{2,1,0:T(8,128)} async-done(((f32[32,40,768]{2,1,0:T(8,128)}), f32[8,40,768]{2,1,0:T(8,128)}) %reduce-scatter.17.cloned.1.call-update) | async-done | bytes 983056 | tf_op jit(solution)/shard_map/reduce_scatter | solution.py:65
  287.1 43.4 %all-gather.21.cloned.1.call-done = bf16[32,40,768]{2,1,0:T(8,128)(2,1)} async-done(((bf16[8,40,768]{2,1,0:T(8,128)(2,1)}), bf16[32,40,768]{2,1,0:T(8,128)(2,1)}) %all-gather.21.cloned.1.call-update) | async-done | bytes 1966096 | tf_op jit(solution)/shard_map/all_gather | solution.py:57
  355.2 143.5 %all-gather.13.cloned.1.call-done = bf16[32,145,1024]{2,0,1:T(8,128)(2,1)} async-done(((bf16[8,145,1024]{2,0,1:T(8,128)(2,1)}), bf16[32,145,1024]{2,0,1:T(8,128)(2,1)}) %all-gather.13.cloned.1.call-update) | async-done | bytes 9502736 | tf_op jit(solution)/shard_map/all_gather | solution.py:279
  520.5 52.0 %reduce-scatter.19.cloned.1.call-done = f32[8,40,768]{2,1,0:T(8,128)} async-done(((f32[32,40,768]{2,1,0:T(8,128)}), f32[8,40,768]{2,1,0:T(8,128)}) %reduce-scatter.19.cloned.1.call-update) | async-done | bytes 983056 | tf_op jit(solution)/shard_map/reduce_scatter | solution.py:65
  576.6 216.7 %all-gather.15.cloned.1.call-done = bf16[32,145,768]{1,0,2:T(8,128)(2,1)} async-done(((bf16[32,145,192]{1,0,2:T(8,128)(2,1)}), bf16[32,145,768]{1,0,2:T(8,128)(2,1)}) %all-gather.15.cloned.1.call-update) | async-done | bytes 7127056 | tf_op jit(solution)/shard_map/all_gather | solution.py:281
  867.5 70.8 %reduce-scatter.21.cloned.1.call-done = f32[8,40,768]{2,1,0:T(8,128)} async-done(((f32[32,40,768]{2,1,0:T(8,128)}), f32[8,40,768]{2,1,0:T(8,128)}) %reduce-scatter.21.cloned.1.call-update) | async-done | bytes 983056 | tf_op jit(solution)/shard_map/reduce_scatter | solution.py:65
  942.3 44.0 %all-gather.25.cloned.1.call-done = bf16[32,40,768]{2,1,0:T(8,128)(2,1)} async-done(((bf16[8,40,768]{2,1,0:T(8,128)(2,1)}), bf16[32,40,768]{2,1,0:T(8,128)(2,1)}) %all-gather.25.cloned.1.call-update) | async-done | bytes 1966096 | tf_op jit(solution)/shard_map/all_gather | solution.py:57
  1005.7 71.6 %reduce-scatter.23.cloned.1.call-done = f32[8,40,768]{2,1,0:T(8,128)} async-done(((f32[32,40,768]{2,1,0:T(8,128)}), f32[8,40,768]{2,1,0:T(8,128)}) %reduce-scatter.23.cloned.1.call-update) | async-done | bytes 983056 | tf_op jit(solution)/shard_map/reduce_scatter | solution.py:65
  1083.0 43.6 %all-gather.27.cloned.1.call-done = bf16[32,40,768]{2,1,0:T(8,128)(2,1)} async-done(((bf16[8,40,768]{2,1,0:T(8,128)(2,1)}), bf16[32,40,768]{2,1,0:T(8,128)(2,1)}) %all-gather.27.cloned.1.call-update) | async-done | bytes 1966096 | tf_op jit(solution)/shard_map/all_gather | solution.py:61
  1139.5 71.6 %reduce-scatter.25.cloned.1.call-done = f32[8,40,768]{2,1,0:T(8,128)} async-done(((f32[32,40,768]{2,1,0:T(8,128)}), f32[8,40,768]{2,1,0:T(8,128)}) %reduce-scatter.25.cloned.1.call-update) | async-done | bytes 983056 | tf_op jit(solution)/shard_map/reduce_scatter | solution.py:71
  1218.7 44.0 %all-gather.29.cloned.1.call-done = bf16[32,40,768]{2,1,0:T(8,128)(2,1)} async-done(((bf16[8,40,768]{2,1,0:T(8,128)(2,1)}), bf16[32,40,768]{2,1,0:T(8,128)(2,1)}) %all-gather.29.cloned.1.call-update) | async-done | bytes 1966096 | tf_op jit(solution)/shard_map/all_gather | solution.py:61
  1287.6 71.4 %reduce-scatter.27.cloned.1.call-done = f32[8,40,768]{2,1,0:T(8,128)} async-done(((f32[32,40,768]{2,1,0:T(8,128)}), f32[8,40,768]{2,1,0:T(8,128)}) %reduce-scatter.27.cloned.1.call-update) | async-done | bytes 983056 | tf_op jit(solution)/shard_map/reduce_scatter | solution.py:71
  1365.0 44.0 %all-gather.31.cloned.1.call-done = bf16[32,40,768]{2,1,0:T(8,128)(2,1)} async-done(((bf16[8,40,768]{2,1,0:T(8,128)(2,1)}), bf16[32,40,768]{2,1,0:T(8,128)(2,1)}) %all-gather.31.cloned.1.call-update) | async-done | bytes 1966096 | tf_op jit(solution)/shard_map/all_gather | solution.py:61
  1443.6 71.6 %reduce-scatter.29.cloned.1.call-done = f32[8,40,768]{2,1,0:T(8,128)} async-done(((f32[32,40,768]{2,1,0:T(8,128)}), f32[8,40,768]{2,1,0:T(8,128)}) %reduce-scatter.29.cloned.1.call-update) | async-done | bytes 983056 | tf_op jit(solution)/shard_map/reduce_scatter | solution.py:71
  1520.1 43.6 %all-gather.33.cloned.1.call-done = bf16[32,40,768]{2,1,0:T(8,128)(2,1)} async-done(((bf16[8,40,768]{2,1,0:T(8,128)(2,1)}), bf16[32,40,768]{2,1,0:T(8,128)(2,1)}) %all-gather.33.cloned.1.call-update) | async-done | bytes 1966096 | tf_op jit(solution)/shard_map/all_gather | solution.py:61
  1577.5 70.8 %reduce-scatter.31.cloned.1.call-done = f32[8,40,768]{2,1,0:T(8,128)} async-done(((f32[32,40,768]{2,1,0:T(8,128)}), f32[8,40,768]{2,1,0:T(8,128)}) %reduce-scatter.31.cloned.1.call-update) | async-done | bytes 983056 | tf_op jit(solution)/shard_map/reduce_scatter | solution.py:71
  1766.7 213.2 %reduce-scatter.37.cloned.1.call-done = f32[192,4640]{1,0:T(8,128)} async-done(((f32[768,4640]{1,0:T(8,128)}), f32[192,4640]{1,0:T(8,128)}) %reduce-scatter.37.cloned.1.call-update) | async-done | bytes 3563536
  2136.1 48.2 %all-reduce = (f32[5,768]{1,0:T(8,128)}, f32[5,768]{1,0:T(8,128)}, f32[5,768]{1,0:T(8,128)}) all-reduce(f32[5,768]{1,0:T(8,128)S(1)} %stack.218, f32[5,768]{1,0:T(8,128)S(1)} %stack.233, f32[5,768]{1,0:T(8,128)S(1)} %stack.239), channel_id=1, replica_groups=mesh['dp'=8,'mp'=4] {'dp','mp'}, use_global_device_ids=true, to_apply=%region_56.58 | all-reduce | flops 11520 | bytes 92160 | tf_op jit(solution)/shard_map/psum | solution.py:380
  2184.4 25.2 all-reduce.1
  2212.3 178.5 %reduce-scatter.35.cloned.1.call-done = f32[8,145,1024]{2,1,0:T(8,128)} async-done(((f32[32,145,1024]{2,1,0:T(8,128)}), f32[8,145,1024]{2,1,0:T(8,128)}) %reduce-scatter.35.cloned.1.call-update) | async-done | bytes 4751376 | tf_op jit(solution)/shard_map/reduce_scatter | solution.py:323
  2398.2 224.3 %all-reduce.5.cloned.1.call-done = (f32[3,3,768,192]{2,3,1,0:T(8,128)}, f32[3,192,768]{2,1,0:T(8,128)}, f32[2,768,768]{2,1,0:T(8,128)}, f32[2,768,768]{2,1,0:T(8,128)}, f32[1024,192]{0,1:T(8,128)}) async-done(((f32[3,3,768,192]{2,3,1,0:T(8,128)}, f32[3,192,768]{2,1,0:T(8,128)}, f32[2,768,768]{2,1,0:T(8,128)}, f32[2,768,768]{2,1,0:T(8,128)}, f32[1024,192]{0,1:T(8,128)}), (f32[3,3,768,192]{2,3,1,0:T(8,128)}, ...) | async-done | bytes 17301520 | tf_op jit(solution)/shard_map/psum | solution.py:367
  (538 shorter events, 602.9 us)
Async XLA Ops:
  7.9 137.3 %reduce-scatter.15.cloned.1.call-start = ((), (), s32[]{:S(2)}) async-start(), calls=%async_computation.15 | async-start | bytes 4915200 | tf_op jit(solution)/shard_map/reduce_scatter | solution.py:65
  73.5 118.4 %all-gather.19.cloned.1.call-start = ((), (), s32[]{:S(2)}) async-start(), calls=%async_computation.16 | async-start | bytes 2457600 | tf_op jit(solution)/shard_map/all_gather | solution.py:57
  147.9 135.0 %reduce-scatter.17.cloned.1.call-start = ((), (), s32[]{:S(2)}) async-start(), calls=%async_computation.17 | async-start | bytes 4915200 | tf_op jit(solution)/shard_map/reduce_scatter | solution.py:65
  211.2 119.3 %all-gather.21.cloned.1.call-start = ((), (), s32[]{:S(2)}) async-start(), calls=%async_computation.18 | async-start | bytes 2457600 | tf_op jit(solution)/shard_map/all_gather | solution.py:57
  286.5 212.2 %all-gather.13.cloned.1.call-start = ((), (), s32[]{:S(2)}) async-start(), calls=%async_computation.12 | async-start | bytes 11878400 | tf_op jit(solution)/shard_map/all_gather | solution.py:279
  287.1 285.4 %reduce-scatter.19.cloned.1.call-start = ((), (), s32[]{:S(2)}) async-start(), calls=%async_computation.19 | async-start | bytes 4915200 | tf_op jit(solution)/shard_map/reduce_scatter | solution.py:65
  354.6 438.6 %all-gather.15.cloned.1.call-start = ((), (), s32[]{:S(2)}) async-start(), calls=%async_computation.13 | async-start | bytes 15728640 | tf_op jit(solution)/shard_map/all_gather | solution.py:281
  520.4 323.3 %all-gather.23.cloned.1.call-start = ((), (), s32[]{:S(2)}) async-start(), calls=%async_computation.20 | async-start | bytes 2457600 | tf_op jit(solution)/shard_map/all_gather | solution.py:57
  576.5 361.8 %reduce-scatter.21.cloned.1.call-start = ((), (), s32[]{:S(2)}) async-start(), calls=%async_computation.21 | async-start | bytes 4915200 | tf_op jit(solution)/shard_map/reduce_scatter | solution.py:65
  867.2 119.0 %all-gather.25.cloned.1.call-start = ((), (), s32[]{:S(2)}) async-start(), calls=%async_computation.22 | async-start | bytes 2457600 | tf_op jit(solution)/shard_map/all_gather | solution.py:57
  942.2 135.1 %reduce-scatter.23.cloned.1.call-start = ((), (), s32[]{:S(2)}) async-start(), calls=%async_computation.23 | async-start | bytes 4915200 | tf_op jit(solution)/shard_map/reduce_scatter | solution.py:65
  1005.6 120.9 %all-gather.27.cloned.1.call-start = ((), (), s32[]{:S(2)}) async-start(), calls=%async_computation.24 | async-start | bytes 2457600 | tf_op jit(solution)/shard_map/all_gather | solution.py:61
  1082.5 128.6 %reduce-scatter.25.cloned.1.call-start = ((), (), s32[]{:S(2)}) async-start(), calls=%async_computation.25 | async-start | bytes 4915200 | tf_op jit(solution)/shard_map/reduce_scatter | solution.py:71
  1139.5 123.2 %all-gather.29.cloned.1.call-start = ((), (), s32[]{:S(2)}) async-start(), calls=%async_computation.26 | async-start | bytes 2457600 | tf_op jit(solution)/shard_map/all_gather | solution.py:61
  1218.6 140.4 %reduce-scatter.27.cloned.1.call-start = ((), (), s32[]{:S(2)}) async-start(), calls=%async_computation.27 | async-start | bytes 4915200 | tf_op jit(solution)/shard_map/reduce_scatter | solution.py:71
  1287.3 121.7 %all-gather.31.cloned.1.call-start = ((), (), s32[]{:S(2)}) async-start(), calls=%async_computation.28 | async-start | bytes 2457600 | tf_op jit(solution)/shard_map/all_gather | solution.py:61
  1365.0 150.3 %reduce-scatter.29.cloned.1.call-start = ((), (), s32[]{:S(2)}) async-start(), calls=%async_computation.29 | async-start | bytes 4915200 | tf_op jit(solution)/shard_map/reduce_scatter | solution.py:71
  1443.6 120.1 %all-gather.33.cloned.1.call-start = ((), (), s32[]{:S(2)}) async-start(), calls=%async_computation.30 | async-start | bytes 2457600 | tf_op jit(solution)/shard_map/all_gather | solution.py:61
  1519.6 128.7 %reduce-scatter.31.cloned.1.call-start = ((), (), s32[]{:S(2)}) async-start(), calls=%async_computation.31 | async-start | bytes 4915200 | tf_op jit(solution)/shard_map/reduce_scatter | solution.py:71
  1576.6 159.4 %all-gather.35.cloned.1.call-start = ((), (), s32[]{:S(2)}) async-start(), calls=%async_computation.32 | async-start | bytes 2457600 | tf_op jit(solution)/shard_map/all_gather | solution.py:61
  1653.5 326.3 %reduce-scatter.37.cloned.1.call-start = ((), (), s32[]{:S(2)}) async-start(), calls=%async_computation.35 | async-start | bytes 18186240
  1735.8 473.8 %reduce-scatter.33.cloned.1.call-start = ((), (), s32[]{:S(2)}) async-start(), calls=%async_computation.33 | async-start | bytes 4915200 | tf_op jit(solution)/shard_map/reduce_scatter | solution.py:71
  1766.6 624.2 %reduce-scatter.35.cloned.1.call-start = ((), (), s32[]{:S(2)}) async-start(), calls=%async_computation.34 | async-start | bytes 24903680 | tf_op jit(solution)/shard_map/reduce_scatter | solution.py:323
  2003.2 619.3 %all-reduce.5.cloned.1.call-start = ((), (), s32[]{:S(2)}) async-start(), calls=%async_computation.36 | async-start | bytes 34603008 | tf_op jit(solution)/shard_map/psum | solution.py:367
  (120 other events, 2778.5 us)
Sparse Core Ops, SparseCore 0:
  9.6 46.2 all-gather.16
  73.6 71.5 reduce-scatter.14
  148.0 43.8 all-gather.18
  211.4 71.5 reduce-scatter.16
  286.6 43.9 all-gather.20
  332.0 166.6 all-gather.12
  501.6 70.8 reduce-scatter.18
  574.7 218.5 all-gather.14
  867.4 70.8 reduce-scatter.20
  942.3 43.8 all-gather.24
  1005.8 71.5 reduce-scatter.22
  1082.7 43.8 all-gather.26
  1139.6 71.5 reduce-scatter.24
  1218.7 43.9 all-gather.28
  1287.5 71.5 reduce-scatter.26
  1365.1 43.8 all-gather.30
  1443.7 71.5 reduce-scatter.28
  1519.7 43.9 all-gather.32
  1576.8 71.5 reduce-scatter.30
  1653.7 43.8 all-gather.34
  1735.9 243.9 reduce-scatter.36
  1982.9 73.7 reduce-scatter.32
  2059.0 331.8 reduce-scatter.34
  2396.7 225.8 all-reduce.4
  (1 shorter events, 41.7 us)
where the time goes:
time: 2650 us; the launch traced here: 2640 us
  waiting for transfers between devices  1950 us (74%)
  local copies, waits for them, and re-layouts  282 us (11%)
  matrix products  232 us (9%)
  other arithmetic  83.5 us (3%)
  blocking collectives  73.4 us (3%)
    reduce_scatter x5, waiting for transfers between devices, settle(): lax.psum_scatter(row_fn(jnp.int32(0), lax.axis_size('mp') * own_rows), 'm...  336 us
    reduce_scatter x5, waiting for transfers between devices, settle_grad(): lax.psum_scatter(row_fn(jnp.int32(0), lax.axis_size('mp') * own_rows), 'm...  286 us
    psum x1, waiting for transfers between devices, on_device(): lax.psum((grad_attention_in, grad_query_value_bias, grad_attention_out, g...  224 us
    all_gather x1, waiting for transfers between devices, on_device(): group_projected = lax.all_gather(columns, 'mp', axis=2, tiled=True)  217 us
    unnamed x26, waiting for transfers between devices  215 us
    reduce_scatter x1, waiting for transfers between devices, on_device(): lax.psum_scatter(product_back(grad_columns, image_weight), 'mp', scatter_...  178 us
    all_gather x5, waiting for transfers between devices, spread(): return lax.all_gather(values, 'mp', axis=0, tiled=True)  177 us
    all_gather x5, waiting for transfers between devices, spread_grad(): return lax.all_gather(values, 'mp', axis=0, tiled=True)  175 us
  transfers between devices with their start and end apart: 25, of which 22 were waited for; matrix products, arithmetic and copies ran while one was open for 14% of the time, Pallas kernels for 0%

commit v1 on v0

v1 whole, which is shorter than its diff:
```python
from functools import partial

import jax
import jax.numpy as jnp
from jax import lax
from jax.experimental import pallas as pl
from jax.experimental.pallas import tpu as pltpu
from jax.sharding import PartitionSpec as P

HEAD_DIM = 64
PAIR = 2 * HEAD_DIM
SLICES = 8
EPSILON = 1e-06
BLOCKED = -1000000000.0
SCALE = HEAD_DIM ** (-0.5)
DISTANCES = ((0, 2, 4, 6), (0, 4, 2, 6))
F32 = jnp.float32
BF16 = jnp.bfloat16

ANY = pl.BlockSpec(memory_space=pl.ANY)
VMEM = pl.BlockSpec(memory_space=pltpu.VMEM)
SMEM = pl.BlockSpec(memory_space=pltpu.SMEM)


def swap(values, bit):
    count = lax.axis_size("dp")
    return lax.ppermute(values, "dp", [(i, i ^ bit) for i in range(count)])


def pass_on(values):
    count = lax.axis_size("mp")
    return lax.ppermute(values, "mp", [(i, (i + 1) % count) for i in range(count)])


def add(left, right):
    return (left.astype(F32) + right.astype(F32)).astype(BF16)


def ring(values):
    parts = [values]
    for _ in range(lax.axis_size("mp") - 1):
        parts.append(pass_on(parts[-1]))
    return parts


def widen(first, second):
    first = jnp.stack([first, swap(first, 2)])
    second = jnp.stack([second, swap(second, 4)])
    both = jnp.stack(
        [
            jnp.concatenate([first, swap(first, 4)]),
            jnp.concatenate([second, swap(second, 2)]),
        ]
    )
    return both, swap(both, 1)


def gather_weights(own):
    others = jnp.stack(ring(own)[1:], axis=1)
    return widen(others[0], others[1])


def reduce_grads(both):
    mp = lax.axis_size("mp")
    first = add(both[0, :2], swap(both[0, 2:], 4))
    second = add(both[1, :2], swap(both[1, 2:], 2))
    total = jnp.stack([add(first[0], swap(first[1], 2)), add(second[0], swap(second[1], 4))], axis=1)
    own = total[1]
    for step in range(1, mp):
        own = add(pass_on(own), total[(step + 1) % mp])
    bit = SLICES
    while bit < lax.axis_size("dp"):
        own = add(own, swap(own, bit))
        bit *= 2
    return widen(own[0], own[1])


def total_everywhere(values):
    bit = 1
    while bit < lax.axis_size("dp"):
        values = values + swap(values, bit)
        bit *= 2
    count = lax.axis_size("mp")
    bit = 1
    while bit < count:
        values = values + lax.ppermute(values, "mp", [(i, i ^ bit) for i in range(count)])
        bit *= 2
    return values


def dot_nn(left, right):
    return lax.dot_general(left, right, (((1,), (0,)), ((), ())), preferred_element_type=F32)


def dot_nt(left, right):
    return lax.dot_general(left, right, (((1,), (1,)), ((), ())), preferred_element_type=F32)


def dot_tn(left, right):
    return lax.dot_general(left, right, (((0,), (0,)), ((), ())), preferred_element_type=F32)


def start(source, target, sem):
    pltpu.make_async_copy(source, target, sem).start()


def finish(whole, sem):
    pltpu.make_async_copy(whole, whole, sem).wait()


def aligned(first, count, step=16):
    return pl.ds(pl.multiple_of(first, step), count)


def each_slice(place, first_step, mp):
    for core in range(2):
        for half in range(2):
            for entry in range(4):
                slot = place[0] ^ (core ^ DISTANCES[half][entry])
                for step in range(first_step, mp):
                    yield core, half, entry, step, slot, (place[1] + mp - step) % mp


def attention_spot(whole, quarter, half, slot, owner):
    span = 4 * quarter // SLICES
    count = quarter // span
    row = owner * quarter + (slot % count) * span + half * (span // 2)
    return whole.at[slot // count, aligned(row, span // 2)]


def load_attention(place, own, pieces, offset, whole, sem):
    mp = pieces[0].shape[2] + 1
    quarter = whole.shape[1] // mp
    rows = quarter // 4
    for mat in range(4):
        start(
            own.at[pl.ds(mat * quarter, quarter)],
            whole.at[mat, aligned(place[1] * quarter, quarter)],
            sem,
        )
    for core, half, entry, step, slot, owner in each_slice(place, 1, mp):
        start(
            pieces[core].at[half, entry, step - 1, pl.ds(offset, rows)],
            attention_spot(whole, quarter, half, slot, owner),
            sem,
        )


def store_attention(place, whole, outs, sem):
    mp = outs[0].shape[2]
    quarter = whole.shape[1] // mp
    for core, half, entry, step, slot, owner in each_slice(place, 0, mp):
        start(
            attention_spot(whole, quarter, half, slot, owner),
            outs[core].at[half, entry, step],
            sem,
        )


def feed_spot(whole, quarter, half, slot, owner):
    span = quarter // SLICES
    return whole.at[half, aligned(owner * quarter + slot * span, span)]


def load_feed(place, own, pieces, offset, whole, sem):
    mp = pieces[0].shape[2] + 1
    quarter = whole.shape[1] // mp
    rows = quarter // SLICES
    for half in range(2):
        start(
            own.at[pl.ds(half * quarter, quarter)],
            whole.at[half, aligned(place[1] * quarter, quarter)],
            sem,
        )
    for core, half, entry, step, slot, owner in each_slice(place, 1, mp):
        start(
            pieces[core].at[half, entry, step - 1, pl.ds(offset, rows)],
            feed_spot(whole, quarter, half, slot, owner),
            sem,
        )


def store_feed(place, whole, outs, sem):
    mp = outs[0].shape[2]
    quarter = whole.shape[1] // mp
    for core, half, entry, step, slot, owner in each_slice(place, 0, mp):
        start(
            feed_spot(whole, quarter, half, slot, owner),
            outs[core].at[half, entry, step],
            sem,
        )


def image_copies(whole, piece, quarter, half, slot, owner, sem, inward):
    rows, width = piece.shape
    span = 2 * rows
    beyond = whole.shape[1] - width
    blocks = width // beyond
    plain = quarter // span
    base = owner * quarter + half * rows

    def move(inner, outer):
        start(inner, outer, sem) if inward else start(outer, inner, sem)

    @pl.when(slot < plain)
    def _():
        move(piece, whole.at[aligned(base + slot * span, rows), pl.ds(0, width)])

    @pl.when(slot >= plain)
    def _():
        for block in range(blocks):
            row = base + block * (quarter // blocks) + (slot - plain) * span
            move(
                piece.at[:, pl.ds(block * beyond, beyond)],
                whole.at[aligned(row, rows), pl.ds(width, beyond)],
            )


def load_image(place, own, pieces, offset, rows, whole, sem):
    mp = pieces[0].shape[2] + 1
    quarter = whole.shape[0] // mp
    start(own, whole.at[aligned(place[1] * quarter, quarter)], sem)
    for core, half, entry, step, slot, owner in each_slice(place, 1, mp):
        piece = pieces[core].at[half, entry, step - 1, pl.ds(offset, rows)]
        image_copies(whole, piece, quarter, half, slot, owner, sem, True)


def store_image(place, whole, outs, sem):
    mp = outs[0].shape[2]
    quarter = whole.shape[0] // mp
    for core, half, entry, step, slot, owner in each_slice(place, 0, mp):
        piece = outs[core].at[half, entry, step]
        image_copies(whole, piece, quarter, half, slot, owner, sem, False)


def norm_rows(values, gain_row, shift_row):
    center = values - jnp.mean(values, axis=-1, keepdims=True)
    moment = jnp.mean(center * center, axis=-1, keepdims=True)
    return center * lax.rsqrt(moment + EPSILON) * gain_row + shift_row


def norm_back(pre_norm, gain_row, grad_out, small):
    center = pre_norm - jnp.mean(pre_norm, axis=-1, keepdims=True)
    scale = lax.rsqrt(jnp.mean(center * center, axis=-1, keepdims=True) + EPSILON)
    normal = center * scale
    lifted = grad_out * gain_row
    grad_pre = scale * (
        lifted
        - jnp.mean(lifted, axis=-1, keepdims=True)
        - normal * jnp.mean(lifted * normal, axis=-1, keepdims=True)
    )
    small[...] = jnp.zeros_like(small)
    small[0:1] = jnp.sum(grad_out * normal, axis=0, keepdims=True)
    small[1:2] = jnp.sum(grad_out, axis=0, keepdims=True)
    small[2:3] = jnp.sum(grad_pre, axis=0, keepdims=True)
    return grad_pre


def column_total(values):
    return jnp.sum(values.astype(F32), axis=0, keepdims=True)


def head_masks(kind):
    lane = lax.broadcasted_iota(jnp.int32, (1, PAIR), 1)
    return (lane < HEAD_DIM).astype(F32).astype(kind), (lane >= HEAD_DIM).astype(F32).astype(kind)


def both_heads(values):
    left, right = head_masks(values.dtype)
    return jnp.concatenate([values * left, values * right], axis=0)


def one_of_heads(values):
    lane = lax.broadcasted_iota(jnp.int32, (1, PAIR), 1)
    rows = values.shape[0] // 2
    return jnp.where(lane < HEAD_DIM, values[:rows], values[rows:])


def softmax(scores):
    raised = jnp.exp(scores - jnp.max(scores, axis=-1, keepdims=True))
    return raised * (1.0 / jnp.sum(raised, axis=-1, keepdims=True))


def self_weights(query, keys, code_col, code_row):
    allowed = jnp.concatenate([code_col, code_col], axis=0) == code_row
    return softmax(jnp.where(allowed, dot_nt(query, keys) * SCALE, BLOCKED))


def cross_weights(query, keys, patches):
    column = lax.broadcasted_iota(jnp.int32, (1, keys.shape[0]), 1)
    return softmax(jnp.where(column < patches, dot_nt(query, keys) * SCALE, BLOCKED))


def score_back(weights, grad_weights):
    along = weights * grad_weights
    return (along - weights * jnp.sum(along, axis=-1, keepdims=True)).astype(BF16)


def gather_rows(picks, rows_ref, target):
    seq = rows_ref.shape[1]
    for row in range(target.shape[0] // seq):
        target[row * seq : (row + 1) * seq] = rows_ref[picks[row]].astype(target.dtype)


def leave_rows(values, target):
    seq = target.shape[1]
    for row in range(target.shape[0]):
        target[row] = values[row * seq : (row + 1) * seq].astype(target.dtype)


def self_forward_kernel(
    pick, offset, place, picks, rows_ref, own, piece0, piece1, bias, params, code_col, code_row,
    out, low, pre, query, keys, value, context, whole, sem, *held,
):
    load_attention(place, own, (piece0, piece1), offset, whole, sem)
    if pick:
        gather_rows(picks, rows_ref, held[0])
        stream = held[0][...]
    else:
        stream = rows_ref[...]
    hb = stream.astype(BF16)
    low[...] = hb
    finish(whole, sem)
    query[...] = (dot_nt(hb, whole[0]) + bias[0:1]).astype(BF16)
    keys[...] = dot_nt(hb, whole[1]).astype(BF16)
    value[...] = (dot_nt(hb, whole[2]) + bias[1:2]).astype(BF16)
    groups, size = code_row.shape
    for group in range(groups):
        rows = slice(group * size, (group + 1) * size)
        for first in range(0, hb.shape[1], PAIR):
            lanes = slice(first, first + PAIR)
            weights = self_weights(
                both_heads(query[rows, lanes]), keys[rows, lanes], code_col[rows], code_row[group : group + 1]
            )
            mixed = one_of_heads(dot_nn(weights.astype(BF16), value[rows, lanes]))
            context[rows, lanes] = mixed.astype(BF16)
    total = dot_nn(context[...], whole[3]) + params[0:1] + stream
    pre[...] = total
    out[...] = norm_rows(total, params[1:2], params[2:3])


def self_backward_kernel(
    leave, offset, place, grad, low, pre, query, keys, value, context, own, piece0, piece1, params, code_col, code_row,
    out, small, keep, send, whole, grads, grad_context, grad_query, grad_keys, grad_value, sem, out_sem,
):
    load_attention(place, own, (piece0, piece1), offset, whole, sem)
    grad_pre = norm_back(pre[...], params[1:2], grad[...], small)
    branch = grad_pre.astype(BF16)
    finish(whole, sem)
    grad_context[...] = dot_nt(branch, whole[3]).astype(BF16)
    grads[3] = dot_tn(context[...], branch).astype(BF16)
    groups, size = code_row.shape
    for group in range(groups):
        rows = slice(group * size, (group + 1) * size)
        for first in range(0, branch.shape[1], PAIR):
            lanes = slice(first, first + PAIR)
            query_pair, context_pair = both_heads(query[rows, lanes]), both_heads(grad_context[rows, lanes])
            weights = self_weights(query_pair, keys[rows, lanes], code_col[rows], code_row[group : group + 1])
            grad_scores = score_back(weights, dot_nt(context_pair, value[rows, lanes]))
            mixed = one_of_heads(dot_nn(grad_scores, keys[rows, lanes])) * SCALE
            grad_query[rows, lanes] = mixed.astype(BF16)
            grad_keys[rows, lanes] = (dot_tn(grad_scores, query_pair) * SCALE).astype(BF16)
            grad_value[rows, lanes] = dot_tn(weights.astype(BF16), context_pair).astype(BF16)
    hb = low[...]
    grads[0] = dot_tn(grad_query[...], hb).astype(BF16)
    grads[1] = dot_tn(grad_keys[...], hb).astype(BF16)
    grads[2] = dot_tn(grad_value[...], hb).astype(BF16)
    store_attention(place, grads, (keep, send), out_sem)
    small[3:4] = column_total(grad_query[...])
    small[4:5] = column_total(grad_value[...])
    total = grad_pre + dot_nn(grad_query[...], whole[0])
    total = total + dot_nn(grad_keys[...], whole[1])
    total = total + dot_nn(grad_value[...], whole[2])
    if leave:
        leave_rows(total, out)
    else:
        out[...] = total
    finish(grads, out_sem)


def gelu_parts(inner):
    spread = 0.5 * (1.0 + lax.erf(inner * (2.0 ** -0.5)))
    return spread


def feed_forward_kernel(
    leave, offset, place, rows_ref, own, piece0, piece1, bias, params,
    out, low, pre, inner, active, whole, sem,
):
    load_feed(place, own, (piece0, piece1), offset, whole, sem)
    stream = rows_ref[...]
    hb = stream.astype(BF16)
    low[...] = hb
    finish(whole, sem)
    size = whole.shape[2]
    total = params[0:1] + stream
    for first in range(0, whole.shape[1], size):
        part = slice(first, first + size)
        units = dot_nt(hb, whole[0, part]) + bias[first // size : first // size + 1]
        inner[:, part] = units
        gated = (units * gelu_parts(units)).astype(BF16)
        active[:, part] = gated
        total = total + dot_nn(gated, whole[1, part])
    pre[...] = total
    result = norm_rows(total, params[1:2], params[2:3])
    if leave:
        leave_rows(result, out)
    else:
        out[...] = result


def feed_backward_kernel(
    pick, offset, place, picks, grad, low, pre, inner, active, own, piece0, piece1, params,
    out, small, keep, send, whole, grads, sem, out_sem, *held,
):
    load_feed(place, own, (piece0, piece1), offset, whole, sem)
    if pick:
        gather_rows(picks, grad, held[0])
        grad = held[0]
    grad_pre = norm_back(pre[...], params[1:2], grad[...], small)
    branch = grad_pre.astype(BF16)
    finish(whole, sem)
    size = whole.shape[2]
    hb = low[...]
    total = grad_pre
    for first in range(0, whole.shape[1], size):
        part = slice(first, first + size)
        grads[1, part] = dot_tn(active[:, part], branch).astype(BF16)
        units = inner[:, part]
        slope = gelu_parts(units) + units * jnp.exp(-0.5 * units * units) * 0.3989422804014327
        grad_units = (dot_nt(branch, whole[1, part]) * slope).astype(BF16)
        grads[0, part] = dot_tn(grad_units, hb).astype(BF16)
        row = 3 + first // size
        small[row : row + 1] = column_total(grad_units)
        total = total + dot_nn(grad_units, whole[0, part])
    store_feed(place, grads, (keep, send), out_sem)
    out[...] = total
    finish(grads, out_sem)


def image_forward_kernel(
    offset, image_offset, image_rows, place, images, own, own_image, piece0, piece1, bias, image_bias,
    projected, keys, value, whole, whole_image, sem, image_sem,
):
    load_image(place, own_image, (piece0, piece1), image_offset, image_rows, whole_image, image_sem)
    load_attention(place, own, (piece0, piece1), offset, whole, sem)
    finish(whole_image, image_sem)
    finish(whole, sem)
    size = images.shape[0] // 4
    for first in range(0, images.shape[0], size):
        rows = slice(first, first + size)
        source = (dot_nt(images[rows], whole_image[...]) + image_bias[...]).astype(BF16)
        projected[rows] = source
        keys[rows] = dot_nt(source, whole[1]).astype(BF16)
        value[rows] = (dot_nt(source, whole[2]) + bias[1:2]).astype(BF16)


def cross_forward_kernel(
    offset, seq, patches, place, rows_ref, keys, value, own, piece0, piece1, bias, params,
    out, low, pre, query, context, whole, mixed, sem,
):
    load_attention(place, own, (piece0, piece1), offset, whole, sem)
    stream = rows_ref[...]
    hb = stream.astype(BF16)
    low[...] = hb
    finish(whole, sem)
    query[...] = (dot_nt(hb, whole[0]) + bias[0:1]).astype(BF16).astype(F32)
    count = stream.shape[0] // seq
    size = keys.shape[0] // count
    for row in range(count):
        rows, places = slice(row * seq, (row + 1) * seq), slice(row * size, (row + 1) * size)
        for first in range(0, hb.shape[1], PAIR):
            lanes = slice(first, first + PAIR)
            weights = cross_weights(both_heads(query[rows, lanes]).astype(BF16), keys[places, lanes], patches)
            mixed[rows, lanes] = one_of_heads(dot_nn(weights.astype(BF16), value[places, lanes]))
    context[...] = mixed[...].astype(BF16)
    total = dot_nn(context[...], whole[3]) + params[0:1] + stream
    pre[...] = total
    out[...] = norm_rows(total, params[1:2], params[2:3])


def cross_backward_kernel(
    offset, seq, patches, place, grad, low, pre, query, context, keys, value, source, own, piece0, piece1, params,
    out, small, keep, send, grad_keys, grad_value, whole, grads, grad_context, grad_query, sem, out_sem,
):
    load_attention(place, own, (piece0, piece1), offset, whole, sem)
    grad_pre = norm_back(pre[...], params[1:2], grad[...], small)
    branch = grad_pre.astype(BF16)
    finish(whole, sem)
    grad_context[...] = dot_nt(branch, whole[3]).astype(BF16).astype(F32)
    grads[3] = dot_tn(context[...], branch).astype(BF16)
    count = branch.shape[0] // seq
    size = keys.shape[0] // count
    for row in range(count):
        rows, places = slice(row * seq, (row + 1) * seq), slice(row * size, (row + 1) * size)
        for first in range(0, branch.shape[1], PAIR):
            lanes = slice(first, first + PAIR)
            query_pair = both_heads(query[rows, lanes]).astype(BF16)
            context_pair = both_heads(grad_context[rows, lanes]).astype(BF16)
            weights = cross_weights(query_pair, keys[places, lanes], patches)
            grad_scores = score_back(weights, dot_nt(context_pair, value[places, lanes]))
            grad_query[rows, lanes] = one_of_heads(dot_nn(grad_scores, keys[places, lanes])) * SCALE
            grad_keys[places, lanes] = (dot_tn(grad_scores, query_pair) * SCALE).astype(BF16)
            grad_value[places, lanes] = dot_tn(weights.astype(BF16), context_pair).astype(BF16)
    query_low = grad_query[...].astype(BF16)
    grads[0] = dot_tn(query_low, low[...]).astype(BF16)
    grads[1] = dot_tn(grad_keys[...], source[...]).astype(BF16)
    grads[2] = dot_tn(grad_value[...], source[...]).astype(BF16)
    store_attention(place, grads, (keep, send), out_sem)
    small[3:4] = column_total(query_low)
    small[4:5] = column_total(grad_value[...])
    out[...] = grad_pre + dot_nn(query_low, whole[0])
    finish(grads, out_sem)


def image_backward_kernel(
    offset, image_offset, image_rows, place, images, grad_keys, grad_value, own, own_image, piece0, piece1,
    out, small, keep, send, whole, whole_image, grads, low, sem, image_sem, out_sem,
):
    load_attention(place, own, (piece0, piece1), offset, whole, sem)
    load_image(place, own_image, (piece0, piece1), image_offset, image_rows, whole_image, image_sem)
    finish(whole, sem)
    finish(whole_image, image_sem)
    count, patches = out.shape[:2]
    size = images.shape[0] // count
    small[...] = jnp.zeros_like(small)
    for row in range(count):
        rows = slice(row * size, (row + 1) * size)
        source = dot_nn(grad_keys[rows], whole[1]) + dot_nn(grad_value[rows], whole[2])
        source = source.astype(BF16)
        low[rows] = source
        out[row] = dot_nn(source, whole_image[...])[:patches]
    grads[...] = dot_tn(low[...], images[...]).astype(BF16)
    store_image(place, grads, (keep, send), out_sem)
    small[0:1] = column_total(low[...])
    finish(grads, out_sem)


def pick_kernel(picks, rows_ref, out):
    for row in range(out.shape[0]):
        out[row] = rows_ref[picks[row]].astype(out.dtype)


def finish_kernel(blocks, mp_quarter, n_held, place, result0, result1, *refs):
    results = (result0, result1)
    outs = refs[n_held:]
    n_outs = sum(2 if kind != "image" else 1 for kind, _, _ in blocks)
    names = []
    for kind, _, _ in blocks:
        names += {"attention": ["attention_in", "attention_out"], "feed": ["feed_in", "feed_out"], "image": ["image"]}[kind]
    unique = list(dict.fromkeys(names))
    targets = dict(zip(unique, outs[: len(unique)]))
    scratch = list(outs[len(unique) :])
    sem, out_sem = scratch[-2:]
    del n_outs
    spot = 0
    filled = []
    for number, (kind, offset, _) in enumerate(blocks):
        buffer = scratch[spot]
        if kind == "attention":
            spot += 3
            quarter = mp_quarter
            span = 4 * quarter // SLICES
            rows, count = span // 2, quarter // span
        elif kind == "feed":
            spot += 3
            quarter = buffer.shape[1]
            span = quarter // SLICES
            rows = span
        else:
            spot += 2
            quarter = mp_quarter
            width = result0.shape[3]
            rows = quarter * buffer.shape[1] // width // SLICES // 2
        for core in range(2):
            for half in range(2):
                for entry in range(4):
                    slot = place[0] ^ (core ^ DISTANCES[half][entry])
                    piece = results[core].at[half, entry, pl.ds(offset, rows)]
                    if kind == "attention":
                        row = (slot % count) * span + half * rows
                        start(piece, buffer.at[slot // count, aligned(row, rows)], sem.at[number])
                    elif kind == "feed":
                        start(piece, buffer.at[half, aligned(slot * span, rows)], sem.at[number])
                    else:
                        image_copies(buffer, piece, quarter, half, slot, 0, sem.at[number], True)
    spot = 0
    for number, (kind, offset, layer) in enumerate(blocks):
        buffer = scratch[spot]
        done = out_sem.at[number]
        if kind == "attention":
            turned, plain = scratch[spot + 1], scratch[spot + 2]
            spot += 3
            finish(buffer.at[:, pl.ds(0, mp_quarter)], sem.at[number])
            for mat in range(3):
                turned[mat] = buffer[mat].astype(F32).T[:, :mp_quarter]
            plain[...] = buffer[3, :mp_quarter].astype(F32)
            start(turned, targets["attention_in"].at[layer], done)
            start(plain, targets["attention_out"].at[layer], done)
        elif kind == "feed":
            turned, plain = scratch[spot + 1], scratch[spot + 2]
            spot += 3
            finish(buffer, sem.at[number])
            turned[...] = buffer[0].astype(F32).T
            plain[...] = buffer[1].astype(F32)
            start(turned, targets["feed_in"].at[layer], done)
            start(plain, targets["feed_out"].at[layer], done)
        else:
            turned = scratch[spot + 1]
            spot += 2
            finish(buffer.at[pl.ds(0, mp_quarter)], sem.at[number])
            turned[...] = buffer[...].astype(F32).T[:, :mp_quarter]
            start(turned, targets["image"], done)
            plain = None
        filled.append((turned, plain, done))
    for turned, plain, done in filled:
        finish(turned, done)
        if plain is not None:
            finish(plain, done)


def shape(dims, kind=F32):
    return jax.ShapeDtypeStruct(tuple(dims), kind)


def call(kernel, ins, outs, scratch, megabytes, flops, aliases=None):
    moved = sum(v.size * v.dtype.itemsize for v, _ in ins) + sum(s.size * s.dtype.itemsize for s, _ in outs)
    return pl.pallas_call(
        kernel,
        in_specs=[spec for _, spec in ins],
        out_specs=[spec for _, spec in outs],
        out_shape=[s for s, _ in outs],
        scratch_shapes=scratch,
        input_output_aliases=aliases or {},
        compiler_params=pltpu.CompilerParams(vmem_limit_bytes=megabytes << 20),
        cost_estimate=pl.CostEstimate(flops=int(flops), bytes_accessed=int(moved), transcendentals=0),
    )(*[v for v, _ in ins])


def on_device(
    tokens, images, segment_of_token, image_of_row, attention_in, query_value_bias, attention_out, output_bias,
    feed_in, feed_bias, feed_out, image_weight, image_bias, norm_gain, norm_bias, cotangent,
):
    mp = lax.axis_size("mp")
    slot = lax.axis_index("dp") % SLICES
    owner = lax.axis_index("mp")
    place = jnp.stack([slot, owner]).astype(jnp.int32)
    own_rows, seq, width = tokens.shape
    group_rows = segment_of_token.shape[0]
    patches, image_width = images.shape[1:]
    quarter = attention_in.shape[3]
    units = feed_in.shape[2]
    n_tokens = own_rows * seq

    local_order = image_of_row % group_rows
    here = owner * own_rows + jnp.arange(own_rows, dtype=jnp.int32)
    chosen = (local_order[None, :] == here[:, None]).astype(jnp.int32)
    source_row = jnp.sum(chosen * jnp.arange(group_rows, dtype=jnp.int32)[None, :], axis=1)
    picks_in = ((owner - source_row // own_rows) % mp) * own_rows + source_row % own_rows
    mine = (jnp.arange(group_rows, dtype=jnp.int32)[None, :] == here[:, None]).astype(jnp.int32)
    image_row = jnp.sum(mine * local_order[None, :], axis=1)
    picks_out = ((owner - image_row // own_rows) % mp) * own_rows + image_row % own_rows
    segments = jnp.sum(chosen[:, :, None] * segment_of_token[None], axis=1)
    code = jnp.arange(own_rows, dtype=jnp.int32)[:, None] * seq + segments
    code_col = code.reshape(n_tokens, 1)
    code_row = code.reshape(own_rows // 2, 2 * seq)

    flat = jnp.concatenate([query_value_bias.reshape(-1), feed_bias.reshape(-1), image_bias])
    flat = jnp.pad(flat, (0, -flat.shape[0] % width)).reshape(-1, width)
    ordered = jnp.stack(ring(flat))[(owner - jnp.arange(mp)) % mp].reshape(mp, -1).astype(F32)
    cut0 = query_value_bias.size
    cut1 = cut0 + feed_bias.size
    head_bias = ordered[:, :cut0].reshape(mp, 3, 2, quarter).transpose(1, 2, 0, 3).reshape(3, 2, width)
    unit_bias = ordered[:, cut0:cut1].reshape(mp, 2, units).transpose(1, 0, 2).reshape(2, -1, width)
    patch_bias = ordered[:, cut1 : cut1 + quarter].reshape(1, width)
    params = jnp.stack([output_bias, norm_gain, norm_bias], axis=1).astype(F32)

    rows_in = jnp.stack(ring(tokens)).reshape(mp * own_rows, seq, width)

    def attention_shard(layer):
        turned = attention_in[layer].transpose(0, 2, 1).reshape(3 * quarter, width)
        return jnp.concatenate([turned, attention_out[layer]])

    def feed_shard(layer):
        return jnp.concatenate([feed_in[layer].T, feed_out[layer]])

    image_shard = image_weight.T
    beyond = image_width - width
    blocks = width // beyond
    image_rest = image_shard[:, width:].reshape(blocks, quarter // blocks, beyond)
    image_rest = image_rest.transpose(1, 0, 2).reshape(quarter // blocks, width)
    image_flat = jnp.concatenate([image_shard[:, :width], image_rest])
    attention_shards = [attention_shard(layer) for layer in range(3)]
    feed_shards = [feed_shard(layer) for layer in range(2)]

    def own_slice(shard, by_half):
        span = shard.shape[0] // SLICES
        if by_half:
            return lax.dynamic_slice_in_dim(shard, slot * span, span).reshape(2, span // 2, width)
        halves = shard.reshape(2, -1, width)
        return lax.dynamic_slice_in_dim(halves, slot * (span // 2), span // 2, axis=1)

    attention_rows = 4 * quarter // SLICES // 2
    feed_rows = units // SLICES
    image_rows = image_flat.shape[0] // SLICES // 2
    text_pieces = gather_weights(own_slice(attention_shards[0], True))
    middle_pieces = gather_weights(
        jnp.concatenate([own_slice(feed_shards[0], False), own_slice(attention_shards[1], True)], axis=1)
    )
    cross_pieces = gather_weights(
        jnp.concatenate([own_slice(attention_shards[2], True), own_slice(image_flat, True)], axis=1)
    )
    last_pieces = gather_weights(own_slice(feed_shards[1], False))
    attention_at = [(text_pieces, 0), (middle_pieces, feed_rows), (cross_pieces, 0)]
    feed_at = [(middle_pieces, 0), (last_pieces, 0)]
    grads_in = jnp.stack(ring(cotangent)).reshape(mp * own_rows, seq, width)

    padded = -(-patches // 16) * 16
    patch_rows = jnp.pad(images, ((0, 0), (0, padded - patches), (0, 0))).reshape(own_rows * padded, image_width)
    n_patches = own_rows * padded

    token_shape = shape((n_tokens, width))
    token_low = shape((n_tokens, width), BF16)
    row_low = shape((own_rows, seq, width), BF16)
    inner_shape = shape((n_tokens, mp * units))
    inner_low = shape((n_tokens, mp * units), BF16)
    patch_low = shape((n_patches, width), BF16)
    square = pltpu.VMEM((4, width, width), BF16)
    wide = pltpu.VMEM((2, mp * units, width), BF16)
    tall = pltpu.VMEM((width, image_width), BF16)
    token_f32 = pltpu.VMEM((n_tokens, width), F32)
    token_bf16 = pltpu.VMEM((n_tokens, width), BF16)
    dma = pltpu.SemaphoreType.DMA
    matmul = 2 * n_tokens * width * width
    patch_matmul = 2 * n_patches * width * width

    def weight_ins(layer):
        (piece0, piece1), _ = attention_at[layer]
        return [(attention_shards[layer], ANY), (piece0, ANY), (piece1, ANY)]

    def feed_ins(layer):
        (piece0, piece1), _ = feed_at[layer]
        return [(feed_shards[layer], ANY), (piece0, ANY), (piece1, ANY)]

    def self_forward(layer, norm, rows, pick):
        return call(
            partial(self_forward_kernel, pick, attention_at[layer][1]),
            [(place, SMEM), (picks_in, SMEM), (rows, VMEM)]
            + weight_ins(layer)
            + [(head_bias[layer], VMEM), (params[norm], VMEM), (code_col, VMEM), (code_row, VMEM)],
            [(token_shape, VMEM), (token_low, VMEM), (token_shape, VMEM)] + [(token_low, VMEM)] * 4,
            [square, dma] + ([token_f32] if pick else []),
            32,
            4 * matmul,
        )

    def self_backward(layer, norm, grad, kept, leave):
        _, low, pre, query, keys, value, context = kept
        return call(
            partial(self_backward_kernel, leave, attention_at[layer][1]),
            [(place, SMEM)]
            + [(v, VMEM) for v in (grad, low, pre, query, keys, value, context)]
            + weight_ins(layer)
            + [(params[norm], VMEM), (code_col, VMEM), (code_row, VMEM)],
            [(row_low if leave else token_shape, VMEM), (shape((8, width)), VMEM)] + [(attention_grad, ANY)] * 2,
            [square, square] + [token_bf16] * 4 + [dma, dma],
            40,
            9 * matmul,
        )

    attention_grad = shape((2, 4, mp, attention_rows, width), BF16)
    feed_grad = shape((2, 4, mp, feed_rows, width), BF16)
    image_grad = shape((2, 4, mp, image_rows, width), BF16)

    def feed_forward(layer, norm, rows, leave):
        return call(
            partial(feed_forward_kernel, leave, feed_at[layer][1]),
            [(place, SMEM), (rows, VMEM)] + feed_ins(layer) + [(unit_bias[layer], VMEM), (params[norm], VMEM)],
            [(row_low if leave else token_shape, VMEM), (token_low, VMEM), (token_shape, VMEM)]
            + [(inner_shape, VMEM), (inner_low, VMEM)],
            [wide, dma],
            40,
            2 * mp * matmul,
        )

    def feed_backward(layer, norm, grad, kept, pick):
        _, low, pre, inner, active = kept
        return call(
            partial(feed_backward_kernel, pick, feed_at[layer][1]),
            [(place, SMEM), (picks_in, SMEM)]
            + [(v, VMEM) for v in (grad, low, pre, inner, active)]
            + feed_ins(layer)
            + [(params[norm], VMEM)],
            [(token_shape, VMEM), (shape((8, width)), VMEM)] + [(feed_grad, ANY)] * 2,
            [wide, wide, dma, dma] + ([token_f32] if pick else []),
            48,
            4 * mp * matmul,
        )

    text_attention = self_forward(0, 0, rows_in, True)
    text_feed = feed_forward(0, 1, text_attention[0], False)
    joining_attention = self_forward(1, 2, text_feed[0], False)
    image_ins = [(image_shard, ANY), (cross_pieces[0], ANY), (cross_pieces[1], ANY)]
    projected, image_keys, image_value = call(
        partial(image_forward_kernel, 0, attention_rows, image_rows),
        [(place, SMEM), (patch_rows, VMEM), (attention_shards[2], ANY)]
        + image_ins
        + [(head_bias[2], VMEM), (patch_bias, VMEM)],
        [(patch_low, VMEM)] * 3,
        [square, tall, dma, dma],
        40,
        3.4 * patch_matmul,
    )
    cross_attention = call(
        partial(cross_forward_kernel, 0, seq, patches),
        [(place, SMEM), (joining_attention[0], VMEM), (image_keys, VMEM), (image_value, VMEM)]
        + weight_ins(2)
        + [(head_bias[2], VMEM), (params[3], VMEM)],
        [(token_shape, VMEM), (token_low, VMEM), (token_shape, VMEM), (token_shape, VMEM), (token_low, VMEM)],
        [square, token_f32, dma],
        32,
        3 * matmul,
    )
    joining_feed = feed_forward(1, 4, cross_attention[0], True)
    rows_out = jnp.stack(ring(joining_feed[0])).reshape(mp * own_rows, seq, width)

    def pick_rows(rows):
        return call(
            pick_kernel, [(picks_out, SMEM), (rows, VMEM)], [(shape((own_rows, seq, width)), VMEM)], [], 16, 0
        )[0]

    mixed_out = pick_rows(rows_out)
    grad, small_joining_feed, keep, send = feed_backward(1, 4, grads_in, joining_feed, True)
    last_result = reduce_grads(add(keep, swap(send, 1)))
    grad, small_cross, keep, send, grad_keys, grad_value = call(
        partial(cross_backward_kernel, 0, seq, patches),
        [(place, SMEM), (grad, VMEM)]
        + [(cross_attention[i], VMEM) for i in (1, 2, 3, 4)]
        + [(image_keys, VMEM), (image_value, VMEM), (projected, VMEM)]
        + weight_ins(2)
        + [(params[3], VMEM)],
        [(token_shape, VMEM), (shape((8, width)), VMEM)] + [(attention_grad, ANY)] * 2 + [(patch_low, VMEM)] * 2,
        [square, square, token_f32, token_f32, dma, dma],
        56,
        5 * matmul + 2 * patch_matmul,
    )
    cross_sum = add(keep, swap(send, 1))
    grad, small_joining, keep, send = self_backward(1, 2, grad, joining_attention, False)
    joining_sum = add(keep, swap(send, 1))
    grad_images, small_image, keep, send = call(
        partial(image_backward_kernel, 0, attention_rows, image_rows),
        [(place, SMEM), (patch_rows, VMEM), (grad_keys, VMEM), (grad_value, VMEM), (attention_shards[2], ANY)]
        + image_ins,
        [(shape(images.shape), VMEM), (shape((8, width)), VMEM)] + [(image_grad, ANY)] * 2,
        [square, tall, tall, pltpu.VMEM((n_patches, width), BF16), dma, dma, dma],
        48,
        4.7 * patch_matmul,
    )
    image_sum = add(keep, swap(send, 1))
    middle_result = reduce_grads(jnp.concatenate([cross_sum, joining_sum, image_sum], axis=3))
    grad, small_text_feed, keep, send = feed_backward(0, 1, grad, text_feed, False)
    feed_result = reduce_grads(add(keep, swap(send, 1)))
    small_early = total_everywhere(
        jnp.concatenate([small_text_feed, small_joining, small_cross, small_joining_feed, small_image])
    )
    rows_back, small_text, keep, send = self_backward(0, 0, grad, text_attention, True)
    text_result = reduce_grads(add(keep, swap(send, 1)))
    small_late = total_everywhere(small_text)
    grad_tokens = pick_rows(jnp.stack(ring(rows_back)).reshape(mp * own_rows, seq, width))

    whole_shapes = {
        "attention_in": shape(attention_in.shape),
        "attention_out": shape(attention_out.shape),
        "feed_in": shape(feed_in.shape),
        "feed_out": shape(feed_out.shape),
        "image": shape(image_weight.shape),
    }
    padded_quarter = -(-quarter // 128) * 128
    scratch_of = {
        "attention": [
            pltpu.VMEM((4, padded_quarter, width), BF16),
            pltpu.VMEM((3, width, quarter), F32),
            pltpu.VMEM((quarter, width), F32),
        ],
        "feed": [
            pltpu.VMEM((2, units, width), BF16),
            pltpu.VMEM((width, units), F32),
            pltpu.VMEM((units, width), F32),
        ],
        "image": [pltpu.VMEM((padded_quarter, image_width), BF16), pltpu.VMEM((image_width, quarter), F32)],
    }
    names_of = {"attention": ["attention_in", "attention_out"], "feed": ["feed_in", "feed_out"], "image": ["image"]}
    written = {}

    def write_out(result, blocks):
        names = list(dict.fromkeys(name for kind, _, _ in blocks for name in names_of[kind]))
        held = [name for name in names if name in written]
        scratch = [entry for kind, _, _ in blocks for entry in scratch_of[kind]]
        results = call(
            partial(finish_kernel, blocks, quarter, len(held)),
            [(place, SMEM), (result[0], ANY), (result[1], ANY)] + [(written[name], ANY) for name in held],
            [(whole_shapes[name], ANY) for name in names],
            scratch + [dma((len(blocks),)), dma((len(blocks),))],
            32,
            0,
            {3 + i: names.index(name) for i, name in enumerate(held)},
        )
        written.update(zip(names, results))

    write_out(last_result, (("feed", 0, 1),))
    write_out(
        middle_result,
        (("attention", 0, 2), ("attention", attention_rows, 1), ("image", 2 * attention_rows, 0)),
    )
    write_out(feed_result, (("feed", 0, 0),))
    write_out(text_result, (("attention", 0, 0),))

    smalls = jnp.concatenate([small_late, small_early]).reshape(6, 8, width)
    order = [0, 1, 2, 3, 4]
    grad_norm_gain = jnp.stack([smalls[i, 0] for i in order])
    grad_norm_bias = jnp.stack([smalls[i, 1] for i in order])
    grad_output_bias = jnp.stack([smalls[i, 2] for i in order])

    def own_part(values):
        return lax.dynamic_slice_in_dim(values, owner * quarter, quarter, axis=values.ndim - 1)

    grad_query_value_bias = own_part(jnp.stack([smalls[i, 3:5] for i in (0, 2, 3)]))
    grad_feed_bias = jnp.stack([smalls[i, 3 : 3 + mp].reshape(-1) for i in (1, 4)])
    grad_feed_bias = lax.dynamic_slice_in_dim(grad_feed_bias, owner * units, units, axis=1)
    grad_image_bias = own_part(smalls[5, 0])
    return (
        mixed_out,
        grad_tokens,
        grad_images,
        written["attention_in"],
        grad_query_value_bias,
        written["attention_out"],
        grad_output_bias,
        written["feed_in"],
        grad_feed_bias,
        written["feed_out"],
        written["image"],
        grad_image_bias,
        grad_norm_gain,
        grad_norm_bias,
    )


def solution(mesh):
    rows = P(("dp", "mp"), None, None)
    return jax.shard_map(
        on_device,
        mesh=mesh,
        in_specs=(
            rows,
            rows,
            P("dp", None),
            P("dp"),
            P(None, None, None, "mp"),
            P(None, None, "mp"),
            P(None, "mp", None),
            P(),
            P(None, None, "mp"),
            P(None, "mp"),
            P(None, "mp", None),
            P(None, "mp"),
            P("mp"),
            P(),
            P(),
            rows,
        ),
        out_specs=(
            rows,
            rows,
            rows,
            P(None, None, None, "mp"),
            P(None, None, "mp"),
            P(None, "mp", None),
            P(),
            P(None, None, "mp"),
            P(None, "mp"),
            P(None, "mp", None),
            P(None, "mp"),
            P("mp"),
            P(),
            P(),
        ),
        check_vma=False,
    )
```

time: 2650 us -> 859 us (0.32)
  waiting for transfers between devices: 1950 us -> 365 us
  Pallas kernels: 0 us -> 235 us
  matrix products: 232 us -> 0 us
  local copies, waits for them, and re-layouts: 282 us -> 103 us
  blocking collectives: 73.4 us -> 0 us
  starting transfers between devices: 3.5 us -> 71.9 us
    reduce_scatter x11 -> x0, waiting for transfers between devices: 800 us -> none  [the longest x5 336 us: settle(): lax.psum_scatter(row_fn(jnp.int32(0), lax.axis_size('mp') * own_rows), 'm...]
    all_gather x12 -> x0, waiting for transfers between devices: 712 us -> none  [the longest x1 217 us: on_device(): group_projected = lax.all_gather(columns, 'mp', axis=2, tiled=True)]
    ppermute x0 -> x111, waiting for transfers between devices: none -> 365 us  [the longest x68 189 us: swap(): return lax.ppermute(values, 'dp', [(i, i ^ bit) for i in range(count)])]
    pallas_call x0 -> x18, Pallas kernels: none -> 235 us  [call(): pl.pallas_call(kernel, in_specs=[spec for _, spec in ins], out_specs=[spe...]
    dot_general x69 -> x0, matrix products: 232 us -> none  [the longest x17 71.1 us: product(): return jnp.dot(values, weight, preferred_element_type=jnp.float32)]
    psum x1 -> x0, waiting for transfers between devices: 224 us -> none  [on_device(): lax.psum((grad_attention_in, grad_query_value_bias, grad_attention_out, g...]
    unnamed x26 -> x0, waiting for transfers between devices: 215 us -> none
    psum x2 -> x0, blocking collectives: 73.4 us -> none  [the longest x1 48.2 us: on_device(): lax.psum((grad_output_bias, grad_norm_gain, grad_norm_bias), ('dp', 'mp'))]
  transfers between devices with their start and end apart: 25 -> 111, of which waited for: 22 -> 58; matrix products, arithmetic and copies ran while one was open for 14% -> 15% of each run, Pallas kernels for 0% -> 11%
where the time goes in v1:
time: 859 us; the launch traced here: 847 us
  waiting for transfers between devices  365 us (42%)
  Pallas kernels  235 us (27%)
  local copies, waits for them, and re-layouts  103 us (12%)
  starting transfers between devices  71.9 us (8%)
  other arithmetic  69.5 us (8%)
    pallas_call x18, Pallas kernels, call(): pl.pallas_call(kernel, in_specs=[spec for _, spec in ins], out_specs=[spe...  235 us
    ppermute x68, waiting for transfers between devices, swap(): return lax.ppermute(values, 'dp', [(i, i ^ bit) for i in range(count)])  189 us
    ppermute x39, waiting for transfers between devices, pass_on(): lax.ppermute(values, 'mp', [(i, (i + 1) % count) for i in range(count)])  166 us
    unnamed x299, local copies, waits for them, and re-layouts  61.6 us
    ppermute x68, starting transfers between devices, swap(): return lax.ppermute(values, 'dp', [(i, i ^ bit) for i in range(count)])  55.5 us
    convert_element_type x22, other arithmetic, add(): return (left.astype(F32) + right.astype(F32)).astype(BF16)  20.6 us
  transfers between devices with their start and end apart: 111, of which 58 were waited for; matrix products, arithmetic and copies ran while one was open for 15% of the time, Pallas kernels for 11%

profile of v1, /device:TPU:0, one launch (start us, length us, event | category | flops | bytes accessed | tf_op | source)
XLA Modules:
  0.0 847.1 jit_solution(2269678862222800665)
XLA Ops:
  19.1 9.4 %collective-permute-done.14 = bf16[2,144,768]{2,1,0:T(8,128)(2,1)} collective-permute-done((bf16[2,144,768]{2,1,0:T(8,128)(2,1)}, bf16[2,144,768]{2,1,0:T(8,128)(2,1)}, u32[]{:S(2)}, u32[]{:S(2)}) %collective-permute-start.14) | collective-permute-done | bytes 442400 | tf_op jit(solution)/shard_map/ppermute | solution.py:32
  44.6 19.1 %collective-permute-done.16 = bf16[2,144,768]{2,1,0:T(8,128)(2,1)} collective-permute-done((bf16[2,144,768]{2,1,0:T(8,128)(2,1)}, bf16[2,144,768]{2,1,0:T(8,128)(2,1)}, u32[]{:S(2)}, u32[]{:S(2)}) %collective-permute-start.16) | collective-permute-done | bytes 442400 | tf_op jit(solution)/shard_map/ppermute | solution.py:32
  70.2 8.8 %collective-permute-done.17 = bf16[3,144,768]{2,1,0:T(8,128)(2,1)S(1)} collective-permute-done((bf16[3,144,768]{2,1,0:T(8,128)(2,1)S(1)}, bf16[3,144,768]{2,1,0:T(8,128)(2,1)S(1)}, u32[]{:S(2)}, u32[]{:S(2)}) %collective-permute-start.17) | collective-permute-done | bytes 663584 | tf_op jit(solution)/shard_map/ppermute | solution.py:27
  125.9 10.1 %collective-permute-done.33 = bf16[3,96,768]{2,1,0:T(8,128)(2,1)S(1)} collective-permute-done((bf16[3,96,768]{2,1,0:T(8,128)(2,1)S(1)}, bf16[3,96,768]{2,1,0:T(8,128)(2,1)S(1)}, u32[]{:S(2)}, u32[]{:S(2)}) %collective-permute-start.33) | collective-permute-done | bytes 442400 | tf_op jit(solution)/shard_map/ppermute | solution.py:27
  145.5 11.5 %collective-permute-done.26 = bf16[2,3,64,768]{3,2,1,0:T(8,128)(2,1)S(1)} collective-permute-done((bf16[2,3,64,768]{3,2,1,0:T(8,128)(2,1)S(1)}, bf16[2,3,64,768]{3,2,1,0:T(8,128)(2,1)S(1)}, u32[]{:S(2)}, u32[]{:S(2)}) %collective-permute-start.26) | collective-permute-done | bytes 589856 | tf_op jit(solution)/shard_map/ppermute | solution.py:27
  162.6 11.6 %collective-permute-done.34 = bf16[2,3,96,768]{3,2,1,0:T(8,128)(2,1)S(1)} collective-permute-done((bf16[2,3,96,768]{3,2,1,0:T(8,128)(2,1)S(1)}, bf16[2,3,96,768]{3,2,1,0:T(8,128)(2,1)S(1)}, u32[]{:S(2)}, u32[]{:S(2)}) %collective-permute-start.34) | collective-permute-done | bytes 884768 | tf_op jit(solution)/shard_map/ppermute | solution.py:27
  194.1 9.3 %collective-permute-done.1 = bf16[8,40,768]{2,1,0:T(8,128)(2,1)} collective-permute-done((bf16[8,40,768]{2,1,0:T(8,128)(2,1)S(1)}, bf16[8,40,768]{2,1,0:T(8,128)(2,1)}, u32[]{:S(2)}, u32[]{:S(2)}) %collective-permute-start.1) | collective-permute-done | bytes 491552 | tf_op jit(solution)/shard_map/ppermute | solution.py:32
  257.7 10.5 %shard_map.266 = (bf16[1280,768]{1,0:T(8,128)(2,1)S(1)}, bf16[1280,768]{1,0:T(8,128)(2,1)S(1)}, bf16[1280,768]{1,0:T(8,128)(2,1)S(1)}) custom-call(s32[2]{0:T(128)S(1)} %pad_add_fusion.place, bf16[1280,1024]{1,0:T(8,128)(2,1)} %bitcast.469, bf16[768,768]{1,0:T(8,128)(2,1)S(1)} %copy-done.2, bf16[192,1024]{1,0:T(8,128)(2,1)S(1)} %bitcast.455, ...), custom_call_target="tpu_custom_call" | custom-call | flops 5133828096 | bytes 14820360 | tf_op jit(solution)/shard_map/pallas_call | solution.py:628
  293.1 20.0 %shard_map.267 = (f32[320,768]{1,0:T(8,128)S(1)}, bf16[320,768]{1,0:T(8,128)(2,1)S(1)}, f32[320,768]{1,0:T(8,128)S(1)}, f32[320,768]{1,0:T(8,128)S(1)}, bf16[320,768]{1,0:T(8,128)(2,1)S(1)}) custom-call(s32[2]{0:T(128)S(1)} %pad_add_fusion.place, f32[320,768]{1,0:T(8,128)S(1)} %get-tuple-element.83.rows_ref, bf16[1280,768]{1,0:T(8,128)(2,1)S(1)} %get-tuple-element.84.keys, ...), custom_call_target="tpu_custom_call" | custom-call | flops 1132462080 | bytes 14760968 | tf_op jit(solution)/shard_map/pallas_call | solution.py:628
  314.1 9.5 %shard_map.268 = (bf16[8,40,768]{2,1,0:T(8,128)(2,1)S(1)}, bf16[320,768]{1,0:T(8,128)(2,1)S(1)}, f32[320,768]{1,0:T(8,128)S(1)}, f32[320,3072]{1,0:T(8,128)}, bf16[320,3072]{1,0:T(8,128)(2,1)S(1)}) custom-call(s32[2]{0:T(128)S(1)} %pad_add_fusion.place, f32[320,768]{1,0:T(8,128)S(1)} %get-tuple-element.86.rows_ref, bf16[1536,768]{1,0:T(8,128)(2,1)S(1)} %copy-done.6, ...), custom_call_target="tpu_custom_call" | custom-call | flops 3019898880 | bytes 18306056 | tf_op jit(solution)/shard_map/pallas_call | solution.py:628
  324.9 19.4 %shard_map.270 = (f32[320,768]{1,0:T(8,128)S(1)}, f32[8,768]{1,0:T(8,128)S(1)}, bf16[2,4,4,96,768]{4,3,2,1,0:T(8,128)(2,1)}, bf16[2,4,4,96,768]{4,3,2,1,0:T(8,128)(2,1)}) custom-call(s32[2]{0:T(128)S(1)} %pad_add_fusion.place, s32[8]{0:T(128)S(1)} %copy-done.47, bf16[32,40,768]{2,1,0:T(8,128)(2,1)S(1)} %bitcast.450, ...), custom_call_target="tpu_custom_call" | custom-call | flops 6039797760 | bytes 29230120 | tf_op jit(solution)/shard_map/pallas_call | solution.py:628
  345.3 38.9 %shard_map.271 = (f32[320,768]{1,0:T(8,128)}, f32[8,768]{1,0:T(8,128)}, bf16[2,4,4,48,768]{4,3,2,1,0:T(8,128)(2,1)}, bf16[2,4,4,48,768]{4,3,2,1,0:T(8,128)(2,1)}...) custom-call(s32[2]{0:T(128)} %copy-done.38, f32[320,768]{1,0:T(8,128)} %copy-done.77, bf16[320,768]{1,0:T(8,128)(2,1)} %copy-done.70, ...), custom_call_target="tpu_custom_call" | custom-call | flops 4907335680 | bytes 25396232 | tf_op jit(solution)/shard_map/pallas_call | solution.py:628
  390.6 27.9 %shard_map.272 = (f32[320,768]{1,0:T(8,128)S(1)}, f32[8,768]{1,0:T(8,128)S(1)}, bf16[2,4,4,48,768]{4,3,2,1,0:T(8,128)(2,1)S(1)}, bf16[2,4,4,48,768]{4,3,2,1,0:T(8,128)(2,1)S(1)}) custom-call(s32[2]{0:T(128)S(1)} %copy-done.39, f32[320,768]{1,0:T(8,128)S(1)} %copy-done.15, bf16[320,768]{1,0:T(8,128)(2,1)S(1)} %copy-done.21, f32[320,768]{1,0:T(8,128)S(1)} %copy-done.14, ...), custom_call_target="tpu_custom_call" | custom-call | flops 3397386240 | bytes 21958152 | tf_op jit(solution)/shard_map/pallas_call | solution.py:628
  421.3 18.7 %shard_map.273 = (f32[320,768]{1,0:T(8,128)S(1)}, f32[8,768]{1,0:T(8,128)S(1)}, bf16[2,4,4,96,768]{4,3,2,1,0:T(8,128)(2,1)}, bf16[2,4,4,96,768]{4,3,2,1,0:T(8,128)(2,1)}) custom-call(s32[2]{0:T(128)S(1)} %copy-done.39, s32[8]{0:T(128)S(1)} %copy-done.48, f32[320,768]{1,0:T(8,128)S(1)} %get-tuple-element.105.grad, bf16[320,768]{1,0:T(8,128)(2,1)S(1)} %copy-done.69, ...), custom_call_target="tpu_custom_call" | custom-call | flops 6039797760 | bytes 31786024 | tf_op jit(solution)/shard_map/pallas_call | solution.py:628
  443.3 24.6 %shard_map.274 = (bf16[8,40,768]{2,1,0:T(8,128)(2,1)S(1)}, f32[8,768]{1,0:T(8,128)S(1)}, bf16[2,4,4,48,768]{4,3,2,1,0:T(8,128)(2,1)S(1)}, bf16[2,4,4,48,768]{4,3,2,1,0:T(8,128)(2,1)}) custom-call(s32[2]{0:T(128)S(1)} %copy-done.39, f32[320,768]{1,0:T(8,128)S(1)} %copy-done.74, bf16[320,768]{1,0:T(8,128)(2,1)S(1)} %copy-done.59, f32[320,768]{1,0:T(8,128)S(1)} %copy-done.53, ...), custom_call_target="tpu_custom_call" | custom-call | flops 3397386240 | bytes 14388744 | tf_op jit(solution)/shard_map/pallas_call | solution.py:628
  470.1 18.4 %shard_map.276 = (f32[8,145,1024]{2,1,0:T(8,128)}, f32[8,768]{1,0:T(8,128)S(1)}, bf16[2,4,4,16,768]{4,3,2,1,0:T(8,128)(2,1)S(1)}, bf16[2,4,4,16,768]{4,3,2,1,0:T(8,128)(2,1)S(1)}) custom-call(s32[2]{0:T(128)S(1)} %copy-done.39, bf16[1280,1024]{1,0:T(8,128)(2,1)} %bitcast.470, bf16[1280,768]{1,0:T(8,128)(2,1)S(1)} %copy-done.75, ...), custom_call_target="tpu_custom_call" | custom-call | flops 7096762368 | bytes 19193864 | tf_op jit(solution)/shard_map/pallas_call | solution.py:628
  503.3 9.0 %collective-permute-done.48 = bf16[2,4,48,768]{3,2,1,0:T(8,128)(2,1)S(1)} collective-permute-done((bf16[2,4,48,768]{3,2,1,0:T(8,128)(2,1)S(1)}, bf16[2,4,48,768]{3,2,1,0:T(8,128)(2,1)S(1)}, u32[]{:S(2)}, u32[]{:S(2)}) %collective-permute-start.48) | collective-permute-done | bytes 589856 | tf_op jit(solution)/shard_map/ppermute | solution.py:27
  528.7 26.7 %collective-permute-done.77 = f32[8,768]{1,0:T(8,128)S(1)} collective-permute-done((f32[8,768]{1,0:T(8,128)S(1)}, f32[8,768]{1,0:T(8,128)S(1)}, u32[]{:S(2)}, u32[]{:S(2)}) %collective-permute-start.77) | collective-permute-done | bytes 24608 | tf_op jit(solution)/shard_map/ppermute | solution.py:27
  622.4 20.2 %collective-permute-done.68 = bf16[2,112,768]{2,1,0:T(8,128)(2,1)S(1)} collective-permute-done((bf16[2,112,768]{2,1,0:T(8,128)(2,1)S(1)}, bf16[2,112,768]{2,1,0:T(8,128)(2,1)S(1)}, u32[]{:S(2)}, u32[]{:S(2)}) %collective-permute-start.68) | collective-permute-done | bytes 344096 | tf_op jit(solution)/shard_map/ppermute | solution.py:32
  656.4 14.5 %collective-permute-done.57 = bf16[48,768]{1,0:T(8,128)(2,1)S(1)} collective-permute-done((bf16[48,768]{1,0:T(8,128)(2,1)S(1)}, bf16[48,768]{1,0:T(8,128)(2,1)S(1)}, u32[]{:S(2)}, u32[]{:S(2)}) %collective-permute-start.57) | collective-permute-done | bytes 73760 | tf_op jit(solution)/shard_map/ppermute | solution.py:27
  681.4 22.1 %collective-permute-done.86 = bf16[2,4,96,768]{3,2,1,0:T(8,128)(2,1)S(1)} collective-permute-done((bf16[2,4,96,768]{3,2,1,0:T(8,128)(2,1)S(1)}, bf16[2,4,96,768]{3,2,1,0:T(8,128)(2,1)S(1)}, u32[]{:S(2)}, u32[]{:S(2)}) %collective-permute-start.86) | collective-permute-done | bytes 1179680 | tf_op jit(solution)/shard_map/ppermute | solution.py:27
  712.0 8.8 %collective-permute-done.102 = bf16[4,96,768]{2,1,0:T(8,128)(2,1)S(1)} collective-permute-done((bf16[4,96,768]{2,1,0:T(8,128)(2,1)S(1)}, bf16[4,96,768]{2,1,0:T(8,128)(2,1)S(1)}, u32[]{:S(2)}, u32[]{:S(2)}) %collective-permute-start.102) | collective-permute-done | bytes 589856 | tf_op jit(solution)/shard_map/ppermute | solution.py:27
  723.1 10.0 %collective-permute-done.89 = bf16[4,96,768]{2,1,0:T(8,128)(2,1)S(1)} collective-permute-done((bf16[4,96,768]{2,1,0:T(8,128)(2,1)S(1)}, bf16[4,96,768]{2,1,0:T(8,128)(2,1)S(1)}, u32[]{:S(2)}, u32[]{:S(2)}) %collective-permute-start.89) | collective-permute-done | bytes 589856 | tf_op jit(solution)/shard_map/ppermute | solution.py:27
  734.1 10.7 %collective-permute-done.103 = bf16[2,96,768]{2,1,0:T(8,128)(2,1)S(1)} collective-permute-done((bf16[2,96,768]{2,1,0:T(8,128)(2,1)S(1)}, bf16[2,96,768]{2,1,0:T(8,128)(2,1)S(1)}, u32[]{:S(2)}, u32[]{:S(2)}) %collective-permute-start.103) | collective-permute-done | bytes 294944 | tf_op jit(solution)/shard_map/ppermute | solution.py:32
  (704 shorter events, 454.2 us)
Async XLA Ops:
  30.7 56.2 %collective-permute-start.30 = (bf16[2,96,768]{2,1,0:T(8,128)(2,1)}, bf16[2,96,768]{2,1,0:T(8,128)(2,1)}, u32[]{:S(2)}, u32[]{:S(2)}) collective-permute-start(bf16[2,96,768]{2,1,0:T(8,128)(2,1)} %constant_dynamic-slice_fusion.1), channel_id=1, source_target_pairs={{0,1},{1,2},{2,3},{3,0},{4,5},{5,6},{6,7},{7,4},{8,9},{9,10},{10,1... | collective-permute-start | bytes 884744 | tf_op jit(solution)/shard_map/ppermute | solution.py:32
  37.5 48.6 %collective-permute-start.22 = (bf16[2,64,768]{2,1,0:T(8,128)(2,1)}, bf16[2,64,768]{2,1,0:T(8,128)(2,1)}, u32[]{:S(2)}, u32[]{:S(2)}) collective-permute-start(bf16[2,64,768]{2,1,0:T(8,128)(2,1)} %pad_maximum_fusion.40), channel_id=1, source_target_pairs={{0,1},{1,2},{2,3},{3,0},{4,5},{5,6},{6,7},{7,4},{8,9},{9,10},{10,1... | collective-permute-start | bytes 589832 | tf_op jit(solution)/shard_map/ppermute | solution.py:32
  44.5 40.2 %collective-permute-start.3 = (bf16[2,48,768]{2,1,0:T(8,128)(2,1)}, bf16[2,48,768]{2,1,0:T(8,128)(2,1)}, u32[]{:S(2)}, u32[]{:S(2)}) collective-permute-start(bf16[2,48,768]{2,1,0:T(8,128)(2,1)} %bitcast.11), channel_id=1, source_target_pairs={{0,1},{1,2},{2,3},{3,0},{4,5},{5,6},{6,7},{7,4},{8,9},{9,10},{10,1... | collective-permute-start | bytes 442376 | tf_op jit(solution)/shard_map/ppermute | solution.py:32
  80.3 36.3 %collective-permute-start.18 = (bf16[2,3,144,768]{3,2,1,0:T(8,128)(2,1)}, bf16[2,3,144,768]{3,2,1,0:T(8,128)(2,1)}, u32[]{:S(2)}, u32[]{:S(2)}) collective-permute-start(bf16[2,3,144,768]{3,2,1,0:T(8,128)(2,1)} %pad_maximum_fusion.16), channel_id=1, source_target_pairs={{0,16},{4,20},{8,24},{12,28},{16,0},{20,4},{24,8},{28,12},{1,17},{... | collective-permute-start | bytes 3981320 | tf_op jit(solution)/shard_map/ppermute | solution.py:27
  82.6 35.7 %collective-permute-start.20 = (bf16[2,3,144,768]{3,2,1,0:T(8,128)(2,1)}, bf16[2,3,144,768]{3,2,1,0:T(8,128)(2,1)}, u32[]{:S(2)}, u32[]{:S(2)}) collective-permute-start(bf16[2,3,144,768]{3,2,1,0:T(8,128)(2,1)} %pad_maximum_fusion.17), channel_id=1, source_target_pairs={{0,8},{4,12},{8,0},{12,4},{16,24},{20,28},{24,16},{28,20},{1,9},{5... | collective-permute-start | bytes 3981320 | tf_op jit(solution)/shard_map/ppermute | solution.py:27
  122.8 146.8 %collective-permute-start.21 = (bf16[2,4,3,144,768]{4,3,2,1,0:T(8,128)(2,1)}, bf16[2,4,3,144,768]{4,3,2,1,0:T(8,128)(2,1)}, u32[]{:S(2)}, u32[]{:S(2)}) collective-permute-start(bf16[2,4,3,144,768]{4,3,2,1,0:T(8,128)(2,1)} %pad_maximum_fusion.1.piece0), channel_id=1, source_target_pairs={{0,4},{4,0},{8,12},{12,8},{16,20},{20,16},{24,28},{28,24},{1,5},{5... | collective-permute-start | bytes 15925256 | tf_op jit(solution)/shard_map/ppermute | solution.py:27
  138.2 36.1 %collective-permute-start.34 = (bf16[2,3,96,768]{3,2,1,0:T(8,128)(2,1)S(1)}, bf16[2,3,96,768]{3,2,1,0:T(8,128)(2,1)S(1)}, u32[]{:S(2)}, u32[]{:S(2)}) collective-permute-start(bf16[2,3,96,768]{3,2,1,0:T(8,128)(2,1)S(1)} %pad_maximum_fusion.21), channel_id=1, source_target_pairs={{0,16},{4,20},{8,24},{12,28},{16,0},{20,4},{24,8},{28,12},{1,17},{... | collective-permute-start | bytes 2654216 | tf_op jit(solution)/shard_map/ppermute | solution.py:27
  184.7 129.3 %collective-permute-start.37 = (bf16[2,4,3,96,768]{4,3,2,1,0:T(8,128)(2,1)}, bf16[2,4,3,96,768]{4,3,2,1,0:T(8,128)(2,1)}, u32[]{:S(2)}, u32[]{:S(2)}) collective-permute-start(bf16[2,4,3,96,768]{4,3,2,1,0:T(8,128)(2,1)} %pad_maximum_fusion.2.piece0), channel_id=1, source_target_pairs={{0,4},{4,0},{8,12},{12,8},{16,20},{20,16},{24,28},{28,24},{1,5},{5... | collective-permute-start | bytes 10616840 | tf_op jit(solution)/shard_map/ppermute | solution.py:27
  186.4 71.3 %collective-permute-start.29 = (bf16[2,4,3,64,768]{4,3,2,1,0:T(8,128)(2,1)}, bf16[2,4,3,64,768]{4,3,2,1,0:T(8,128)(2,1)}, u32[]{:S(2)}, u32[]{:S(2)}) collective-permute-start(bf16[2,4,3,64,768]{4,3,2,1,0:T(8,128)(2,1)} %pad_maximum_fusion.4.piece0), channel_id=1, source_target_pairs={{0,4},{4,0},{8,12},{12,8},{16,20},{20,16},{24,28},{28,24},{1,5},{5... | collective-permute-start | bytes 7077896 | tf_op jit(solution)/shard_map/ppermute | solution.py:27
  203.4 41.9 %collective-permute-start.10 = (bf16[2,4,3,48,768]{4,3,2,1,0:T(8,128)(2,1)}, bf16[2,4,3,48,768]{4,3,2,1,0:T(8,128)(2,1)}, u32[]{:S(2)}, u32[]{:S(2)}) collective-permute-start(bf16[2,4,3,48,768]{4,3,2,1,0:T(8,128)(2,1)} %pad_maximum_fusion.10.piece0), channel_id=1, source_target_pairs={{0,4},{4,0},{8,12},{12,8},{16,20},{20,16},{24,28},{28,24},{1,5},{5... | collective-permute-start | bytes 5308424 | tf_op jit(solution)/shard_map/ppermute | solution.py:27
  468.4 32.7 %collective-permute-start.61 = (bf16[2,4,4,48,768]{4,3,2,1,0:T(8,128)(2,1)S(1)}, bf16[2,4,4,48,768]{4,3,2,1,0:T(8,128)(2,1)S(1)}, u32[]{:S(2)}, u32[]{:S(2)}) collective-permute-start(bf16[2,4,4,48,768]{4,3,2,1,0:T(8,128)(2,1)S(1)} %get-tuple-element.126), channel_id=1, source_target_pairs={{0,4},{4,0},{8,12},{12,8},{16,20},{20,16},{24,28},{28,24},{1,5},{5... | collective-permute-start | bytes 7077896 | tf_op jit(solution)/shard_map/ppermute | solution.py:27
  492.2 123.4 %collective-permute-start.98 = (bf16[2,4,4,96,768]{4,3,2,1,0:T(8,128)(2,1)}, bf16[2,4,4,96,768]{4,3,2,1,0:T(8,128)(2,1)}, u32[]{:S(2)}, u32[]{:S(2)}) collective-permute-start(bf16[2,4,4,96,768]{4,3,2,1,0:T(8,128)(2,1)} %get-tuple-element.142), channel_id=1, source_target_pairs={{0,4},{4,0},{8,12},{12,8},{16,20},{20,16},{24,28},{28,24},{1,5},{5... | collective-permute-start | bytes 14155784 | tf_op jit(solution)/shard_map/ppermute | solution.py:27
  518.8 56.9 %collective-permute-start.63 = (bf16[2,4,112,768]{3,2,1,0:T(8,128)(2,1)S(1)}, bf16[2,4,112,768]{3,2,1,0:T(8,128)(2,1)S(1)}, u32[]{:S(2)}, u32[]{:S(2)}) collective-permute-start(bf16[2,4,112,768]{3,2,1,0:T(8,128)(2,1)S(1)} %get-tuple-element.195), channel_id=1, source_target_pairs={{0,16},{4,20},{8,24},{12,28},{16,0},{20,4},{24,8},{28,12},{1,17},{... | collective-permute-start | bytes 4128776 | tf_op jit(solution)/shard_map/ppermute | solution.py:27
  519.9 58.8 %collective-permute-start.65 = (bf16[2,4,112,768]{3,2,1,0:T(8,128)(2,1)S(1)}, bf16[2,4,112,768]{3,2,1,0:T(8,128)(2,1)S(1)}, u32[]{:S(2)}, u32[]{:S(2)}) collective-permute-start(bf16[2,4,112,768]{3,2,1,0:T(8,128)(2,1)S(1)} %get-tuple-element.194), channel_id=1, source_target_pairs={{0,8},{4,12},{8,0},{12,4},{16,24},{20,28},{24,16},{28,20},{1,9},{5... | collective-permute-start | bytes 4128776 | tf_op jit(solution)/shard_map/ppermute | solution.py:27
  562.6 81.1 %collective-permute-start.85 = (bf16[2,4,4,96,768]{4,3,2,1,0:T(8,128)(2,1)}, bf16[2,4,4,96,768]{4,3,2,1,0:T(8,128)(2,1)}, u32[]{:S(2)}, u32[]{:S(2)}) collective-permute-start(bf16[2,4,4,96,768]{4,3,2,1,0:T(8,128)(2,1)} %get-tuple-element.140), channel_id=1, source_target_pairs={{0,4},{4,0},{8,12},{12,8},{16,20},{20,16},{24,28},{28,24},{1,5},{5... | collective-permute-start | bytes 14155784 | tf_op jit(solution)/shard_map/ppermute | solution.py:27
  607.9 47.4 %collective-permute-start.38 = (bf16[8,40,768]{2,1,0:T(8,128)(2,1)S(1)}, bf16[8,40,768]{2,1,0:T(8,128)(2,1)S(1)}, u32[]{:S(2)}, u32[]{:S(2)}) collective-permute-start(bf16[8,40,768]{2,1,0:T(8,128)(2,1)S(1)} %copy-done.17), channel_id=1, source_target_pairs={{0,1},{1,2},{2,3},{3,0},{4,5},{5,6},{6,7},{7,4},{8,9},{9,10},{10,1... | collective-permute-start | bytes 1474568 | tf_op jit(solution)/shard_map/ppermute | solution.py:32
  607.9 71.4 %collective-permute-start.45 = (bf16[8,40,768]{2,1,0:T(8,128)(2,1)S(1)}, bf16[8,40,768]{2,1,0:T(8,128)(2,1)}, u32[]{:S(2)}, u32[]{:S(2)}) collective-permute-start(bf16[8,40,768]{2,1,0:T(8,128)(2,1)S(1)} %collective-permute-done.44), channel_id=1, source_target_pairs={{0,1},{1,2},{2,3},{3,0},{4,5},{5,6},{6,7},{7,4},{8,9},{9,10},{10,1... | collective-permute-start | bytes 1474568 | tf_op jit(solution)/shard_map/ppermute | solution.py:32
  621.3 58.1 %collective-permute-start.101 = (bf16[2,4,96,768]{3,2,1,0:T(8,128)(2,1)S(1)}, bf16[2,4,96,768]{3,2,1,0:T(8,128)(2,1)S(1)}, u32[]{:S(2)}, u32[]{:S(2)}) collective-permute-start(bf16[2,4,96,768]{3,2,1,0:T(8,128)(2,1)S(1)} %get-tuple-element.198), channel_id=1, source_target_pairs={{0,8},{4,12},{8,0},{12,4},{16,24},{20,28},{24,16},{28,20},{1,9},{5... | collective-permute-start | bytes 3538952 | tf_op jit(solution)/shard_map/ppermute | solution.py:27
  642.5 37.0 %collective-permute-start.99 = (bf16[2,4,96,768]{3,2,1,0:T(8,128)(2,1)S(1)}, bf16[2,4,96,768]{3,2,1,0:T(8,128)(2,1)S(1)}, u32[]{:S(2)}, u32[]{:S(2)}) collective-permute-start(bf16[2,4,96,768]{3,2,1,0:T(8,128)(2,1)S(1)} %get-tuple-element.199), channel_id=1, source_target_pairs={{0,16},{4,20},{8,24},{12,28},{16,0},{20,4},{24,8},{28,12},{1,17},{... | collective-permute-start | bytes 3538952 | tf_op jit(solution)/shard_map/ppermute | solution.py:27
  679.4 116.3 %collective-permute-start.39 = (bf16[8,40,768]{2,1,0:T(8,128)(2,1)S(1)}, bf16[8,40,768]{2,1,0:T(8,128)(2,1)}, u32[]{:S(2)}, u32[]{:S(2)}) collective-permute-start(bf16[8,40,768]{2,1,0:T(8,128)(2,1)S(1)} %collective-permute-done.38), channel_id=1, source_target_pairs={{0,1},{1,2},{2,3},{3,0},{4,5},{5,6},{6,7},{7,4},{8,9},{9,10},{10,1... | collective-permute-start | bytes 1474568 | tf_op jit(solution)/shard_map/ppermute | solution.py:32
  679.5 117.9 %collective-permute-start.46 = (bf16[8,40,768]{2,1,0:T(8,128)(2,1)}, bf16[8,40,768]{2,1,0:T(8,128)(2,1)}, u32[]{:S(2)}, u32[]{:S(2)}) collective-permute-start(bf16[8,40,768]{2,1,0:T(8,128)(2,1)} %collective-permute-done.45), channel_id=1, source_target_pairs={{0,1},{1,2},{2,3},{3,0},{4,5},{5,6},{6,7},{7,4},{8,9},{9,10},{10,1... | collective-permute-start | bytes 1474568 | tf_op jit(solution)/shard_map/ppermute | solution.py:32
  710.9 34.1 %collective-permute-start.73 = (bf16[2,112,768]{2,1,0:T(8,128)(2,1)S(1)}, bf16[2,112,768]{2,1,0:T(8,128)(2,1)S(1)}, u32[]{:S(2)}, u32[]{:S(2)}) collective-permute-start(bf16[2,112,768]{2,1,0:T(8,128)(2,1)S(1)} %pad_maximum_fusion.33), channel_id=1, source_target_pairs={{0,8},{4,12},{8,0},{12,4},{16,24},{20,28},{24,16},{28,20},{1,9},{5... | collective-permute-start | bytes 1032200 | tf_op jit(solution)/shard_map/ppermute | solution.py:27
  795.7 40.2 %collective-permute-start.110 = (bf16[2,4,96,768]{3,2,1,0:T(8,128)(2,1)}, bf16[2,4,96,768]{3,2,1,0:T(8,128)(2,1)}, u32[]{:S(2)}, u32[]{:S(2)}) collective-permute-start(bf16[2,4,96,768]{3,2,1,0:T(8,128)(2,1)} %pad_maximum_fusion.19.result0), channel_id=1, source_target_pairs={{0,4},{4,0},{8,12},{12,8},{16,20},{20,16},{24,28},{28,24},{1,5},{5... | collective-permute-start | bytes 3538952 | tf_op jit(solution)/shard_map/ppermute | solution.py:27
  796.3 44.5 %collective-permute-start.97 = (bf16[2,4,96,768]{3,2,1,0:T(8,128)(2,1)S(1)}, bf16[2,4,96,768]{3,2,1,0:T(8,128)(2,1)}, u32[]{:S(2)}, u32[]{:S(2)}) collective-permute-start(bf16[2,4,96,768]{3,2,1,0:T(8,128)(2,1)S(1)} %pad_maximum_fusion.18.result0), channel_id=1, source_target_pairs={{0,4},{4,0},{8,12},{12,8},{16,20},{20,16},{24,28},{28,24},{1,5},{5... | collective-permute-start | bytes 3538952 | tf_op jit(solution)/shard_map/ppermute | solution.py:27
  (229 other events, 2846.7 us)

commit v2 on v1

v2 whole, which is shorter than its diff:
```python
from functools import partial

import jax
import jax.numpy as jnp
from jax import lax
from jax.experimental import pallas as pl
from jax.experimental.pallas import tpu as pltpu
from jax.sharding import PartitionSpec as P

HEAD_DIM = 64
STACK = 4 * HEAD_DIM
TOGETHER = 6
SLICES = 8
EPSILON = 1e-06
BLOCKED = -1000000000.0
SCALE = HEAD_DIM ** (-0.5)
DISTANCES = ((0, 2, 4, 6), (0, 4, 2, 6))
F32 = jnp.float32
BF16 = jnp.bfloat16

ANY = pl.BlockSpec(memory_space=pl.ANY)
VMEM = pl.BlockSpec(memory_space=pltpu.VMEM)
SMEM = pl.BlockSpec(memory_space=pltpu.SMEM)


def swap(values, bit):
    count = lax.axis_size("dp")
    return lax.ppermute(values, "dp", [(i, i ^ bit) for i in range(count)])


def pass_on(values, way=1):
    count = lax.axis_size("mp")
    return lax.ppermute(values, "mp", [(i, (i + way) % count) for i in range(count)])


def swap_owner(values, bit):
    count = lax.axis_size("mp")
    return lax.ppermute(values, "mp", [(i, i ^ bit) for i in range(count)])


def added(*terms):
    total = terms[0].astype(F32)
    for term in terms[1:]:
        total = total + term
    return total.astype(BF16)


def dot_nn(left, right):
    return lax.dot_general(left, right, (((1,), (0,)), ((), ())), preferred_element_type=F32)


def dot_nt(left, right):
    return lax.dot_general(left, right, (((1,), (1,)), ((), ())), preferred_element_type=F32)


def dot_tn(left, right):
    return lax.dot_general(left, right, (((0,), (0,)), ((), ())), preferred_element_type=F32)


def start(source, target, sem):
    pltpu.make_async_copy(source, target, sem).start()


def finish(whole, sem):
    pltpu.make_async_copy(whole, whole, sem).wait()


def aligned(first, count, step=16):
    return pl.ds(pl.multiple_of(first, step), count)


def each_slice(place, first_step, mp):
    for core in range(2):
        for half in range(2):
            for entry in range(4):
                slot = place[0] ^ (core ^ DISTANCES[half][entry])
                for step in range(first_step, mp):
                    yield core, half, entry, step, slot, (place[1] + mp - step) % mp


def piece_of(pieces, core, half, entry):
    return pieces[4 * core + 2 * half + entry // 2].at[entry % 2]


def attention_spot(whole, quarter, half, slot, owner):
    span = 4 * quarter // SLICES
    count = quarter // span
    row = owner * quarter + (slot % count) * span + half * (span // 2)
    return whole.at[slot // count, aligned(row, span // 2)]


def load_attention(place, own, pieces, offset, layer, whole, sems):
    mp = pieces[0].shape[1] + 1
    quarter = whole.shape[1] // mp
    rows = quarter // 4
    for mat in range(4):
        source = own[0].at[layer, mat] if mat < 3 else own[1].at[layer]
        start(source, whole.at[mat, aligned(place[1] * quarter, quarter)], sems.at[mat])
    for core, half, entry, step, slot, owner in each_slice(place, 1, mp):
        start(
            piece_of(pieces, core, half, entry).at[step - 1, pl.ds(offset, rows)],
            attention_spot(whole, quarter, half, slot, owner),
            sems.at[slot // 2],
        )


def store_attention(place, whole, outs, offset, sem):
    mp = outs[0].shape[2]
    quarter = whole.shape[1] // mp
    for core, half, entry, step, slot, owner in each_slice(place, 0, mp):
        start(
            attention_spot(whole, quarter, half, slot, owner),
            outs[core].at[half, entry, step, pl.ds(offset, quarter // 4)],
            sem,
        )


def feed_spot(whole, half, slot, owner):
    span = whole.shape[2] // SLICES
    return whole.at[half, owner, aligned(slot * span, span)]


def load_feed(place, own, pieces, offset, layer, whole, sems):
    mp = pieces[0].shape[1] + 1
    rows = whole.shape[2] // SLICES
    for half in range(2):
        start(own[half].at[layer], whole.at[half, place[1]], sems.at[half, place[1]])
    for core, half, entry, step, slot, owner in each_slice(place, 1, mp):
        start(
            piece_of(pieces, core, half, entry).at[step - 1, pl.ds(offset, rows)],
            feed_spot(whole, half, slot, owner),
            sems.at[half, owner],
        )


def store_feed(place, whole, outs, sem):
    mp = outs[0].shape[2]
    for core, half, entry, step, slot, owner in each_slice(place, 0, mp):
        start(feed_spot(whole, half, slot, owner), outs[core].at[half, entry, step], sem)


def image_copies(whole, piece, quarter, half, slot, owner, sem, inward):
    rows, width = piece.shape
    span = 2 * rows
    beyond = whole.shape[1] - width
    blocks = width // beyond
    plain = quarter // span
    base = owner * quarter + half * rows

    def move(inner, outer):
        start(inner, outer, sem) if inward else start(outer, inner, sem)

    @pl.when(slot < plain)
    def _():
        move(piece, whole.at[aligned(base + slot * span, rows), pl.ds(0, width)])

    @pl.when(slot >= plain)
    def _():
        for block in range(blocks):
            row = base + block * (quarter // blocks) + (slot - plain) * span
            move(
                piece.at[:, pl.ds(block * beyond, beyond)],
                whole.at[aligned(row, rows), pl.ds(width, beyond)],
            )


def load_image(place, own, pieces, offset, rows, whole, sem):
    mp = pieces[0].shape[1] + 1
    quarter = whole.shape[0] // mp
    start(own, whole.at[aligned(place[1] * quarter, quarter)], sem)
    for core, half, entry, step, slot, owner in each_slice(place, 1, mp):
        piece = piece_of(pieces, core, half, entry).at[step - 1, pl.ds(offset, rows)]
        image_copies(whole, piece, quarter, half, slot, owner, sem, True)


def store_image(place, whole, outs, offset, rows, sem):
    mp = outs[0].shape[2]
    quarter = whole.shape[0] // mp
    for core, half, entry, step, slot, owner in each_slice(place, 0, mp):
        piece = outs[core].at[half, entry, step, pl.ds(offset, rows)]
        image_copies(whole, piece, quarter, half, slot, owner, sem, False)


def norm_rows(values, gain_row, shift_row):
    center = values - jnp.mean(values, axis=-1, keepdims=True)
    moment = jnp.mean(center * center, axis=-1, keepdims=True)
    return center * lax.rsqrt(moment + EPSILON) * gain_row + shift_row


def norm_back(pre_norm, gain_row, grad_out, small):
    center = pre_norm - jnp.mean(pre_norm, axis=-1, keepdims=True)
    scale = lax.rsqrt(jnp.mean(center * center, axis=-1, keepdims=True) + EPSILON)
    normal = center * scale
    lifted = grad_out * gain_row
    grad_pre = scale * (
        lifted
        - jnp.mean(lifted, axis=-1, keepdims=True)
        - normal * jnp.mean(lifted * normal, axis=-1, keepdims=True)
    )
    small[...] = jnp.zeros_like(small)
    small[0:1] = jnp.sum(grad_out * normal, axis=0, keepdims=True)
    small[1:2] = jnp.sum(grad_out, axis=0, keepdims=True)
    small[2:3] = jnp.sum(grad_pre, axis=0, keepdims=True)
    return grad_pre


def column_total(values):
    return jnp.sum(values.astype(F32), axis=0, keepdims=True)


def spread_heads(values):
    lane = lax.broadcasted_iota(jnp.int32, (1, values.shape[1]), 1)
    parts = []
    for first in range(0, values.shape[1], HEAD_DIM):
        mask = ((lane >= first) & (lane < first + HEAD_DIM)).astype(F32).astype(values.dtype)
        parts.append(values * mask)
    return jnp.concatenate(parts, axis=0)


def pick_heads(values):
    lane = lax.broadcasted_iota(jnp.int32, (1, values.shape[1]), 1)
    rows = values.shape[0] * HEAD_DIM // values.shape[1]
    picked = values[:rows]
    for head in range(1, values.shape[1] // HEAD_DIM):
        picked = jnp.where(lane >= head * HEAD_DIM, values[head * rows : (head + 1) * rows], picked)
    return picked


def softmax(scores):
    raised = jnp.exp(scores - jnp.max(scores, axis=-1, keepdims=True))
    return raised * (1.0 / jnp.sum(raised, axis=-1, keepdims=True))


def score_back(weights, grad_weights):
    along = weights * grad_weights
    return (along - weights * jnp.sum(along, axis=-1, keepdims=True)).astype(BF16)


def attention_units(count, row_size, place_size, width):
    units = []
    for number in range(count):
        rows = slice(number * row_size, (number + 1) * row_size)
        places = slice(number * place_size, (number + 1) * place_size)
        units += [(number, rows, places, slice(first, first + STACK)) for first in range(0, width, STACK)]
    return [units[first : first + TOGETHER] for first in range(0, len(units), TOGETHER)]


def attend_forward(units, allowed, query, keys, value, context):
    for group in units:
        scores = [dot_nt(spread_heads(query[rows, lanes]).astype(BF16), keys[at, lanes]) for _, rows, at, lanes in group]
        weights = [
            softmax(jnp.where(allowed(unit[0]), score * SCALE, BLOCKED)).astype(BF16)
            for unit, score in zip(group, scores)
        ]
        for (_, rows, at, lanes), weight in zip(group, weights):
            context[rows, lanes] = pick_heads(dot_nn(weight, value[at, lanes])).astype(context.dtype)


def attend_backward(units, allowed, query, keys, value, grad_context, grad_query, grad_keys, grad_value):
    for group in units:
        queries = [spread_heads(query[rows, lanes]).astype(BF16) for _, rows, _, lanes in group]
        contexts = [spread_heads(grad_context[rows, lanes]).astype(BF16) for _, rows, _, lanes in group]
        scores = [dot_nt(one, keys[at, lanes]) for one, (_, _, at, lanes) in zip(queries, group)]
        grad_weights = [dot_nt(one, value[at, lanes]) for one, (_, _, at, lanes) in zip(contexts, group)]
        weights = [
            softmax(jnp.where(allowed(unit[0]), score * SCALE, BLOCKED)) for unit, score in zip(group, scores)
        ]
        grad_scores = [score_back(one, other) for one, other in zip(weights, grad_weights)]
        for weight, one, (_, _, at, lanes) in zip(weights, contexts, group):
            grad_value[at, lanes] = dot_tn(weight.astype(BF16), one).astype(BF16)
        for grad_score, one, (_, _, at, lanes) in zip(grad_scores, queries, group):
            grad_keys[at, lanes] = (dot_tn(grad_score, one) * SCALE).astype(BF16)
        for grad_score, (_, rows, at, lanes) in zip(grad_scores, group):
            mixed = pick_heads(dot_nn(grad_score, keys[at, lanes])) * SCALE
            grad_query[rows, lanes] = mixed.astype(grad_query.dtype)


def same_segment(code_col, code_row):
    size = code_row.shape[1]

    def allowed(group):
        column = code_col[group * size : (group + 1) * size]
        return jnp.concatenate([column] * (STACK // HEAD_DIM), axis=0) == code_row[group : group + 1]

    return allowed


def real_patch(size, patches):
    column = lax.broadcasted_iota(jnp.int32, (1, size), 1)
    return lambda row: column < patches


def gather_rows(picks, rows_ref, target):
    seq = rows_ref.shape[1]
    for row in range(target.shape[0] // seq):
        target[row * seq : (row + 1) * seq] = rows_ref[picks[row]].astype(target.dtype)


def leave_rows(values, target):
    seq = target.shape[1]
    for row in range(target.shape[0]):
        target[row] = values[row * seq : (row + 1) * seq].astype(target.dtype)


def slice_kernel(place, inward, outward, feed_in, feed_out, image, text, first, joining, cross, last, sems):
    slot = place[0]
    quarter, width = inward.shape[2:]
    span = 4 * quarter // SLICES
    count = quarter // span
    rows = span // 2

    def attention(layer, target, offset, sem):
        for half in range(2):
            row = (slot % count) * span + half * rows
            spot = target.at[half, pl.ds(offset, rows)]

            @pl.when(slot < 3 * count)
            def _():
                start(inward.at[layer, slot // count, aligned(row, rows)], spot, sem)

            @pl.when(slot >= 3 * count)
            def _():
                start(outward.at[layer, aligned(row, rows)], spot, sem)

    def feed(layer, target, sem):
        size = feed_in.shape[1] // SLICES
        for half, source in enumerate((feed_in, feed_out)):
            start(source.at[layer, aligned(slot * size, size)], target.at[half, pl.ds(0, size)], sem)

    image_rows = cross.shape[1] - rows
    attention(0, text, 0, sems.at[0])
    attention(2, cross, 0, sems.at[3])
    for half in range(2):
        image_copies(image, cross.at[half, pl.ds(rows, image_rows)], quarter, half, slot, 0, sems.at[3], False)
    feed(0, first, sems.at[1])
    attention(1, joining, 0, sems.at[2])
    feed(1, last, sems.at[4])
    for number, target in enumerate((text, first, joining, cross, last)):
        finish(target, sems.at[number])


def self_forward_kernel(
    pick, layer, norm, offset, place, picks, rows_ref, inward, outward, *refs,
):
    pieces, refs = refs[:8], refs[8:]
    bias, params, code_col, code_row, out, low, pre, query, keys, value, context, whole, sems, *held = refs
    load_attention(place, (inward, outward), pieces, offset, layer, whole, sems)
    if pick:
        gather_rows(picks, rows_ref, held[0])
        stream = held[0][...]
    else:
        stream = rows_ref[...]
    hb = stream.astype(BF16)
    low[...] = hb
    finish(whole.at[0], sems.at[0])
    query[...] = (dot_nt(hb, whole[0]) + bias[2 * layer : 2 * layer + 1]).astype(BF16)
    finish(whole.at[1], sems.at[1])
    keys[...] = dot_nt(hb, whole[1]).astype(BF16)
    finish(whole.at[2], sems.at[2])
    value[...] = (dot_nt(hb, whole[2]) + bias[2 * layer + 1 : 2 * layer + 2]).astype(BF16)
    groups, size = code_row.shape
    units = attention_units(groups, size, size, hb.shape[1])
    attend_forward(units, same_segment(code_col, code_row), query, keys, value, context)
    finish(whole.at[3], sems.at[3])
    total = dot_nn(context[...], whole[3]) + params[3 * norm : 3 * norm + 1] + stream
    pre[...] = total
    out[...] = norm_rows(total, params[3 * norm + 1 : 3 * norm + 2], params[3 * norm + 2 : 3 * norm + 3])


def self_backward_kernel(
    leave, layer, norm, offset, spot, n_held, place, grad, low, pre, query, keys, value, context, inward, outward, *refs,
):
    pieces, refs = refs[:8], refs[8:]
    params, code_col, code_row = refs[:3]
    out, small, keep, send, whole, grads, grad_context, grad_query, grad_keys, grad_value, sems, out_sem = refs[3 + n_held :]
    load_attention(place, (inward, outward), pieces, offset, layer, whole, sems)
    grad_pre = norm_back(pre[...], params[3 * norm + 1 : 3 * norm + 2], grad[...], small)
    branch = grad_pre.astype(BF16)
    finish(whole.at[3], sems.at[3])
    grad_context[...] = dot_nt(branch, whole[3]).astype(BF16)
    grads[3] = dot_tn(context[...], branch).astype(BF16)
    groups, size = code_row.shape
    units = attention_units(groups, size, size, branch.shape[1])
    attend_backward(
        units, same_segment(code_col, code_row), query, keys, value, grad_context, grad_query, grad_keys, grad_value
    )
    hb = low[...]
    grads[0] = dot_tn(grad_query[...], hb).astype(BF16)
    grads[1] = dot_tn(grad_keys[...], hb).astype(BF16)
    grads[2] = dot_tn(grad_value[...], hb).astype(BF16)
    store_attention(place, grads, (keep, send), spot, out_sem)
    small[3:4] = column_total(grad_query[...])
    small[4:5] = column_total(grad_value[...])
    total = grad_pre
    for mat, part in enumerate((grad_query, grad_keys, grad_value)):
        finish(whole.at[mat], sems.at[mat])
        total = total + dot_nn(part[...], whole[mat])
    if leave:
        leave_rows(total, out)
    else:
        out[...] = total
    finish(grads, out_sem)


def feed_forward_kernel(
    leave, layer, norm, offset, place, rows_ref, first_weight, second_weight, *refs,
):
    pieces, refs = refs[:8], refs[8:]
    bias, params, out, low, pre, slope, active, whole, sems = refs
    load_feed(place, (first_weight, second_weight), pieces, offset, layer, whole, sems)
    stream = rows_ref[...]
    hb = stream.astype(BF16)
    low[...] = hb
    parts, size = whole.shape[1], whole.shape[3]
    total = params[3 * norm : 3 * norm + 1] + stream
    for part in range(parts):
        lanes = slice(part * size, (part + 1) * size)
        row = 6 + layer * parts + part
        finish(whole.at[0, part], sems.at[0, part])
        units = dot_nn(hb, whole[0, part]) + bias[row : row + 1]
        share = 0.5 * (1.0 + lax.erf(units * (2.0 ** -0.5)))
        slope[:, lanes] = share + units * jnp.exp(-0.5 * units * units) * 0.3989422804014327
        gated = (units * share).astype(BF16)
        active[:, lanes] = gated
        finish(whole.at[1, part], sems.at[1, part])
        total = total + dot_nn(gated, whole[1, part])
    pre[...] = total
    result = norm_rows(total, params[3 * norm + 1 : 3 * norm + 2], params[3 * norm + 2 : 3 * norm + 3])
    if leave:
        leave_rows(result, out)
    else:
        out[...] = result


def feed_backward_kernel(
    pick, layer, norm, offset, place, picks, grad, low, pre, slope, active, first_weight, second_weight, *refs,
):
    pieces, refs = refs[:8], refs[8:]
    params, out, small, keep, send, whole, grads, sems, out_sem, *held = refs
    load_feed(place, (first_weight, second_weight), pieces, offset, layer, whole, sems)
    if pick:
        gather_rows(picks, grad, held[0])
        grad = held[0]
    grad_pre = norm_back(pre[...], params[3 * norm + 1 : 3 * norm + 2], grad[...], small)
    branch = grad_pre.astype(BF16)
    parts, size = whole.shape[1], whole.shape[3]
    hb = low[...]
    total = grad_pre
    for part in range(parts):
        lanes = slice(part * size, (part + 1) * size)
        grads[1, part] = dot_tn(active[:, lanes], branch).astype(BF16)
        finish(whole.at[1, part], sems.at[1, part])
        grad_units = (dot_nt(branch, whole[1, part]) * slope[:, lanes]).astype(BF16)
        grads[0, part] = dot_tn(hb, grad_units).astype(BF16)
        small[3 + part : 4 + part] = column_total(grad_units)
        finish(whole.at[0, part], sems.at[0, part])
        total = total + dot_nt(grad_units, whole[0, part])
    store_feed(place, grads, (keep, send), out_sem)
    out[...] = total
    finish(grads, out_sem)


def finish_all(whole, sems):
    for mat in range(whole.shape[0]):
        finish(whole.at[mat], sems.at[mat])


def image_forward_kernel(
    layer, offset, image_offset, image_rows, place, images, image, inward, outward, *refs,
):
    pieces, refs = refs[:8], refs[8:]
    bias, projected, keys, value, whole, whole_image, sems, image_sem = refs
    load_image(place, image, pieces, image_offset, image_rows, whole_image, image_sem)
    load_attention(place, (inward, outward), pieces, offset, layer, whole, sems)
    finish(whole_image, image_sem)
    size = images.shape[0] // 4
    last = bias.shape[0] - 1
    for first in range(0, images.shape[0], size):
        rows = slice(first, first + size)
        source = (dot_nt(images[rows], whole_image[...]) + bias[last : last + 1]).astype(BF16)
        projected[rows] = source
        if first == 0:
            finish_all(whole, sems)
        keys[rows] = dot_nt(source, whole[1]).astype(BF16)
        value[rows] = (dot_nt(source, whole[2]) + bias[2 * layer + 1 : 2 * layer + 2]).astype(BF16)


def cross_forward_kernel(
    layer, norm, offset, seq, patches, place, rows_ref, keys, value, inward, outward, *refs,
):
    pieces, refs = refs[:8], refs[8:]
    bias, params, out, low, pre, query, context, whole, mixed, sems = refs
    load_attention(place, (inward, outward), pieces, offset, layer, whole, sems)
    stream = rows_ref[...]
    hb = stream.astype(BF16)
    low[...] = hb
    finish_all(whole, sems)
    query[...] = (dot_nt(hb, whole[0]) + bias[2 * layer : 2 * layer + 1]).astype(BF16).astype(F32)
    count = stream.shape[0] // seq
    size = keys.shape[0] // count
    units = attention_units(count, seq, size, hb.shape[1])
    attend_forward(units, real_patch(size, patches), query, keys, value, mixed)
    context[...] = mixed[...].astype(BF16)
    total = dot_nn(context[...], whole[3]) + params[3 * norm : 3 * norm + 1] + stream
    pre[...] = total
    out[...] = norm_rows(total, params[3 * norm + 1 : 3 * norm + 2], params[3 * norm + 2 : 3 * norm + 3])


def cross_backward_kernel(
    layer, norm, offset, spot, seq, patches, place, grad, low, pre, query, context, keys, value, source, inward, outward,
    *refs,
):
    pieces, refs = refs[:8], refs[8:]
    params, out, small, keep, send, grad_keys, grad_value, whole, grads, grad_context, grad_query, sems, out_sem = refs
    load_attention(place, (inward, outward), pieces, offset, layer, whole, sems)
    grad_pre = norm_back(pre[...], params[3 * norm + 1 : 3 * norm + 2], grad[...], small)
    branch = grad_pre.astype(BF16)
    finish_all(whole, sems)
    grad_context[...] = dot_nt(branch, whole[3]).astype(BF16).astype(F32)
    grads[3] = dot_tn(context[...], branch).astype(BF16)
    count = branch.shape[0] // seq
    size = keys.shape[0] // count
    units = attention_units(count, seq, size, branch.shape[1])
    attend_backward(
        units, real_patch(size, patches), query, keys, value, grad_context, grad_query, grad_keys, grad_value
    )
    query_low = grad_query[...].astype(BF16)
    grads[0] = dot_tn(query_low, low[...]).astype(BF16)
    grads[1] = dot_tn(grad_keys[...], source[...]).astype(BF16)
    grads[2] = dot_tn(grad_value[...], source[...]).astype(BF16)
    store_attention(place, grads, (keep, send), spot, out_sem)
    small[3:4] = column_total(query_low)
    small[4:5] = column_total(grad_value[...])
    out[...] = grad_pre + dot_nn(query_low, whole[0])
    finish(grads, out_sem)


def image_backward_kernel(
    layer, offset, image_offset, image_rows, spot, n_held, place, images, grad_keys, grad_value, image, inward, outward,
    *refs,
):
    pieces, refs = refs[:8], refs[8 + n_held :]
    out, small, keep, send, whole, whole_image, grads, low, sems, image_sem, out_sem = refs
    load_attention(place, (inward, outward), pieces, offset, layer, whole, sems)
    load_image(place, image, pieces, image_offset, image_rows, whole_image, image_sem)
    finish_all(whole, sems)
    finish(whole_image, image_sem)
    count, patches = out.shape[:2]
    size = images.shape[0] // count
    small[...] = jnp.zeros_like(small)
    for row in range(count):
        rows = slice(row * size, (row + 1) * size)
        source = dot_nn(grad_keys[rows], whole[1]) + dot_nn(grad_value[rows], whole[2])
        source = source.astype(BF16)
        low[rows] = source
        out[row] = dot_nn(source, whole_image[...])[:patches]
    grads[...] = dot_tn(low[...], images[...]).astype(BF16)
    store_image(place, grads, (keep, send), spot, image_rows, out_sem)
    small[0:1] = column_total(low[...])
    finish(grads, out_sem)


def pick_kernel(picks, rows_ref, out):
    for row in range(out.shape[0]):
        out[row] = rows_ref[picks[row]].astype(out.dtype)


def finish_kernel(blocks, quarter, names, held, place, *refs):
    results, refs = refs[:8], refs[8:]
    width = results[0].shape[2]
    targets = dict(zip(names, refs[held:]))
    scratch = refs[held + len(names) :]
    sem, out_sem = scratch[-2:]
    for number, (kind, offset, _) in enumerate(blocks):
        buffer = scratch[2 * number]
        for core in range(2):
            for half in range(2):
                for entry in range(4):
                    slot = place[0] ^ (core ^ DISTANCES[half][entry])
                    piece = piece_of(results, core, half, entry)
                    if kind == "attention":
                        rows = quarter // 4
                        spot = attention_spot(buffer, quarter, half, slot, 0)
                        start(piece.at[pl.ds(offset, rows)], spot, sem.at[number])
                    elif kind == "feed":
                        rows = buffer.shape[1] // SLICES
                        spot = buffer.at[half, aligned(slot * rows, rows)]
                        start(piece.at[pl.ds(offset, rows)], spot, sem.at[number])
                    else:
                        rows = quarter * buffer.shape[1] // width // SLICES // 2
                        piece = piece.at[pl.ds(offset, rows)]
                        image_copies(buffer, piece, quarter, half, slot, 0, sem.at[number], True)
    for number, (kind, _, layer) in enumerate(blocks):
        buffer, wide = scratch[2 * number : 2 * number + 2]
        done = out_sem.at[number]
        finish(buffer, sem.at[number])
        wide[...] = buffer[...].astype(F32)
        if kind == "attention":
            start(wide.at[pl.ds(0, 3)], targets["attention_in"].at[layer], done)
            start(wide.at[3], targets["attention_out"].at[layer], done)
        elif kind == "feed":
            start(wide.at[0], targets["feed_in"].at[layer], done)
            start(wide.at[1], targets["feed_out"].at[layer], done)
        else:
            start(wide, targets["image"], done)
    for number in range(len(blocks)):
        finish(scratch[2 * number + 1], out_sem.at[number])


def shape(dims, kind=F32):
    return jax.ShapeDtypeStruct(tuple(dims), kind)


def call(kernel, ins, outs, scratch, megabytes, aliases=None):
    return pl.pallas_call(
        kernel,
        in_specs=[spec for _, spec in ins],
        out_specs=[spec for _, spec in outs],
        out_shape=[s for s, _ in outs],
        scratch_shapes=scratch,
        input_output_aliases=aliases or {},
        compiler_params=pltpu.CompilerParams(vmem_limit_bytes=megabytes << 20),
        cost_estimate=pl.CostEstimate(flops=0, bytes_accessed=0, transcendentals=0),
    )(*[v for v, _ in ins])


class Ring:
    def __init__(self, at, name, own):
        self.at, self.name = at, name
        at[name] = {0: own}

    def up(self):
        parts = self.at[self.name]
        parts[1] = pass_on(parts[0])

    def down(self):
        parts = self.at[self.name]
        parts[3] = pass_on(parts[0], -1)

    def far(self):
        parts = self.at[self.name]
        parts[2] = pass_on(parts[1])

    def take(self):
        parts = self.at.pop(self.name)
        return [parts[i] for i in range(4)]


class Widen:
    def __init__(self, at, name, first, second):
        self.at, self.name = at, name
        at[name] = {"own": (first, second)}

    def one(self):
        held = self.at[self.name]
        first, second = held.pop("own")
        held["both"] = (first, swap(first, 2), second, swap(second, 4))

    def two(self):
        held = self.at[self.name]
        both = held.pop("both")
        near = jnp.stack(both[:2]), jnp.stack(both[2:])
        held["near"] = near
        held["far"] = swap(near[0], 4), swap(near[1], 2)
        held["near core"] = swap(near[0], 1), swap(near[1], 1)

    def core(self):
        held = self.at[self.name]
        held["far core"] = swap(held["far"][0], 1), swap(held["far"][1], 1)

    def take(self):
        held = self.at.pop(self.name)
        return [held[kind + core][half] for core in ("", " core") for half in range(2) for kind in ("near", "far")]


class Reduce:
    def __init__(self, at, name, keep, send):
        self.at, self.name = at, name
        at[name] = {"keep": keep, "send": send}

    def core(self):
        held = self.at[self.name]
        held["core"] = swap(held.pop("send"), 1)

    def one(self):
        held = self.at[self.name]
        keep, core = held["keep"], held["core"]
        held["one"] = swap(added(keep[0, 2:], core[0, 2:]), 4), swap(added(keep[1, 2:], core[1, 2:]), 2)

    def two(self):
        held = self.at[self.name]
        keep, core, one = held["keep"], held["core"], held["one"]
        held["two"] = (
            swap(added(keep[0, 1], core[0, 1], one[0][1]), 2),
            swap(added(keep[1, 1], core[1, 1], one[1][1]), 4),
        )

    def part(self, step, *more):
        held = self.at[self.name]
        keep, core, one, two = held["keep"], held["core"], held["one"], held["two"]
        return jnp.stack(
            [
                added(keep[i, 0, step], core[i, 0, step], one[i][0, step], two[i][step], *[term[i] for term in more])
                for i in range(2)
            ]
        )

    def far(self):
        held = self.at[self.name]
        held["far"] = pass_on(self.part(2))

    def near(self):
        held = self.at[self.name]
        held["up"] = pass_on(self.part(3, held.pop("far")))
        held["down"] = pass_on(self.part(1), -1)

    def widen(self):
        held = self.at[self.name]
        own = self.part(0, held["up"], held["down"])
        self.at.pop(self.name)
        bit = SLICES
        while bit < lax.axis_size("dp"):
            own = added(own, swap(own, bit))
            bit *= 2
        return Widen(self.at, self.name, own[0], own[1])


def on_device(
    tokens, images, segment_of_token, image_of_row, attention_in, query_value_bias, attention_out, output_bias,
    feed_in, feed_bias, feed_out, image_weight, image_bias, norm_gain, norm_bias, cotangent,
):
    mp = lax.axis_size("mp")
    slot = lax.axis_index("dp") % SLICES
    owner = lax.axis_index("mp")
    place = jnp.stack([slot, owner]).astype(jnp.int32)
    own_rows, seq, width = tokens.shape
    group_rows = segment_of_token.shape[0]
    patches, image_width = images.shape[1:]
    quarter = attention_in.shape[3]
    units = feed_in.shape[2]
    n_tokens = own_rows * seq
    inward = attention_in.transpose(0, 1, 3, 2)
    image = image_weight.T

    attention_rows = quarter // 4
    feed_rows = units // SLICES
    image_rows = quarter * image_width // width // SLICES // 2

    token_shape = shape((n_tokens, width))
    token_low = shape((n_tokens, width), BF16)
    row_low = shape((own_rows, seq, width), BF16)
    inner_shape = shape((n_tokens, mp * units))
    inner_low = shape((n_tokens, mp * units), BF16)
    padded = -(-patches // 16) * 16
    n_patches = own_rows * padded
    patch_low = shape((n_patches, width), BF16)
    small_shape = shape((8, width))
    attention_grad = shape((2, 4, mp, attention_rows, width), BF16)
    feed_grad = shape((2, 4, mp, feed_rows, width), BF16)
    image_grad = shape((2, 4, mp, image_rows, width), BF16)
    square = pltpu.VMEM((4, width, width), BF16)
    wide = pltpu.VMEM((2, mp, units, width), BF16)
    tall = pltpu.VMEM((width, image_width), BF16)
    token_f32 = pltpu.VMEM((n_tokens, width), F32)
    token_bf16 = pltpu.VMEM((n_tokens, width), BF16)
    dma = pltpu.SemaphoreType.DMA
    matmul = 2 * n_tokens * width * width
    patch_matmul = 2 * n_patches * width * width

    local_order = image_of_row % group_rows
    here = owner * own_rows + jnp.arange(own_rows, dtype=jnp.int32)
    chosen = (local_order[None, :] == here[:, None]).astype(jnp.int32)
    source_row = jnp.sum(chosen * jnp.arange(group_rows, dtype=jnp.int32)[None, :], axis=1)
    picks_in = ((owner - source_row // own_rows) % mp) * own_rows + source_row % own_rows
    mine = (jnp.arange(group_rows, dtype=jnp.int32)[None, :] == here[:, None]).astype(jnp.int32)
    image_row = jnp.sum(mine * local_order[None, :], axis=1)
    picks_out = ((owner - image_row // own_rows) % mp) * own_rows + image_row % own_rows
    segments = jnp.sum(chosen[:, :, None] * segment_of_token[None], axis=1)
    code = jnp.arange(own_rows, dtype=jnp.int32)[:, None] * seq + segments
    code_col = code.reshape(n_tokens, 1)
    code_row = code.reshape(own_rows // 2, 2 * seq)

    text, first, joining, cross, last = call(
        slice_kernel,
        [(place, SMEM)] + [(v, ANY) for v in (inward, attention_out, feed_in, feed_out, image)],
        [
            (shape((2, rows, width), BF16), ANY)
            for rows in (attention_rows, feed_rows, attention_rows, attention_rows + image_rows, feed_rows)
        ],
        [dma((5,))],
        16,
    )
    at = {}

    def step():
        done = lax.optimization_barrier(at)
        at.clear()
        at.update(done)

    flat = jnp.concatenate([query_value_bias.reshape(-1, quarter), feed_bias.reshape(-1, quarter), image_bias[None]])
    rings = {
        name: Ring(at, name, own)
        for name, own in (
            ("text", text), ("first", first), ("joining", joining), ("cross", cross), ("last", last),
            ("bias", flat), ("tokens", tokens), ("cotangent", cotangent),
        )
    }

    def gathered(name):
        parts = rings[name].take()[1:]
        return Widen(at, name, jnp.stack([part[0] for part in parts]), jnp.stack([part[1] for part in parts]))

    def both_ways(name):
        rings[name].up()
        rings[name].down()

    def far(name):
        rings[name].far()

    both_ways("text")
    both_ways("cross")
    both_ways("bias")
    step()
    far("text")
    far("cross")
    far("bias")
    both_ways("first")
    step()
    text_wide, cross_wide = gathered("text"), gathered("cross")
    bias_parts = rings["bias"].take()
    text_wide.one()
    cross_wide.one()
    far("first")
    both_ways("joining")
    step()
    first_wide = gathered("first")
    text_wide.two()
    cross_wide.two()
    first_wide.one()
    far("joining")
    rings["tokens"].up()
    both_ways("last")
    step()
    joining_wide = gathered("joining")
    text_wide.core()
    cross_wide.core()
    first_wide.two()
    joining_wide.one()
    rings["tokens"].down()
    far("last")
    step()

    ordered = jnp.stack(bias_parts)[(owner - jnp.arange(mp)) % mp].astype(F32)
    rows_of = units // quarter
    bias = jnp.concatenate(
        [
            ordered[:, :6].transpose(1, 0, 2).reshape(6, width),
            ordered[:, 6 : 6 + 2 * rows_of].reshape(mp, 2, units).transpose(1, 0, 2).reshape(2 * mp, width),
            ordered[:, 6 + 2 * rows_of].reshape(1, width),
        ]
    )
    params = jnp.stack([output_bias, norm_gain, norm_bias], axis=1).astype(F32).reshape(-1, width)

    attention_pieces = [text_wide.take(), None, cross_wide.take()]
    feed_pieces = [None, None]

    def attention_ins(layer):
        return [(inward, ANY), (attention_out, ANY)] + [(piece, ANY) for piece in attention_pieces[layer]]

    def feed_ins(layer):
        return [(feed_in, ANY), (feed_out, ANY)] + [(piece, ANY) for piece in feed_pieces[layer]]

    def self_forward(layer, norm, rows, pick):
        return call(
            partial(self_forward_kernel, pick, layer, norm, 0),
            [(place, SMEM), (picks_in, SMEM), (rows, VMEM)]
            + attention_ins(layer)
            + [(bias, VMEM), (params, VMEM), (code_col, VMEM), (code_row, VMEM)],
            [(token_shape, VMEM), (token_low, VMEM), (token_shape, VMEM)] + [(token_low, VMEM)] * 4,
            [square, dma((4,))] + ([token_f32] if pick else []),
            32,
        )

    def self_backward(layer, norm, grad, kept, leave, spot, rows, held):
        _, low, pre, query, keys, value, context = kept
        grads = shape((2, 4, mp, rows, width), BF16)
        n_before = 8 + 2 + 8 + 3
        return call(
            partial(self_backward_kernel, leave, layer, norm, 0, spot, len(held)),
            [(place, SMEM)]
            + [(v, VMEM) for v in (grad, low, pre, query, keys, value, context)]
            + attention_ins(layer)
            + [(params, VMEM), (code_col, VMEM), (code_row, VMEM)]
            + [(v, ANY) for v in held],
            [(row_low if leave else token_shape, VMEM), (small_shape, VMEM)] + [(grads, ANY)] * 2,
            [square, square] + [token_bf16] * 4 + [dma((4,)), dma],
            40,
            {n_before + i: 2 + i for i in range(len(held))},
        )

    def feed_forward(layer, norm, rows, leave):
        return call(
            partial(feed_forward_kernel, leave, layer, norm, 0),
            [(place, SMEM), (rows, VMEM)] + feed_ins(layer) + [(bias, VMEM), (params, VMEM)],
            [(row_low if leave else token_shape, VMEM), (token_low, VMEM), (token_shape, VMEM)]
            + [(inner_shape, VMEM), (inner_low, VMEM)],
            [wide, dma((2, mp))],
            40,
        )

    def feed_backward(layer, norm, grad, kept, pick):
        _, low, pre, slope, active = kept
        return call(
            partial(feed_backward_kernel, pick, layer, norm, 0),
            [(place, SMEM), (picks_in, SMEM)]
            + [(v, VMEM) for v in (grad, low, pre, slope, active)]
            + feed_ins(layer)
            + [(params, VMEM)],
            [(token_shape, VMEM), (small_shape, VMEM)] + [(feed_grad, ANY)] * 2,
            [wide, wide, dma((2, mp)), dma] + ([token_f32] if pick else []),
            48,
        )

    def pick_rows(parts):
        rows = jnp.stack(parts).reshape(mp * own_rows, seq, width)
        return call(
            pick_kernel, [(picks_out, SMEM), (rows, VMEM)], [(shape((own_rows, seq, width)), VMEM)], [], 16
        )[0]

    patch_rows = jnp.pad(images, ((0, 0), (0, padded - patches), (0, 0))).reshape(n_patches, image_width)
    joining_wide.two()
    first_wide.core()
    last_wide = gathered("last")
    last_wide.one()
    far("tokens")
    at["patches"] = call(
        partial(image_forward_kernel, 2, 0, attention_rows, image_rows),
        [(place, SMEM), (patch_rows, VMEM), (image, ANY)] + attention_ins(2) + [(bias, VMEM)],
        [(patch_low, VMEM)] * 3,
        [square, tall, dma((4,)), dma],
        40,
    )
    step()

    feed_pieces[0] = first_wide.take()
    joining_wide.core()
    last_wide.two()
    rings["cotangent"].up()
    rows_in = jnp.stack(rings["tokens"].take()).reshape(mp * own_rows, seq, width)
    text_attention = self_forward(0, 0, rows_in, True)
    text_feed = feed_forward(0, 1, text_attention[0], False)
    at["stream"] = text_feed[0]
    step()

    attention_pieces[1] = joining_wide.take()
    last_wide.core()
    rings["cotangent"].down()
    joining_attention = self_forward(1, 2, at.pop("stream"), False)
    at["stream"] = joining_attention[0]
    step()

    feed_pieces[1] = last_wide.take()
    far("cotangent")
    projected, image_keys, image_value = at.pop("patches")
    cross_attention = call(
        partial(cross_forward_kernel, 2, 3, 0, seq, patches),
        [(place, SMEM), (at.pop("stream"), VMEM), (image_keys, VMEM), (image_value, VMEM)]
        + attention_ins(2)
        + [(bias, VMEM), (params, VMEM)],
        [(token_shape, VMEM), (token_low, VMEM), (token_shape, VMEM), (token_shape, VMEM), (token_low, VMEM)],
        [square, token_f32, dma((4,))],
        32,
    )
    joining_feed = feed_forward(1, 4, cross_attention[0], True)
    mixed_ring = Ring(at, "mixed", joining_feed[0])
    step()

    rows_grad = jnp.stack(rings["cotangent"].take()).reshape(mp * own_rows, seq, width)
    grad, small_joining_feed, keep, send = feed_backward(1, 4, rows_grad, joining_feed, True)
    at["grad"] = grad
    last_grads = Reduce(at, "last", keep, send)
    step()

    last_grads.core()
    mixed_ring.up()
    middle_grad = shape((2, 4, mp, 2 * attention_rows, width), BF16)
    grad, small_cross, keep, send, grad_keys, grad_value = call(
        partial(cross_backward_kernel, 2, 3, 0, 0, seq, patches),
        [(place, SMEM), (at.pop("grad"), VMEM)]
        + [(cross_attention[i], VMEM) for i in (1, 2, 3, 4)]
        + [(image_keys, VMEM), (image_value, VMEM), (projected, VMEM)]
        + attention_ins(2)
        + [(params, VMEM)],
        [(token_shape, VMEM), (small_shape, VMEM)] + [(middle_grad, ANY)] * 2 + [(patch_low, VMEM)] * 2,
        [square, square, token_f32, token_f32, dma((4,)), dma],
        56,
    )
    at["grad"] = grad
    at["patch grads"] = grad_keys, grad_value
    step()

    last_grads.one()
    mixed_ring.down()
    grad, small_joining, keep, send = self_backward(
        1, 2, at.pop("grad"), joining_attention, False, attention_rows, 2 * attention_rows, (keep, send)
    )
    at["grad"] = grad
    middle_grads = Reduce(at, "middle", keep, send)
    step()

    last_grads.two()
    middle_grads.core()
    mixed_ring.far()
    grad, small_text_feed, keep, send = feed_backward(0, 1, at.pop("grad"), text_feed, False)
    at["grad"] = grad
    first_grads = Reduce(at, "first", keep, send)
    step()

    mixed_out = pick_rows(mixed_ring.take())
    last_grads.far()
    middle_grads.one()
    first_grads.core()
    rows_back, small_text, keep, send = self_backward(
        0, 0, at.pop("grad"), text_attention, True, 0, attention_rows + image_rows, ()
    )
    back_ring = Ring(at, "back", rows_back)
    step()

    last_grads.near()
    middle_grads.two()
    first_grads.one()
    back_ring.up()
    grad_keys, grad_value = at.pop("patch grads")
    grad_images, small_image, keep, send = call(
        partial(image_backward_kernel, 2, 0, attention_rows, image_rows, attention_rows, 2),
        [(place, SMEM), (patch_rows, VMEM), (grad_keys, VMEM), (grad_value, VMEM), (image, ANY)]
        + attention_ins(2)
        + [(keep, ANY), (send, ANY)],
        [(shape(images.shape), VMEM), (small_shape, VMEM)] + [(shape(keep.shape, BF16), ANY)] * 2,
        [square, tall, tall, pltpu.VMEM((n_patches, width), BF16), dma((4,)), dma, dma],
        48,
        {15: 2, 16: 3},
    )
    text_grads = Reduce(at, "text", keep, send)
    at["small"] = jnp.concatenate(
        [small_text, small_text_feed, small_joining, small_cross, small_joining_feed, small_image]
    )
    step()

    first_grads.two()
    text_grads.core()
    middle_grads.far()
    back_ring.down()
    last_result = last_grads.widen()
    step()

    text_grads.one()
    last_result.one()
    middle_grads.near()
    back_ring.far()
    step()

    grad_tokens = pick_rows(back_ring.take())
    text_grads.two()
    last_result.two()
    first_grads.far()
    middle_result = middle_grads.widen()
    middle_result.one()
    at["small"] = at["small"] + swap(at["small"], 1)
    step()

    last_result.core()
    middle_result.two()
    first_grads.near()
    text_grads.far()
    at["small"] = at["small"] + swap(at["small"], 2)
    step()

    middle_result.core()
    first_result = first_grads.widen()
    first_result.one()
    text_grads.near()
    at["small"] = at["small"] + swap(at["small"], 4)
    step()

    first_result.two()
    text_result = text_grads.widen()
    text_result.one()
    at["small"] = at["small"] + swap_owner(at["small"], 1)
    step()

    first_result.core()
    text_result.two()
    smalls = at["small"] + swap_owner(at["small"], 2)
    bit = SLICES
    while bit < lax.axis_size("dp"):
        smalls = smalls + swap(smalls, bit)
        bit *= 2
    at["small"] = smalls
    step()

    text_result.core()

    whole_shapes = {
        "attention_in": shape(inward.shape),
        "attention_out": shape(attention_out.shape),
        "feed_in": shape(feed_in.shape),
        "feed_out": shape(feed_out.shape),
        "image": shape(image.shape),
    }
    block_of = {"attention": (4, quarter, width), "feed": (2, units, width), "image": (quarter, image_width)}
    names_of = {"attention": ["attention_in", "attention_out"], "feed": ["feed_in", "feed_out"], "image": ["image"]}
    written = {}

    def write_out(result, *blocks):
        names = list(dict.fromkeys(name for kind, _, _ in blocks for name in names_of[kind]))
        names = [name for name in names if name in written] + [name for name in names if name not in written]
        held = [name for name in names if name in written]
        scratch = [pltpu.VMEM(block_of[kind], form) for kind, _, _ in blocks for form in (BF16, F32)]
        results = call(
            partial(finish_kernel, blocks, quarter, names, len(held)),
            [(place, SMEM)] + [(v, ANY) for v in result.take()] + [(written[name], ANY) for name in held],
            [(whole_shapes[name], ANY) for name in names],
            scratch + [dma((len(blocks),)), dma((len(blocks),))],
            40,
            {9 + i: i for i in range(len(held))},
        )
        written.update(zip(names, results))

    write_out(last_result, ("feed", 0, 1))
    write_out(middle_result, ("attention", 0, 2), ("attention", attention_rows, 1))
    write_out(first_result, ("feed", 0, 0))
    write_out(text_result, ("attention", 0, 0), ("image", attention_rows, 0))

    smalls = at["small"].reshape(6, 8, width)

    def own_part(values):
        return lax.dynamic_slice_in_dim(values, owner * quarter, quarter, axis=values.ndim - 1)

    grad_query_value_bias = own_part(jnp.stack([smalls[i, 3:5] for i in (0, 2, 3)]))
    grad_feed_bias = jnp.stack([smalls[i, 3 : 3 + mp].reshape(-1) for i in (1, 4)])
    grad_feed_bias = lax.dynamic_slice_in_dim(grad_feed_bias, owner * units, units, axis=1)
    return (
        mixed_out,
        grad_tokens,
        grad_images,
        written["attention_in"].transpose(0, 1, 3, 2),
        grad_query_value_bias,
        written["attention_out"],
        smalls[:5, 2],
        written["feed_in"],
        grad_feed_bias,
        written["feed_out"],
        written["image"].T,
        own_part(smalls[5, 0]),
        smalls[:5, 0],
        smalls[:5, 1],
    )


def solution(mesh):
    rows = P(("dp", "mp"), None, None)
    return jax.shard_map(
        on_device,
        mesh=mesh,
        in_specs=(
            rows,
            rows,
            P("dp", None),
            P("dp"),
            P(None, None, None, "mp"),
            P(None, None, "mp"),
            P(None, "mp", None),
            P(),
            P(None, None, "mp"),
            P(None, "mp"),
            P(None, "mp", None),
            P(None, "mp"),
            P("mp"),
            P(),
            P(),
            rows,
        ),
        out_specs=(
            rows,
            rows,
            rows,
            P(None, None, None, "mp"),
            P(None, None, "mp"),
            P(None, "mp", None),
            P(),
            P(None, None, "mp"),
            P(None, "mp"),
            P(None, "mp", None),
            P(None, "mp"),
            P("mp"),
            P(),
            P(),
        ),
        check_vma=False,
    )
```

time: 859 us -> 708 us (0.82)
  waiting for transfers between devices: 365 us -> 194 us
  starting transfers between devices: 71.9 us -> 144 us
  Pallas kernels: 235 us -> 213 us
  local copies, waits for them, and re-layouts: 103 us -> 83.6 us
  other arithmetic: 69.5 us -> 59.2 us
    ppermute x68 -> x95, waiting for transfers between devices: 189 us -> 83.4 us  [swap(): return lax.ppermute(values, 'dp', [(i, i ^ bit) for i in range(count)])]
    ppermute x43 -> x44, waiting for transfers between devices: 175 us -> 111 us  [the longest x42 105 us: pass_on(): lax.ppermute(values, 'mp', [(i, (i + way) % count) for i in range(count)])]
    ppermute x43 -> x44, starting transfers between devices: 16.4 us -> 71.1 us  [the longest x42 66.9 us: pass_on(): lax.ppermute(values, 'mp', [(i, (i + way) % count) for i in range(count)])]
    pallas_call x18 -> x19, Pallas kernels: 235 us -> 213 us  [call(): pl.pallas_call(kernel, in_specs=[spec for _, spec in ins], out_specs=[spe...]
    ppermute x68 -> x95, starting transfers between devices: 55.5 us -> 72.6 us  [swap(): return lax.ppermute(values, 'dp', [(i, i ^ bit) for i in range(count)])]
    convert_element_type x23 -> x22, other arithmetic: 21.3 us -> 35.2 us  [the longest x20 35.2 us: added(): return total.astype(BF16)]
    unnamed x299 -> x487, local copies, waits for them, and re-layouts: 61.6 us -> 75 us
    another operation x57 -> x45, other arithmetic: 30.9 us -> 18.2 us  [the longest x18 10.7 us: two(): near = (jnp.stack(both[:2]), jnp.stack(both[2:]))]
  transfers between devices with their start and end apart: 111 -> 139, of which waited for: 58 -> 43; matrix products, arithmetic and copies ran while one was open for 15% -> 9% of each run, Pallas kernels for 11% -> 26%
where the time goes in v2:
time: 708 us; the launch traced here: 698 us
  Pallas kernels  213 us (30%)
  waiting for transfers between devices  194 us (27%)
  starting transfers between devices  144 us (20%)
  local copies, waits for them, and re-layouts  83.6 us (12%)
  other arithmetic  59.2 us (8%)
    pallas_call x19, Pallas kernels, call(): pl.pallas_call(kernel, in_specs=[spec for _, spec in ins], out_specs=[spe...  213 us
    ppermute x42, waiting for transfers between devices, pass_on(): lax.ppermute(values, 'mp', [(i, (i + way) % count) for i in range(count)])  105 us
    ppermute x95, waiting for transfers between devices, swap(): return lax.ppermute(values, 'dp', [(i, i ^ bit) for i in range(count)])  83.4 us
    unnamed x487, local copies, waits for them, and re-layouts  75 us
    ppermute x95, starting transfers between devices, swap(): return lax.ppermute(values, 'dp', [(i, i ^ bit) for i in range(count)])  72.6 us
    ppermute x42, starting transfers between devices, pass_on(): lax.ppermute(values, 'mp', [(i, (i + way) % count) for i in range(count)])  66.9 us
    convert_element_type x20, other arithmetic, added(): return total.astype(BF16)  35.2 us
  transfers between devices with their start and end apart: 139, of which 43 were waited for; matrix products, arithmetic and copies ran while one was open for 9% of the time, Pallas kernels for 26%

profile of v2, /device:TPU:0, one launch (start us, length us, event | category | flops | bytes accessed | tf_op | source)
XLA Modules:
  0.0 698.2 jit_solution(4108117888837951174)
XLA Ops:
  19.3 11.7 %collective-permute-done = bf16[15,192]{1,0:T(8,128)(2,1)S(1)} collective-permute-done((bf16[15,192]{1,0:T(8,128)(2,1)S(1)}, bf16[15,192]{1,0:T(8,128)(2,1)S(1)}, u32[]{:S(2)}, u32[]{:S(2)}) %collective-permute-start) | collective-permute-done | bytes 5792 | tf_op jit(solution)/shard_map/ppermute | solution.py:33
  41.4 15.9 %collective-permute-done.6 = bf16[15,192]{1,0:T(8,128)(2,1)S(1)} collective-permute-done((bf16[15,192]{1,0:T(8,128)(2,1)S(1)}, bf16[15,192]{1,0:T(8,128)(2,1)S(1)}, u32[]{:S(2)}, u32[]{:S(2)}) %collective-permute-start.6) | collective-permute-done | bytes 5792 | tf_op jit(solution)/shard_map/ppermute | solution.py:33
  79.8 9.3 %collective-permute-done.24 = bf16[2,48,768]{2,1,0:T(8,128)(2,1)S(1)} collective-permute-done((bf16[2,48,768]{2,1,0:T(8,128)(2,1)S(1)}, bf16[2,48,768]{2,1,0:T(8,128)(2,1)S(1)}, u32[]{:S(2)}, u32[]{:S(2)}) %collective-permute-start.24) | collective-permute-done | bytes 147488 | tf_op jit(solution)/shard_map/ppermute | solution.py:33
  103.8 15.6 %collective-permute-done.31 = bf16[8,40,768]{2,1,0:T(8,128)(2,1)} collective-permute-done((bf16[8,40,768]{2,1,0:T(8,128)(2,1)}, bf16[8,40,768]{2,1,0:T(8,128)(2,1)}, u32[]{:S(2)}, u32[]{:S(2)}) %collective-permute-start.31) | collective-permute-done | bytes 491552 | tf_op jit(solution)/shard_map/ppermute | solution.py:33
  150.5 11.5 %collective-permute-done.34.refs_1_ = bf16[2,3,96,768]{3,2,1,0:T(8,128)(2,1)} collective-permute-done((bf16[2,3,96,768]{3,2,1,0:T(8,128)(2,1)}, bf16[2,3,96,768]{3,2,1,0:T(8,128)(2,1)}, u32[]{:S(2)}, u32[]{:S(2)}) %collective-permute-start.34) | collective-permute-done | bytes 884768 | tf_op jit(solution)/shard_map/ppermute | solution.py:28
  172.4 7.4 %collective-permute-done.46.refs_1_ = bf16[2,3,48,768]{3,2,1,0:T(8,128)(2,1)S(1)} collective-permute-done((bf16[2,3,48,768]{3,2,1,0:T(8,128)(2,1)S(1)}, bf16[2,3,48,768]{3,2,1,0:T(8,128)(2,1)S(1)}, u32[]{:S(2)}, u32[]{:S(2)}) %collective-permute-start.46) | collective-permute-done | bytes 442400 | tf_op jit(solution)/shard_map/ppermute | solution.py:28
  202.7 13.8 %shard_map.264 = (bf16[1280,768]{1,0:T(8,128)(2,1)S(1)}, bf16[1280,768]{1,0:T(8,128)(2,1)S(1)}, bf16[1280,768]{1,0:T(8,128)(2,1)S(1)}) custom-call(s32[2]{0:T(128)S(1)} %copy-done.172, bf16[1280,1024]{1,0:T(8,128)(2,1)S(1)} %bitcast.389, bf16[192,1024]{1,0:T(8,128)(2,1)S(1)} %bitcast.395, bf16[3,3,192,768]{3,2,1,0:T(8,128)(2,1)} %bitcast.380, ...), custom_call_target="tpu_custom_call" | custom-call | tf_op jit(solution)/shard_map/pallas_call | solution.py:615
  239.0 11.0 %shard_map.265 = (f32[320,768]{1,0:T(8,128)S(1)}, bf16[320,768]{1,0:T(8,128)(2,1)S(1)}, f32[320,768]{1,0:T(8,128)S(1)}, bf16[320,768]{1,0:T(8,128)(2,1)S(1)}, bf...) custom-call(s32[2]{0:T(128)S(1)} %copy-done.173, s32[8]{0:T(128)S(1)} %fusion.84.picks, ...), custom_call_target="tpu_custom_call" | custom-call | tf_op jit(solution)/shard_map/pallas_call | solution.py:615
  254.1 9.6 %shard_map.266 = (f32[320,768]{1,0:T(8,128)S(1)}, bf16[320,768]{1,0:T(8,128)(2,1)S(1)}, f32[320,768]{1,0:T(8,128)S(1)}, f32[320,3072]{1,0:T(8,128)}, bf16[320,3072]{1,0:T(8,128)(2,1)S(1)}) custom-call(s32[2]{0:T(128)S(1)} %copy-done.173, f32[320,768]{1,0:T(8,128)S(1)} %get-tuple-element.648.rows_ref, bf16[2,768,768]{2,1,0:T(8,128)(2,1)} %first_weight.7, ...), custom_call_target="tpu_custom_call" | custom-call | tf_op jit(solution)/shard_map/pallas_call | solution.py:615
  273.3 10.4 %shard_map.267 = (f32[320,768]{1,0:T(8,128)S(1)}, bf16[320,768]{1,0:T(8,128)(2,1)S(1)}, f32[320,768]{1,0:T(8,128)S(1)}, bf16[320,768]{1,0:T(8,128)(2,1)S(1)}, bf...) custom-call(s32[2]{0:T(128)S(1)} %copy-done.173, s32[8]{0:T(128)S(1)} %fusion.84.picks, ...), custom_call_target="tpu_custom_call" | custom-call | tf_op jit(solution)/shard_map/pallas_call | solution.py:615
  289.8 9.1 %shard_map.268 = (f32[320,768]{1,0:T(8,128)S(1)}, bf16[320,768]{1,0:T(8,128)(2,1)S(1)}, f32[320,768]{1,0:T(8,128)S(1)}, f32[320,768]{1,0:T(8,128)S(1)}, bf16[320,768]{1,0:T(8,128)(2,1)S(1)}) custom-call(s32[2]{0:T(128)S(1)} %copy-done.173, f32[320,768]{1,0:T(8,128)S(1)} %get-tuple-element.682.rows_ref, bf16[1280,768]{1,0:T(8,128)(2,1)S(1)} %copy-done.43, ...), custom_call_target="tpu_custom_call" | custom-call | tf_op jit(solution)/shard_map/pallas_call | solution.py:615
  303.0 12.9 %shard_map.269 = (bf16[8,40,768]{2,1,0:T(8,128)(2,1)S(1)}, bf16[320,768]{1,0:T(8,128)(2,1)S(1)}, f32[320,768]{1,0:T(8,128)S(1)}, f32[320,3072]{1,0:T(8,128)}, bf16[320,3072]{1,0:T(8,128)(2,1)S(1)}) custom-call(s32[2]{0:T(128)S(1)} %copy-done.173, f32[320,768]{1,0:T(8,128)S(1)} %get-tuple-element.685.rows_ref, bf16[2,768,768]{2,1,0:T(8,128)(2,1)S(1)} %copy-done.7, ...), custom_call_target="tpu_custom_call" | custom-call | tf_op jit(solution)/shard_map/pallas_call | solution.py:615
  318.2 24.4 %shard_map.270 = (f32[320,768]{1,0:T(8,128)}, f32[8,768]{1,0:T(8,128)S(1)}, bf16[2,4,4,96,768]{4,3,2,1,0:T(8,128)(2,1)}, bf16[2,4,4,96,768]{4,3,2,1,0:T(8,128)(2,1)}) custom-call(s32[2]{0:T(128)S(1)} %copy-done.173, s32[8]{0:T(128)S(1)} %fusion.84.picks, bf16[32,40,768]{2,1,0:T(8,128)(2,1)} %bitcast.401, bf16[320,768]{1,0:T(8,128)(2,1)S(1)} %get-tuple-element.699.low, ...), custom_call_target="tpu_custom_call" | custom-call | tf_op jit(solution)/shard_map/pallas_call | solution.py:615
  344.6 21.0 %shard_map.271 = (f32[320,768]{1,0:T(8,128)}, f32[8,768]{1,0:T(8,128)}, bf16[2,4,4,96,768]{4,3,2,1,0:T(8,128)(2,1)}, bf16[2,4,4,96,768]{4,3,2,1,0:T(8,128)(2,1)}...) custom-call(s32[2]{0:T(128)} %copy-done.171, f32[320,768]{1,0:T(8,128)} %get-tuple-element.707.grad, ...), custom_call_target="tpu_custom_call" | custom-call | tf_op jit(solution)/shard_map/pallas_call | solution.py:615
  376.4 16.1 %shard_map.272 = (f32[320,768]{1,0:T(8,128)S(1)}, f32[8,768]{1,0:T(8,128)S(1)}, bf16[2,4,4,96,768]{4,3,2,1,0:T(8,128)(2,1)}, bf16[2,4,4,96,768]{4,3,2,1,0:T(8,128)(2,1)}) custom-call(s32[2]{0:T(128)S(1)} %copy-done.174, f32[320,768]{1,0:T(8,128)S(1)} %copy-done.115, ...), custom_call_target="tpu_custom_call", output_to_operand_aliasing={{2}: (21, {}), {3}: (22, {})} | custom-call | tf_op jit(solution)/shard_map/pallas_call | solution.py:615
  405.8 20.2 %shard_map.273 = (f32[320,768]{1,0:T(8,128)}, f32[8,768]{1,0:T(8,128)S(1)}, bf16[2,4,4,96,768]{4,3,2,1,0:T(8,128)(2,1)}, bf16[2,4,4,96,768]{4,3,2,1,0:T(8,128)(2,1)}) custom-call(s32[2]{0:T(128)S(1)} %copy-done.174, s32[8]{0:T(128)S(1)} %copy-done.176, f32[320,768]{1,0:T(8,128)} %copy-done.112, bf16[320,768]{1,0:T(8,128)(2,1)S(1)} %copy-done.132, ...), custom_call_target="tpu_custom_call" | custom-call | tf_op jit(solution)/shard_map/pallas_call | solution.py:615
  437.8 15.9 %shard_map.275 = (bf16[8,40,768]{2,1,0:T(8,128)(2,1)S(1)}, f32[8,768]{1,0:T(8,128)S(1)}, bf16[2,4,4,64,768]{4,3,2,1,0:T(8,128)(2,1)}, bf16[2,4,4,64,768]{4,3,2,1,0:T(8,128)(2,1)}) custom-call(s32[2]{0:T(128)S(1)} %copy-done.174, f32[320,768]{1,0:T(8,128)S(1)} %copy-done.111, bf16[320,768]{1,0:T(8,128)(2,1)S(1)} %copy-done.122, f32[320,768]{1,0:T(8,128)S(1)} %copy-done.107, ...), custom_call_target="tpu_custom_call" | custom-call | tf_op jit(solution)/shard_map/pallas_call | solution.py:615
  486.9 21.0 %shard_map.276 = (f32[8,145,1024]{2,1,0:T(8,128)}, f32[8,768]{1,0:T(8,128)S(1)}, bf16[2,4,4,64,768]{4,3,2,1,0:T(8,128)(2,1)}, bf16[2,4,4,64,768]{4,3,2,1,0:T(8,128)(2,1)}) custom-call(s32[2]{0:T(128)S(1)} %copy-done.174, bf16[1280,1024]{1,0:T(8,128)(2,1)} %bitcast.390, ...), custom_call_target="tpu_custom_call", output_to_operand_aliasing={{2}: (15, {}), {3}: (16, {})} | custom-call | tf_op jit(solution)/shard_map/pallas_call | solution.py:615
  518.8 9.7 %collective-permute-done.87 = bf16[2,96,768]{2,1,0:T(8,128)(2,1)S(1)} collective-permute-done((bf16[2,96,768]{2,1,0:T(8,128)(2,1)S(1)}, bf16[2,96,768]{2,1,0:T(8,128)(2,1)S(1)}, u32[]{:S(2)}, u32[]{:S(2)}) %collective-permute-start.87) | collective-permute-done | bytes 294944 | tf_op jit(solution)/shard_map/ppermute | solution.py:33
  540.4 11.3 %collective-permute-done.92 = bf16[2,96,768]{2,1,0:T(8,128)(2,1)S(1)} collective-permute-done((bf16[2,96,768]{2,1,0:T(8,128)(2,1)S(1)}, bf16[2,96,768]{2,1,0:T(8,128)(2,1)S(1)}, u32[]{:S(2)}, u32[]{:S(2)}) %collective-permute-start.92) | collective-permute-done | bytes 294944 | tf_op jit(solution)/shard_map/ppermute | solution.py:33
  572.1 9.5 %collective-permute-done.98.refs_3_ = bf16[2,96,768]{2,1,0:T(8,128)(2,1)S(1)} collective-permute-done((bf16[2,96,768]{2,1,0:T(8,128)(2,1)S(1)}, bf16[2,96,768]{2,1,0:T(8,128)(2,1)S(1)}, u32[]{:S(2)}, u32[]{:S(2)}) %collective-permute-start.98) | collective-permute-done | bytes 294944 | tf_op jit(solution)/shard_map/ppermute | solution.py:28
  594.6 8.4 %collective-permute-done.115 = bf16[2,64,768]{2,1,0:T(8,128)(2,1)S(1)} collective-permute-done((bf16[2,64,768]{2,1,0:T(8,128)(2,1)S(1)}, bf16[2,64,768]{2,1,0:T(8,128)(2,1)S(1)}, u32[]{:S(2)}, u32[]{:S(2)}) %collective-permute-start.115) | collective-permute-done | bytes 196640 | tf_op jit(solution)/shard_map/ppermute | solution.py:33
  605.3 7.2 %collective-permute-done.111.refs_3_ = bf16[2,96,768]{2,1,0:T(8,128)(2,1)S(1)} collective-permute-done((bf16[2,96,768]{2,1,0:T(8,128)(2,1)S(1)}, bf16[2,96,768]{2,1,0:T(8,128)(2,1)S(1)}, u32[]{:S(2)}, u32[]{:S(2)}) %collective-permute-start.111) | collective-permute-done | bytes 294944 | tf_op jit(solution)/shard_map/ppermute | solution.py:28
  659.9 7.5 %copy.67 = f32[8,145,1024]{2,0,1:T(8,128)} copy(f32[8,145,1024]{2,1,0:T(8,128)} %get-tuple-element.1058) | data formatting | bytes 9502720
  (890 shorter events, 383.7 us)
Async XLA Ops:
  10.1 24.5 %collective-permute-start.2 = (bf16[2,64,768]{2,1,0:T(8,128)(2,1)S(1)}, bf16[2,64,768]{2,1,0:T(8,128)(2,1)S(1)}, u32[]{:S(2)}, u32[]{:S(2)}) collective-permute-start(bf16[2,64,768]{2,1,0:T(8,128)(2,1)S(1)} %get-tuple-element.521), channel_id=1, source_target_pairs={{0,1},{1,2},{2,3},{3,0},{4,5},{5,6},{6,7},{7,4},{8,9},{9,10},{10,1... | collective-permute-start | bytes 589832 | tf_op jit(solution)/shard_map/ppermute | solution.py:33
  93.9 25.5 %collective-permute-start.18 = (bf16[2,3,64,768]{3,2,1,0:T(8,128)(2,1)S(1)}, bf16[2,3,64,768]{3,2,1,0:T(8,128)(2,1)S(1)}, u32[]{:S(2)}, u32[]{:S(2)}) collective-permute-start(bf16[2,3,64,768]{3,2,1,0:T(8,128)(2,1)S(1)} %pad_maximum_fusion.8.refs_0_), channel_id=1, source_target_pairs={{0,16},{4,20},{8,24},{12,28},{16,0},{20,4},{24,8},{28,12},{1,17},{... | collective-permute-start | bytes 1769480 | tf_op jit(solution)/shard_map/ppermute | solution.py:28
  171.1 48.0 %collective-permute-start.44 = (bf16[2,3,96,768]{3,2,1,0:T(8,128)(2,1)}, bf16[2,3,96,768]{3,2,1,0:T(8,128)(2,1)}, u32[]{:S(2)}, u32[]{:S(2)}) collective-permute-start(bf16[2,3,96,768]{3,2,1,0:T(8,128)(2,1)} %collective-permute-done.34.refs_1_), channel_id=1, source_target_pairs={{0,4},{4,0},{8,12},{12,8},{16,20},{20,16},{24,28},{28,24},{1,5},{5... | collective-permute-start | bytes 2654216 | tf_op jit(solution)/shard_map/ppermute | solution.py:28
  179.8 39.3 %collective-permute-start.45 = (bf16[2,3,96,768]{3,2,1,0:T(8,128)(2,1)}, bf16[2,3,96,768]{3,2,1,0:T(8,128)(2,1)}, u32[]{:S(2)}, u32[]{:S(2)}) collective-permute-start(bf16[2,3,96,768]{3,2,1,0:T(8,128)(2,1)} %collective-permute-done.35.refs_3_), channel_id=1, source_target_pairs={{0,4},{4,0},{8,12},{12,8},{16,20},{20,16},{24,28},{28,24},{1,5},{5... | collective-permute-start | bytes 2654216 | tf_op jit(solution)/shard_map/ppermute | solution.py:28
  181.9 37.2 %collective-permute-start.52 = (bf16[8,40,768]{2,1,0:T(8,128)(2,1)}, bf16[8,40,768]{2,1,0:T(8,128)(2,1)}, u32[]{:S(2)}, u32[]{:S(2)}) collective-permute-start(bf16[8,40,768]{2,1,0:T(8,128)(2,1)} %collective-permute-done.31), channel_id=1, source_target_pairs={{0,1},{1,2},{2,3},{3,0},{4,5},{5,6},{6,7},{7,4},{8,9},{9,10},{10,1... | collective-permute-start | bytes 1474568 | tf_op jit(solution)/shard_map/ppermute | solution.py:33
  185.7 33.4 %collective-permute-start.50 = (bf16[3,96,768]{2,1,0:T(8,128)(2,1)}, bf16[3,96,768]{2,1,0:T(8,128)(2,1)}, u32[]{:S(2)}, u32[]{:S(2)}) collective-permute-start(bf16[3,96,768]{2,1,0:T(8,128)(2,1)} %pad_maximum_fusion.16), channel_id=1, source_target_pairs={{0,8},{4,12},{8,0},{12,4},{16,24},{20,28},{24,16},{28,20},{1,9},{5... | collective-permute-start | bytes 1327112 | tf_op jit(solution)/shard_map/ppermute | solution.py:28
  188.2 30.9 %collective-permute-start.51 = (bf16[3,96,768]{2,1,0:T(8,128)(2,1)}, bf16[3,96,768]{2,1,0:T(8,128)(2,1)}, u32[]{:S(2)}, u32[]{:S(2)}) collective-permute-start(bf16[3,96,768]{2,1,0:T(8,128)(2,1)} %pad_maximum_fusion.17), channel_id=1, source_target_pairs={{0,16},{4,20},{8,24},{12,28},{16,0},{20,4},{24,8},{28,12},{1,17},{... | collective-permute-start | bytes 1327112 | tf_op jit(solution)/shard_map/ppermute | solution.py:28
  221.2 45.5 %collective-permute-start.56 = (bf16[2,3,96,768]{3,2,1,0:T(8,128)(2,1)S(1)}, bf16[2,3,96,768]{3,2,1,0:T(8,128)(2,1)}, u32[]{:S(2)}, u32[]{:S(2)}) collective-permute-start(bf16[2,3,96,768]{3,2,1,0:T(8,128)(2,1)S(1)} %pad_maximum_fusion.6.refs_0_), channel_id=1, source_target_pairs={{0,16},{4,20},{8,24},{12,28},{16,0},{20,4},{24,8},{28,12},{1,17},{... | collective-permute-start | bytes 2654216 | tf_op jit(solution)/shard_map/ppermute | solution.py:28
  223.0 43.8 %collective-permute-start.58 = (bf16[2,3,96,768]{3,2,1,0:T(8,128)(2,1)S(1)}, bf16[2,3,96,768]{3,2,1,0:T(8,128)(2,1)}, u32[]{:S(2)}, u32[]{:S(2)}) collective-permute-start(bf16[2,3,96,768]{3,2,1,0:T(8,128)(2,1)S(1)} %pad_maximum_fusion.6.refs_0_), channel_id=1, source_target_pairs={{0,4},{4,0},{8,12},{12,8},{16,20},{20,16},{24,28},{28,24},{1,5},{5... | collective-permute-start | bytes 2654216 | tf_op jit(solution)/shard_map/ppermute | solution.py:28
  224.2 42.5 %collective-permute-start.57 = (bf16[2,3,96,768]{3,2,1,0:T(8,128)(2,1)S(1)}, bf16[2,3,96,768]{3,2,1,0:T(8,128)(2,1)}, u32[]{:S(2)}, u32[]{:S(2)}) collective-permute-start(bf16[2,3,96,768]{3,2,1,0:T(8,128)(2,1)S(1)} %pad_maximum_fusion.7.refs_2_), channel_id=1, source_target_pairs={{0,8},{4,12},{8,0},{12,4},{16,24},{20,28},{24,16},{28,20},{1,9},{5... | collective-permute-start | bytes 2654216 | tf_op jit(solution)/shard_map/ppermute | solution.py:28
  224.6 42.2 %collective-permute-start.59 = (bf16[2,3,96,768]{3,2,1,0:T(8,128)(2,1)S(1)}, bf16[2,3,96,768]{3,2,1,0:T(8,128)(2,1)}, u32[]{:S(2)}, u32[]{:S(2)}) collective-permute-start(bf16[2,3,96,768]{3,2,1,0:T(8,128)(2,1)S(1)} %pad_maximum_fusion.7.refs_2_), channel_id=1, source_target_pairs={{0,4},{4,0},{8,12},{12,8},{16,20},{20,16},{24,28},{28,24},{1,5},{5... | collective-permute-start | bytes 2654216 | tf_op jit(solution)/shard_map/ppermute | solution.py:28
  227.8 38.9 %collective-permute-start.53 = (bf16[8,40,768]{2,1,0:T(8,128)(2,1)}, bf16[8,40,768]{2,1,0:T(8,128)(2,1)S(1)}, u32[]{:S(2)}, u32[]{:S(2)}) collective-permute-start(bf16[8,40,768]{2,1,0:T(8,128)(2,1)} %param.31), channel_id=1, source_target_pairs={{0,1},{1,2},{2,3},{3,0},{4,5},{5,6},{6,7},{7,4},{8,9},{9,10},{10,1... | collective-permute-start | bytes 1474568 | tf_op jit(solution)/shard_map/ppermute | solution.py:33
  289.7 26.4 %collective-permute-start.63 = (bf16[8,40,768]{2,1,0:T(8,128)(2,1)}, bf16[8,40,768]{2,1,0:T(8,128)(2,1)S(1)}, u32[]{:S(2)}, u32[]{:S(2)}) collective-permute-start(bf16[8,40,768]{2,1,0:T(8,128)(2,1)} %copy-done.201), channel_id=1, source_target_pairs={{0,1},{1,2},{2,3},{3,0},{4,5},{5,6},{6,7},{7,4},{8,9},{9,10},{10,1... | collective-permute-start | bytes 1474568 | tf_op jit(solution)/shard_map/ppermute | solution.py:33
  368.9 28.1 %collective-permute-start.66 = (bf16[2,4,96,768]{3,2,1,0:T(8,128)(2,1)S(1)}, bf16[2,4,96,768]{3,2,1,0:T(8,128)(2,1)S(1)}, u32[]{:S(2)}, u32[]{:S(2)}) collective-permute-start(bf16[2,4,96,768]{3,2,1,0:T(8,128)(2,1)S(1)} %get-tuple-element.1113), channel_id=1, source_target_pairs={{0,16},{4,20},{8,24},{12,28},{16,0},{20,4},{24,8},{28,12},{1,17},{... | collective-permute-start | bytes 3538952 | tf_op jit(solution)/shard_map/ppermute | solution.py:28
  370.1 27.9 %collective-permute-start.67 = (bf16[2,4,96,768]{3,2,1,0:T(8,128)(2,1)S(1)}, bf16[2,4,96,768]{3,2,1,0:T(8,128)(2,1)S(1)}, u32[]{:S(2)}, u32[]{:S(2)}) collective-permute-start(bf16[2,4,96,768]{3,2,1,0:T(8,128)(2,1)S(1)} %get-tuple-element.1112), channel_id=1, source_target_pairs={{0,8},{4,12},{8,0},{12,4},{16,24},{20,28},{24,16},{28,20},{1,9},{5... | collective-permute-start | bytes 3538952 | tf_op jit(solution)/shard_map/ppermute | solution.py:28
  398.0 28.2 %collective-permute-start.71 = (bf16[2,4,4,96,768]{4,3,2,1,0:T(8,128)(2,1)}, bf16[2,4,4,96,768]{4,3,2,1,0:T(8,128)(2,1)}, u32[]{:S(2)}, u32[]{:S(2)}) collective-permute-start(bf16[2,4,4,96,768]{4,3,2,1,0:T(8,128)(2,1)} %get-tuple-element.749), channel_id=1, source_target_pairs={{0,4},{4,0},{8,12},{12,8},{16,20},{20,16},{24,28},{28,24},{1,5},{5... | collective-permute-start | bytes 14155784 | tf_op jit(solution)/shard_map/ppermute | solution.py:28
  426.1 31.6 %collective-permute-start.73 = (bf16[2,4,4,96,768]{4,3,2,1,0:T(8,128)(2,1)}, bf16[2,4,4,96,768]{4,3,2,1,0:T(8,128)(2,1)}, u32[]{:S(2)}, u32[]{:S(2)}) collective-permute-start(bf16[2,4,4,96,768]{4,3,2,1,0:T(8,128)(2,1)} %get-tuple-element.768), channel_id=1, source_target_pairs={{0,4},{4,0},{8,12},{12,8},{16,20},{20,16},{24,28},{28,24},{1,5},{5... | collective-permute-start | bytes 14155784 | tf_op jit(solution)/shard_map/ppermute | solution.py:28
  429.3 28.1 %collective-permute-start.75 = (bf16[2,4,96,768]{3,2,1,0:T(8,128)(2,1)S(1)}, bf16[2,4,96,768]{3,2,1,0:T(8,128)(2,1)S(1)}, u32[]{:S(2)}, u32[]{:S(2)}) collective-permute-start(bf16[2,4,96,768]{3,2,1,0:T(8,128)(2,1)S(1)} %get-tuple-element.1107), channel_id=1, source_target_pairs={{0,16},{4,20},{8,24},{12,28},{16,0},{20,4},{24,8},{28,12},{1,17},{... | collective-permute-start | bytes 3538952 | tf_op jit(solution)/shard_map/ppermute | solution.py:28
  430.0 27.7 %collective-permute-start.76 = (bf16[2,4,96,768]{3,2,1,0:T(8,128)(2,1)S(1)}, bf16[2,4,96,768]{3,2,1,0:T(8,128)(2,1)S(1)}, u32[]{:S(2)}, u32[]{:S(2)}) collective-permute-start(bf16[2,4,96,768]{3,2,1,0:T(8,128)(2,1)S(1)} %get-tuple-element.1106), channel_id=1, source_target_pairs={{0,8},{4,12},{8,0},{12,4},{16,24},{20,28},{24,16},{28,20},{1,9},{5... | collective-permute-start | bytes 3538952 | tf_op jit(solution)/shard_map/ppermute | solution.py:28
  462.7 45.3 %collective-permute-start.78 = (bf16[2,4,96,768]{3,2,1,0:T(8,128)(2,1)}, bf16[2,4,96,768]{3,2,1,0:T(8,128)(2,1)S(1)}, u32[]{:S(2)}, u32[]{:S(2)}) collective-permute-start(bf16[2,4,96,768]{3,2,1,0:T(8,128)(2,1)} %get-tuple-element.1105), channel_id=1, source_target_pairs={{0,16},{4,20},{8,24},{12,28},{16,0},{20,4},{24,8},{28,12},{1,17},{... | collective-permute-start | bytes 3538952 | tf_op jit(solution)/shard_map/ppermute | solution.py:28
  464.0 44.0 %collective-permute-start.79 = (bf16[2,4,96,768]{3,2,1,0:T(8,128)(2,1)}, bf16[2,4,96,768]{3,2,1,0:T(8,128)(2,1)S(1)}, u32[]{:S(2)}, u32[]{:S(2)}) collective-permute-start(bf16[2,4,96,768]{3,2,1,0:T(8,128)(2,1)} %get-tuple-element.1104), channel_id=1, source_target_pairs={{0,8},{4,12},{8,0},{12,4},{16,24},{20,28},{24,16},{28,20},{1,9},{5... | collective-permute-start | bytes 3538952 | tf_op jit(solution)/shard_map/ppermute | solution.py:28
  475.0 32.9 %collective-permute-start.82 = (bf16[4,96,768]{2,1,0:T(8,128)(2,1)}, bf16[4,96,768]{2,1,0:T(8,128)(2,1)}, u32[]{:S(2)}, u32[]{:S(2)}) collective-permute-start(bf16[4,96,768]{2,1,0:T(8,128)(2,1)} %get-tuple-element.1103), channel_id=1, source_target_pairs={{0,8},{4,12},{8,0},{12,4},{16,24},{20,28},{24,16},{28,20},{1,9},{5... | collective-permute-start | bytes 1769480 | tf_op jit(solution)/shard_map/ppermute | solution.py:28
  479.2 28.7 %collective-permute-start.83 = (bf16[4,96,768]{2,1,0:T(8,128)(2,1)}, bf16[4,96,768]{2,1,0:T(8,128)(2,1)}, u32[]{:S(2)}, u32[]{:S(2)}) collective-permute-start(bf16[4,96,768]{2,1,0:T(8,128)(2,1)} %get-tuple-element.1102), channel_id=1, source_target_pairs={{0,16},{4,20},{8,24},{12,28},{16,0},{20,4},{24,8},{28,12},{1,17},{... | collective-permute-start | bytes 1769480 | tf_op jit(solution)/shard_map/ppermute | solution.py:28
  529.3 27.0 %collective-permute-start.89 = (bf16[8,40,768]{2,1,0:T(8,128)(2,1)S(1)}, bf16[8,40,768]{2,1,0:T(8,128)(2,1)S(1)}, u32[]{:S(2)}, u32[]{:S(2)}) collective-permute-start(bf16[8,40,768]{2,1,0:T(8,128)(2,1)S(1)} %copy-done.195), channel_id=1, source_target_pairs={{0,1},{1,2},{2,3},{3,0},{4,5},{5,6},{6,7},{7,4},{8,9},{9,10},{10,1... | collective-permute-start | bytes 1474568 | tf_op jit(solution)/shard_map/ppermute | solution.py:33
  (352 other events, 4113.8 us)

commit v3 on v2

v3 whole, which is shorter than its diff:
```python
from functools import partial

import jax
import jax.numpy as jnp
from jax import lax
from jax.experimental import pallas as pl
from jax.experimental.pallas import tpu as pltpu
from jax.sharding import PartitionSpec as P

HEAD_DIM = 64
STACK = 4 * HEAD_DIM
TOGETHER = 6
SLICES = 8
EPSILON = 1e-06
BLOCKED = -1000000000.0
SCALE = HEAD_DIM ** (-0.5)
DISTANCES = ((0, 2, 4, 6), (0, 4, 2, 6))
ATTENTION, FEED, IMAGE, ATTENTION_IN, ATTENTION_OUT, FEED_IN, FEED_OUT = range(7)
SMALL, TOKENS, COTANGENT = "small", "tokens", "cotangent"
F32 = jnp.float32
BF16 = jnp.bfloat16

ANY = pl.BlockSpec(memory_space=pl.ANY)
VMEM = pl.BlockSpec(memory_space=pltpu.VMEM)
SMEM = pl.BlockSpec(memory_space=pltpu.SMEM)


def swap(values, bit):
    count = lax.axis_size("dp")
    return lax.ppermute(values, "dp", [(i, i ^ bit) for i in range(count)])


def pass_on(values, way=1):
    count = lax.axis_size("mp")
    return lax.ppermute(values, "mp", [(i, (i + way) % count) for i in range(count)])


def swap_owner(values, bit):
    count = lax.axis_size("mp")
    return lax.ppermute(values, "mp", [(i, i ^ bit) for i in range(count)])


def added(*terms):
    total = terms[0].astype(F32)
    for term in terms[1:]:
        total = total + term
    return total.astype(BF16)


def dot_nn(left, right):
    return lax.dot_general(left, right, (((1,), (0,)), ((), ())), preferred_element_type=F32)


def dot_nt(left, right):
    return lax.dot_general(left, right, (((1,), (1,)), ((), ())), preferred_element_type=F32)


def dot_tn(left, right):
    return lax.dot_general(left, right, (((0,), (0,)), ((), ())), preferred_element_type=F32)


def start(source, target, sem):
    pltpu.make_async_copy(source, target, sem).start()


def finish(whole, sem):
    pltpu.make_async_copy(whole, whole, sem).wait()


def aligned(first, count, step=16):
    return pl.ds(pl.multiple_of(first, step), count)


def each_slice(place, first_step, mp):
    for core in range(2):
        for half in range(2):
            for entry in range(4):
                slot = place[0] ^ (core ^ DISTANCES[half][entry])
                for step in range(first_step, mp):
                    yield core, half, entry, step, slot, (place[1] + mp - step) % mp


def piece_of(pieces, core, half, entry):
    if len(pieces) == 2:
        return pieces[core].at[half, entry]
    return pieces[2 * core + entry // 2].at[half, entry % 2]


def attention_spot(whole, quarter, half, slot, owner):
    span = 4 * quarter // SLICES
    count = quarter // span
    row = owner * quarter + (slot % count) * span + half * (span // 2)
    return whole.at[slot // count, aligned(row, span // 2)]


def load_attention(place, own, pieces, offset, layer, whole, sems):
    mp = pieces[0].shape[2] + 1
    quarter = whole.shape[1] // mp
    rows = quarter // 4
    for mat in range(4):
        source = own[0].at[layer, mat] if mat < 3 else own[1].at[layer]
        start(source, whole.at[mat, aligned(place[1] * quarter, quarter)], sems.at[mat])
    for core, half, entry, step, slot, owner in each_slice(place, 1, mp):
        start(
            piece_of(pieces, core, half, entry).at[step - 1, pl.ds(offset, rows)],
            attention_spot(whole, quarter, half, slot, owner),
            sems.at[slot // 2],
        )


def store_attention(place, whole, outs, offset, sem):
    mp = outs[0].shape[2]
    quarter = whole.shape[1] // mp
    for core, half, entry, step, slot, owner in each_slice(place, 0, mp):
        start(
            attention_spot(whole, quarter, half, slot, owner),
            outs[core].at[half, entry, step, pl.ds(offset, quarter // 4)],
            sem,
        )


def feed_spot(whole, half, slot, step):
    span = whole.shape[2] // SLICES
    return whole.at[half, step, aligned(slot * span, span)]


def load_feed(place, own, pieces, offset, layer, half, step, whole, sems):
    rows = whole.shape[2] // SLICES
    if step == 0:
        start(own[half].at[layer], whole.at[half, 0], sems.at[half, 0])
        return
    for core in range(2):
        for entry in range(4):
            slot = place[0] ^ (core ^ DISTANCES[half][entry])
            start(
                piece_of(pieces, core, half, entry).at[step - 1, pl.ds(offset, rows)],
                feed_spot(whole, half, slot, step),
                sems.at[half, step],
            )


def store_feed(place, whole, outs, half, step, sem):
    for core in range(2):
        for entry in range(4):
            slot = place[0] ^ (core ^ DISTANCES[half][entry])
            start(feed_spot(whole, half, slot, step), outs[core].at[half, entry, step], sem)


def image_copies(whole, piece, quarter, half, slot, owner, sem, inward):
    rows, width = piece.shape
    span = 2 * rows
    beyond = whole.shape[1] - width
    blocks = width // beyond
    plain = quarter // span
    base = owner * quarter + half * rows

    def move(inner, outer):
        start(inner, outer, sem) if inward else start(outer, inner, sem)

    @pl.when(slot < plain)
    def _():
        move(piece, whole.at[aligned(base + slot * span, rows), pl.ds(0, width)])

    @pl.when(slot >= plain)
    def _():
        for block in range(blocks):
            row = base + block * (quarter // blocks) + (slot - plain) * span
            move(
                piece.at[:, pl.ds(block * beyond, beyond)],
                whole.at[aligned(row, rows), pl.ds(width, beyond)],
            )


def load_image(place, own, pieces, offset, rows, whole, sem):
    mp = pieces[0].shape[2] + 1
    quarter = whole.shape[0] // mp
    start(own, whole.at[aligned(place[1] * quarter, quarter)], sem)
    for core, half, entry, step, slot, owner in each_slice(place, 1, mp):
        piece = piece_of(pieces, core, half, entry).at[step - 1, pl.ds(offset, rows)]
        image_copies(whole, piece, quarter, half, slot, owner, sem, True)


def store_image(place, whole, outs, offset, rows, sem):
    mp = outs[0].shape[2]
    quarter = whole.shape[0] // mp
    for core, half, entry, step, slot, owner in each_slice(place, 0, mp):
        piece = outs[core].at[half, entry, step, pl.ds(offset, rows)]
        image_copies(whole, piece, quarter, half, slot, owner, sem, False)


def norm_rows(values, gain_row, shift_row):
    center = values - jnp.mean(values, axis=-1, keepdims=True)
    moment = jnp.mean(center * center, axis=-1, keepdims=True)
    return center * lax.rsqrt(moment + EPSILON) * gain_row + shift_row


def norm_back(pre_norm, gain_row, grad_out, small):
    center = pre_norm - jnp.mean(pre_norm, axis=-1, keepdims=True)
    scale = lax.rsqrt(jnp.mean(center * center, axis=-1, keepdims=True) + EPSILON)
    normal = center * scale
    lifted = grad_out * gain_row
    grad_pre = scale * (
        lifted
        - jnp.mean(lifted, axis=-1, keepdims=True)
        - normal * jnp.mean(lifted * normal, axis=-1, keepdims=True)
    )
    small[...] = jnp.zeros_like(small)
    small[0:1] = jnp.sum(grad_out * normal, axis=0, keepdims=True)
    small[1:2] = jnp.sum(grad_out, axis=0, keepdims=True)
    small[2:3] = jnp.sum(grad_pre, axis=0, keepdims=True)
    return grad_pre


def column_total(values):
    return jnp.sum(values.astype(F32), axis=0, keepdims=True)


def spread_heads(values):
    lane = lax.broadcasted_iota(jnp.int32, (1, values.shape[1]), 1)
    parts = []
    for first in range(0, values.shape[1], HEAD_DIM):
        mask = ((lane >= first) & (lane < first + HEAD_DIM)).astype(F32).astype(values.dtype)
        parts.append(values * mask)
    return jnp.concatenate(parts, axis=0)


def pick_heads(values):
    lane = lax.broadcasted_iota(jnp.int32, (1, values.shape[1]), 1)
    rows = values.shape[0] * HEAD_DIM // values.shape[1]
    picked = values[:rows]
    for head in range(1, values.shape[1] // HEAD_DIM):
        picked = jnp.where(lane >= head * HEAD_DIM, values[head * rows : (head + 1) * rows], picked)
    return picked


def softmax(scores):
    raised = jnp.exp(scores - jnp.max(scores, axis=-1, keepdims=True))
    return raised * (1.0 / jnp.sum(raised, axis=-1, keepdims=True))


def score_back(weights, grad_weights):
    along = weights * grad_weights
    return (along - weights * jnp.sum(along, axis=-1, keepdims=True)).astype(BF16)


def attention_units(count, row_size, place_size, width):
    units = []
    for number in range(count):
        rows = slice(number * row_size, (number + 1) * row_size)
        places = slice(number * place_size, (number + 1) * place_size)
        units += [(number, rows, places, slice(first, first + STACK)) for first in range(0, width, STACK)]
    return [units[first : first + TOGETHER] for first in range(0, len(units), TOGETHER)]


def attend_forward(units, allowed, query, keys, value, context):
    for group in units:
        scores = [dot_nt(spread_heads(query[rows, lanes]).astype(BF16), keys[at, lanes]) for _, rows, at, lanes in group]
        weights = [
            softmax(jnp.where(allowed(unit[0]), score * SCALE, BLOCKED)).astype(BF16)
            for unit, score in zip(group, scores)
        ]
        for (_, rows, at, lanes), weight in zip(group, weights):
            context[rows, lanes] = pick_heads(dot_nn(weight, value[at, lanes])).astype(context.dtype)


def attend_backward(units, allowed, query, keys, value, grad_context, grad_query, grad_keys, grad_value):
    for group in units:
        queries = [spread_heads(query[rows, lanes]).astype(BF16) for _, rows, _, lanes in group]
        contexts = [spread_heads(grad_context[rows, lanes]).astype(BF16) for _, rows, _, lanes in group]
        scores = [dot_nt(one, keys[at, lanes]) for one, (_, _, at, lanes) in zip(queries, group)]
        grad_weights = [dot_nt(one, value[at, lanes]) for one, (_, _, at, lanes) in zip(contexts, group)]
        weights = [
            softmax(jnp.where(allowed(unit[0]), score * SCALE, BLOCKED)) for unit, score in zip(group, scores)
        ]
        grad_scores = [score_back(one, other) for one, other in zip(weights, grad_weights)]
        for weight, one, (_, _, at, lanes) in zip(weights, contexts, group):
            grad_value[at, lanes] = dot_tn(weight.astype(BF16), one).astype(BF16)
        for grad_score, one, (_, _, at, lanes) in zip(grad_scores, queries, group):
            grad_keys[at, lanes] = (dot_tn(grad_score, one) * SCALE).astype(BF16)
        for grad_score, (_, rows, at, lanes) in zip(grad_scores, group):
            mixed = pick_heads(dot_nn(grad_score, keys[at, lanes])) * SCALE
            grad_query[rows, lanes] = mixed.astype(grad_query.dtype)


def same_segment(code_col, code_row):
    size = code_row.shape[1]

    def allowed(group):
        column = code_col[group * size : (group + 1) * size]
        return jnp.concatenate([column] * (STACK // HEAD_DIM), axis=0) == code_row[group : group + 1]

    return allowed


def real_patch(size, patches):
    column = lax.broadcasted_iota(jnp.int32, (1, size), 1)
    return lambda row: column < patches


def pick_copies(picks, parts, target, sem):
    size = parts[0].shape[0]
    for row in range(target.shape[0]):
        for number, part in enumerate(parts):

            @pl.when(picks[row] // size == number)
            def _():
                start(part.at[picks[row] % size], target.at[row], sem)


def flat_rows(rows_ref, target):
    seq = rows_ref.shape[1]
    for row in range(rows_ref.shape[0]):
        target[row * seq : (row + 1) * seq] = rows_ref[row].astype(target.dtype)


def leave_rows(values, target):
    seq = target.shape[1]
    for row in range(target.shape[0]):
        target[row] = values[row * seq : (row + 1) * seq].astype(target.dtype)


def slice_kernel(place, biases, inward, outward, feed_in, feed_out, image, first, second, third, sems):
    slot = place[0]
    quarter, width = inward.shape[2:]
    span = 4 * quarter // SLICES
    count = quarter // span
    rows = span // 2
    feed_rows = feed_in.shape[1] // SLICES
    bias_rows = biases.shape[1]
    image_rows = first.shape[1] - 2 * rows - bias_rows
    weights = first.at[:, pl.ds(0, 2 * rows + image_rows)]
    first[:, 2 * rows + image_rows :] = biases[...]

    def attention(layer, target, offset, sem):
        for half in range(2):
            row = (slot % count) * span + half * rows
            spot = target.at[half, pl.ds(offset, rows)]

            @pl.when(slot < 3 * count)
            def _():
                start(inward.at[layer, slot // count, aligned(row, rows)], spot, sem)

            @pl.when(slot >= 3 * count)
            def _():
                start(outward.at[layer, aligned(row, rows)], spot, sem)

    def feed(layer, target, offset, sem):
        for half, source in enumerate((feed_in, feed_out)):
            spot = target.at[half, pl.ds(offset, feed_rows)]
            start(source.at[layer, aligned(slot * feed_rows, feed_rows)], spot, sem)

    attention(0, first, 0, sems.at[0])
    attention(2, first, rows, sems.at[0])
    for half in range(2):
        spot = first.at[half, pl.ds(2 * rows, image_rows)]
        image_copies(image, spot, quarter, half, slot, 0, sems.at[0], False)
    feed(0, second, 0, sems.at[1])
    attention(1, second, feed_rows, sems.at[1])
    feed(1, third, 0, sems.at[2])
    for number, target in enumerate((weights, second, third)):
        finish(target, sems.at[number])


def self_forward_kernel(
    layer, norm, offset, n_parts, n_pieces, place, picks, *refs,
):
    parts, (inward, outward), refs = refs[:n_parts], refs[n_parts : n_parts + 2], refs[n_parts + 2 :]
    pieces, refs = refs[:n_pieces], refs[n_pieces:]
    bias, params, code_col, code_row, out, low, pre, query, keys, value, context, kept, whole, sems, out_sem, *held = refs
    if held:
        pick_copies(picks, parts, held[0], held[2])
    load_attention(place, (inward, outward), pieces, offset, layer, whole, sems)
    if held:
        finish(held[0], held[2])
        flat_rows(held[0], held[1])
        stream = held[1][...]
    else:
        stream = parts[0][...]
    hb = stream.astype(BF16)
    low[...] = hb
    finish(whole.at[0], sems.at[0])
    query[...] = (dot_nt(hb, whole[0]) + bias[2 * layer : 2 * layer + 1]).astype(BF16)
    finish(whole.at[1], sems.at[1])
    keys[...] = dot_nt(hb, whole[1]).astype(BF16)
    finish(whole.at[2], sems.at[2])
    value[...] = (dot_nt(hb, whole[2]) + bias[2 * layer + 1 : 2 * layer + 2]).astype(BF16)
    groups, size = code_row.shape
    units = attention_units(groups, size, size, hb.shape[1])
    attend_forward(units, same_segment(code_col, code_row), query, keys, value, context)
    finish(whole.at[3], sems.at[3])
    start(whole, kept, out_sem)
    total = dot_nn(context[...], whole[3]) + params[3 * norm : 3 * norm + 1] + stream
    pre[...] = total
    out[...] = norm_rows(total, params[3 * norm + 1 : 3 * norm + 2], params[3 * norm + 2 : 3 * norm + 3])
    finish(whole, out_sem)


def load_kept(kept, whole, sems, order):
    for mat in order:
        start(kept.at[mat], whole.at[mat], sems.at[mat])


def self_backward_kernel(
    leave, norm, spot, n_held, place, grad, low, pre, query, keys, value, context, kept, params, code_col, code_row, *refs,
):
    out, small, keep, send, whole, grads, grad_context, grad_query, grad_keys, grad_value, sems, out_sem = refs[n_held:]
    load_kept(kept, whole, sems, (3, 0, 1, 2))
    grad_pre = norm_back(pre[...], params[3 * norm + 1 : 3 * norm + 2], grad[...], small)
    branch = grad_pre.astype(BF16)
    finish(whole.at[3], sems.at[3])
    grad_context[...] = dot_nt(branch, whole[3]).astype(BF16)
    grads[3] = dot_tn(context[...], branch).astype(BF16)
    groups, size = code_row.shape
    units = attention_units(groups, size, size, branch.shape[1])
    attend_backward(
        units, same_segment(code_col, code_row), query, keys, value, grad_context, grad_query, grad_keys, grad_value
    )
    hb = low[...]
    grads[0] = dot_tn(grad_query[...], hb).astype(BF16)
    grads[1] = dot_tn(grad_keys[...], hb).astype(BF16)
    grads[2] = dot_tn(grad_value[...], hb).astype(BF16)
    store_attention(place, grads, (keep, send), spot, out_sem)
    small[3:4] = column_total(grad_query[...])
    small[4:5] = column_total(grad_value[...])
    total = grad_pre
    for mat, part in enumerate((grad_query, grad_keys, grad_value)):
        finish(whole.at[mat], sems.at[mat])
        total = total + dot_nn(part[...], whole[mat])
    if leave:
        leave_rows(total, out)
    else:
        out[...] = total
    finish(grads, out_sem)


def feed_forward_kernel(
    layer, norm, offset, n_pieces, place, rows_ref, first_weight, second_weight, *refs,
):
    pieces, refs = refs[:n_pieces], refs[n_pieces:]
    bias, params, out, low, pre, slope_out, active_out, kept, whole, slope, active, sems, out_sem = refs
    parts = whole.shape[1]
    for step in range(parts):
        for half in range(2):
            load_feed(place, (first_weight, second_weight), pieces, offset, layer, half, step, whole, sems)
    stream = rows_ref[...]
    hb = stream.astype(BF16)
    low[...] = hb
    total = params[3 * norm : 3 * norm + 1] + stream
    for step in range(parts):
        row = 6 + layer * parts + (place[1] + parts - step) % parts
        finish(whole.at[0, step], sems.at[0, step])
        units = dot_nn(hb, whole[0, step]) + bias[pl.ds(row, 1)]
        share = 0.5 * (1.0 + lax.erf(units * (2.0 ** -0.5)))
        slope[step] = share + units * jnp.exp(-0.5 * units * units) * 0.3989422804014327
        start(slope.at[step], slope_out.at[step], out_sem)
        gated = (units * share).astype(BF16)
        active[step] = gated
        start(active.at[step], active_out.at[step], out_sem)
        start(whole.at[0, step], kept.at[0, step], out_sem)
        finish(whole.at[1, step], sems.at[1, step])
        start(whole.at[1, step], kept.at[1, step], out_sem)
        total = total + dot_nn(gated, whole[1, step])
    pre[...] = total
    out[...] = norm_rows(total, params[3 * norm + 1 : 3 * norm + 2], params[3 * norm + 2 : 3 * norm + 3])
    finish(slope, out_sem)
    finish(active, out_sem)
    finish(whole, out_sem)


def feed_backward_kernel(
    norm, place, grad_in, low_in, pre_in, slope_in, active_in, kept, params,
    out, small, keep, send, whole, grads, grad, low, pre, slope, active, row_sems, sems, out_sem,
):
    parts = whole.shape[1]
    start(grad_in, grad, row_sems.at[0])
    start(pre_in, pre, row_sems.at[1])
    for step in range(parts):
        start(active_in.at[step], active.at[step], row_sems.at[3 + step])
        start(kept.at[1, step], whole.at[1, step], sems.at[1, step])
        start(slope_in.at[step], slope.at[step], row_sems.at[3 + parts + step])
        if step == 0:
            start(low_in, low, row_sems.at[2])
        start(kept.at[0, step], whole.at[0, step], sems.at[0, step])
    finish(grad, row_sems.at[0])
    finish(pre, row_sems.at[1])
    grad_pre = norm_back(pre[...], params[3 * norm + 1 : 3 * norm + 2], grad[...], small)
    branch = grad_pre.astype(BF16)
    total = grad_pre
    for step in range(parts):
        finish(active.at[step], row_sems.at[3 + step])
        grads[1, step] = dot_tn(active[step], branch).astype(BF16)
        store_feed(place, grads, (keep, send), 1, step, out_sem)
        finish(whole.at[1, step], sems.at[1, step])
        finish(slope.at[step], row_sems.at[3 + parts + step])
        grad_units = (dot_nt(branch, whole[1, step]) * slope[step]).astype(BF16)
        if step == 0:
            finish(low, row_sems.at[2])
        grads[0, step] = dot_tn(low[...], grad_units).astype(BF16)
        store_feed(place, grads, (keep, send), 0, step, out_sem)
        small[pl.ds(3 + (place[1] + parts - step) % parts, 1)] = column_total(grad_units)
        finish(whole.at[0, step], sems.at[0, step])
        total = total + dot_nt(grad_units, whole[0, step])
    out[...] = total
    finish(grads, out_sem)


def feed_both_kernel(
    layer, norm, offset, n_parts, n_pieces, place, picks, rows_ref, first_weight, second_weight, *refs,
):
    arrived, pieces, refs = refs[:n_parts], refs[n_parts : n_parts + n_pieces], refs[n_parts + n_pieces :]
    bias, params, mixed, out, small, keep, send, whole, grads, slope, active, low, pre, grad, held, sems, row_sem, out_sem = refs
    parts = whole.shape[1]
    for step in range(parts):
        for half in range(2):
            load_feed(place, (first_weight, second_weight), pieces, offset, layer, half, step, whole, sems)
    pick_copies(picks, arrived, held, row_sem)
    stream = rows_ref[...]
    low[...] = stream.astype(BF16)
    total = params[3 * norm : 3 * norm + 1] + stream
    for step in range(parts):
        row = 6 + layer * parts + (place[1] + parts - step) % parts
        finish(whole.at[0, step], sems.at[0, step])
        units = dot_nn(low[...], whole[0, step]) + bias[pl.ds(row, 1)]
        share = 0.5 * (1.0 + lax.erf(units * (2.0 ** -0.5)))
        slope[step] = share + units * jnp.exp(-0.5 * units * units) * 0.3989422804014327
        gated = (units * share).astype(BF16)
        active[step] = gated
        finish(whole.at[1, step], sems.at[1, step])
        total = total + dot_nn(gated, whole[1, step])
    pre[...] = total
    gain, shift = params[3 * norm + 1 : 3 * norm + 2], params[3 * norm + 2 : 3 * norm + 3]
    leave_rows(norm_rows(total, gain, shift), mixed)
    finish(held, row_sem)
    flat_rows(held, grad)
    grad_pre = norm_back(pre[...], gain, grad[...], small)
    branch = grad_pre.astype(BF16)
    total = grad_pre
    for step in range(parts):
        grads[1, step] = dot_tn(active[step], branch).astype(BF16)
        store_feed(place, grads, (keep, send), 1, step, out_sem)
        grad_units = (dot_nt(branch, whole[1, step]) * slope[step]).astype(BF16)
        grads[0, step] = dot_tn(low[...], grad_units).astype(BF16)
        store_feed(place, grads, (keep, send), 0, step, out_sem)
        small[pl.ds(3 + (place[1] + parts - step) % parts, 1)] = column_total(grad_units)
        total = total + dot_nt(grad_units, whole[0, step])
    out[...] = total
    finish(grads, out_sem)


def finish_all(whole, sems):
    for mat in range(whole.shape[0]):
        finish(whole.at[mat], sems.at[mat])


def image_forward_kernel(
    layer, offset, image_offset, image_rows, n_pieces, place, images, image, inward, outward, *refs,
):
    pieces, refs = refs[:n_pieces], refs[n_pieces:]
    bias, projected, keys, value, kept_image, whole, whole_image, sems, image_sem, out_sem = refs
    load_image(place, image, pieces, image_offset, image_rows, whole_image, image_sem)
    load_attention(place, (inward, outward), pieces, offset, layer, whole, sems)
    finish(whole_image, image_sem)
    start(whole_image, kept_image, out_sem)
    size = images.shape[0] // 4
    last = bias.shape[0] - 1
    for first in range(0, images.shape[0], size):
        rows = slice(first, first + size)
        source = (dot_nt(images[rows], whole_image[...]) + bias[last : last + 1]).astype(BF16)
        projected[rows] = source
        if first == 0:
            finish_all(whole, sems)
        keys[rows] = dot_nt(source, whole[1]).astype(BF16)
        value[rows] = (dot_nt(source, whole[2]) + bias[2 * layer + 1 : 2 * layer + 2]).astype(BF16)
    finish(whole_image, out_sem)


def cross_forward_kernel(
    layer, norm, offset, seq, patches, n_pieces, place, rows_ref, keys, value, inward, outward, *refs,
):
    pieces, refs = refs[:n_pieces], refs[n_pieces:]
    bias, params, out, low, pre, query, context, kept, whole, mixed, sems, out_sem = refs
    load_attention(place, (inward, outward), pieces, offset, layer, whole, sems)
    stream = rows_ref[...]
    hb = stream.astype(BF16)
    low[...] = hb
    finish_all(whole, sems)
    start(whole, kept, out_sem)
    query[...] = (dot_nt(hb, whole[0]) + bias[2 * layer : 2 * layer + 1]).astype(BF16).astype(F32)
    count = stream.shape[0] // seq
    size = keys.shape[0] // count
    units = attention_units(count, seq, size, hb.shape[1])
    attend_forward(units, real_patch(size, patches), query, keys, value, mixed)
    context[...] = mixed[...].astype(BF16)
    total = dot_nn(context[...], whole[3]) + params[3 * norm : 3 * norm + 1] + stream
    pre[...] = total
    out[...] = norm_rows(total, params[3 * norm + 1 : 3 * norm + 2], params[3 * norm + 2 : 3 * norm + 3])
    finish(whole, out_sem)


def cross_backward_kernel(
    norm, seq, patches, place, grad, low, pre, query, context, keys, value, kept, params,
    out, small, grad_keys, grad_value, branch_out, query_out, whole, grad_context, grad_query, sems,
):
    load_kept(kept, whole, sems, (3, 0))
    grad_pre = norm_back(pre[...], params[3 * norm + 1 : 3 * norm + 2], grad[...], small)
    branch = grad_pre.astype(BF16)
    branch_out[...] = branch
    finish(whole.at[3], sems.at[3])
    grad_context[...] = dot_nt(branch, whole[3]).astype(BF16).astype(F32)
    count = branch.shape[0] // seq
    size = keys.shape[0] // count
    units = attention_units(count, seq, size, branch.shape[1])
    attend_backward(
        units, real_patch(size, patches), query, keys, value, grad_context, grad_query, grad_keys, grad_value
    )
    query_low = grad_query[...].astype(BF16)
    query_out[...] = query_low
    small[3:4] = column_total(query_low)
    small[4:5] = column_total(grad_value[...])
    finish(whole.at[0], sems.at[0])
    out[...] = grad_pre + dot_nn(query_low, whole[0])


def cross_weights_kernel(
    spot, place, context, branch, grad_query, low, grad_keys, grad_value, source, keep_held, send_held,
    keep, send, grads, out_sem,
):
    grads[3] = dot_tn(context[...], branch[...]).astype(BF16)
    grads[0] = dot_tn(grad_query[...], low[...]).astype(BF16)
    grads[1] = dot_tn(grad_keys[...], source[...]).astype(BF16)
    grads[2] = dot_tn(grad_value[...], source[...]).astype(BF16)
    store_attention(place, grads, (keep, send), spot, out_sem)
    finish(grads, out_sem)


def image_backward_kernel(
    image_rows, spot, n_held, place, images, grad_keys, grad_value, kept, kept_image, *refs,
):
    out, small, keep, send, whole, whole_image, grads, low, sems, image_sem, out_sem = refs[n_held:]
    load_kept(kept, whole, sems, (1, 2))
    start(kept_image, whole_image, image_sem)
    finish(whole.at[1], sems.at[1])
    finish(whole.at[2], sems.at[2])
    finish(whole_image, image_sem)
    patches, count = out.shape[:2]
    size = images.shape[0] // count
    small[...] = jnp.zeros_like(small)
    for row in range(count):
        rows = slice(row * size, (row + 1) * size)
        source = dot_nn(grad_keys[rows], whole[1]) + dot_nn(grad_value[rows], whole[2])
        source = source.astype(BF16)
        low[rows] = source
        out[:, row, :] = dot_nn(source, whole_image[...])[:patches]
    grads[...] = dot_tn(low[...], images[...]).astype(BF16)
    store_image(place, grads, (keep, send), spot, image_rows, out_sem)
    small[0:1] = column_total(low[...])
    finish(grads, out_sem)


def combine_kernel(
    keep, core, one0, one1, two0, two1, own, down, across, up, kept, arrived, first, second, sems,
):
    for half, (one, two) in enumerate(((one0, two0), (one1, two1))):
        start(keep.at[half, 0], kept.at[half], sems.at[0])
        start(core.at[half, 0], arrived.at[half], sems.at[1])
        start(one.at[0], first.at[half], sems.at[2])
        start(two, second.at[half], sems.at[3])
    for number, target in enumerate((kept, arrived, first, second)):
        finish(target, sems.at[number])
    for step, target in enumerate((own, down, across, up)):
        for half in range(2):
            total = kept[half, step].astype(F32) + arrived[half, step].astype(F32)
            total = total + first[half, step].astype(F32) + second[half, step].astype(F32)
            target[half] = total.astype(target.dtype)


def pick_kernel(picks, *refs):
    *parts, out, held, sem = refs
    pick_copies(picks, parts, held, sem)
    finish(held, sem)
    out[...] = held[...].astype(out.dtype)


def finish_kernel(blocks, quarter, names, held, n_results, place, *refs):
    results, refs = refs[:n_results], refs[n_results:]
    width = results[0].shape[3]
    targets = dict(zip(names, refs[held:]))
    scratch = refs[held + len(names) :]
    sem, out_sem = scratch[-2:]
    for number, (kind, offset, _) in enumerate(blocks):
        buffer = scratch[2 * number]
        for core in range(2):
            for half in range(2):
                for entry in range(4):
                    if n_results == 1:
                        slot = core ^ DISTANCES[half][entry]
                        piece = results[0].at[slot, half]
                    else:
                        slot = place[0] ^ (core ^ DISTANCES[half][entry])
                        piece = piece_of(results, core, half, entry)
                    if kind == ATTENTION:
                        rows = quarter // 4
                        spot = attention_spot(buffer, quarter, half, slot, 0)
                        start(piece.at[pl.ds(offset, rows)], spot, sem.at[number])
                    elif kind == FEED:
                        rows = buffer.shape[1] // SLICES
                        spot = buffer.at[half, aligned(slot * rows, rows)]
                        start(piece.at[pl.ds(offset, rows)], spot, sem.at[number])
                    else:
                        rows = quarter * buffer.shape[1] // width // SLICES // 2
                        piece = piece.at[pl.ds(offset, rows)]
                        image_copies(buffer, piece, quarter, half, slot, 0, sem.at[number], True)
    for number, (kind, _, layer) in enumerate(blocks):
        buffer, wide = scratch[2 * number : 2 * number + 2]
        done = out_sem.at[number]
        finish(buffer, sem.at[number])
        wide[...] = buffer[...].astype(F32)
        if kind == ATTENTION:
            start(wide.at[pl.ds(0, 3)], targets[ATTENTION_IN].at[layer], done)
            start(wide.at[3], targets[ATTENTION_OUT].at[layer], done)
        elif kind == FEED:
            start(wide.at[0], targets[FEED_IN].at[layer], done)
            start(wide.at[1], targets[FEED_OUT].at[layer], done)
        else:
            start(wide, targets[IMAGE], done)
    for number in range(len(blocks)):
        finish(scratch[2 * number + 1], out_sem.at[number])


def shape(dims, kind=F32):
    return jax.ShapeDtypeStruct(tuple(dims), kind)


def call(kernel, ins, outs, scratch, aliases=None):
    return pl.pallas_call(
        kernel,
        in_specs=[spec for _, spec in ins],
        out_specs=[spec for _, spec in outs],
        out_shape=[s for s, _ in outs],
        scratch_shapes=scratch,
        input_output_aliases=aliases or {},
        compiler_params=pltpu.CompilerParams(vmem_limit_bytes=60 << 20),
        cost_estimate=pl.CostEstimate(flops=0, bytes_accessed=0, transcendentals=0),
    )(*[v for v, _ in ins])


class Ring:
    def __init__(self, at, name, own):
        self.at, self.name = at, name
        at[name] = {0: own}

    def up(self):
        parts = self.at[self.name]
        parts[1] = pass_on(parts[0])

    def down(self):
        parts = self.at[self.name]
        parts[3] = pass_on(parts[0], -1)

    def far(self):
        parts = self.at[self.name]
        parts[2] = pass_on(parts[1])

    def direct(self):
        parts = self.at[self.name]
        for way in (1, 2, 3):
            parts[way] = pass_on(parts[0], way)

    def take(self):
        parts = self.at.pop(self.name)
        return [parts[i] for i in range(4)]


class Widen:
    def __init__(self, at, name, first, second):
        self.at, self.name = at, name
        at[name] = {"own": (first, second)}

    def one(self):
        held = self.at[self.name]
        first, second = held.pop("own")
        held["both"] = (first, swap(first, 2), second, swap(second, 4))

    def two(self):
        held = self.at[self.name]
        both = held.pop("both")
        near = jnp.stack(both[:2]), jnp.stack(both[2:])
        held["near"] = near
        held["far"] = swap(near[0], 4), swap(near[1], 2)

    def direct(self):
        held = self.at[self.name]
        own = held.pop("own")
        held["lines"] = [jnp.stack(own)] + [swap(jnp.stack(own), bit) for bit in (2, 4, 6)]

    def two_early(self):
        self.two()
        held = self.at[self.name]
        held["near all"] = jnp.stack(held.pop("near"))
        held["near core"] = swap(held["near all"], 1)

    def core_late(self):
        held = self.at[self.name]
        held["far all"] = jnp.stack(held.pop("far"))
        held["far core"] = swap(held["far all"], 1)

    def core_direct(self):
        held = self.at[self.name]
        lines = held.pop("lines")
        order = [[distance // 2 for distance in half] for half in DISTANCES]
        held["all"] = jnp.stack([jnp.stack([lines[i][half] for i in order[half]]) for half in range(2)])
        held["core"] = swap(held["all"], 1)

    def core(self):
        held = self.at[self.name]
        near, far = held.pop("near"), held.pop("far")
        held["all"] = jnp.stack([jnp.concatenate([near[half], far[half]]) for half in range(2)])
        held["core"] = swap(held["all"], 1)

    def take(self):
        held = self.at.pop(self.name)
        if "all" in held:
            return held["all"], held["core"]
        return held["near all"], held["far all"], held["near core"], held["far core"]


class Reduce:
    def __init__(self, at, name, keep, send):
        self.at, self.name = at, name
        at[name] = {"keep": keep, "send": send}

    def core(self):
        held = self.at[self.name]
        held["core"] = swap(held.pop("send"), 1)

    def one(self):
        held = self.at[self.name]
        keep, core = held["keep"], held["core"]
        held["one"] = swap(added(keep[0, 2:], core[0, 2:]), 4), swap(added(keep[1, 2:], core[1, 2:]), 2)

    def two(self):
        held = self.at[self.name]
        keep, core, one = held["keep"], held["core"], held["one"]
        held["two"] = (
            swap(added(keep[0, 1], core[0, 1], one[0][1]), 2),
            swap(added(keep[1, 1], core[1, 1], one[1][1]), 4),
        )

    def combine(self):
        held = self.at[self.name]
        arrays = [held[name] for name in ("keep", "core")] + list(held["one"]) + list(held["two"])
        rows, width = arrays[0].shape[3:]
        mp = arrays[0].shape[2]
        outs = [shape((2, rows, width), kind) for kind in (F32, BF16, BF16, F32)]
        parts = call(
            combine_kernel,
            [(v, ANY) for v in arrays],
            [(v, VMEM) for v in outs],
            [pltpu.VMEM((2, mp, rows, width), BF16)] * 4 + [pltpu.SemaphoreType.DMA((4,))],
        )
        self.at[self.name] = {"own": parts[0], "parts": parts[1:]}

    def join(self, other):
        theirs = self.at.pop(other.name)
        held = self.at[self.name]
        held["own"] = jnp.concatenate([held["own"], theirs["own"]], axis=1)
        held["parts"] = [jnp.concatenate(pair, axis=1) for pair in zip(held["parts"], theirs["parts"])]

    def far(self):
        held = self.at[self.name]
        held["far"] = pass_on(held["parts"][1])

    def near(self):
        held = self.at[self.name]
        down, _, up = held.pop("parts")
        held["up"] = pass_on(added(up, held.pop("far")))
        held["down"] = pass_on(down, -1)

    def direct(self):
        held = self.at[self.name]
        down, across, up = held.pop("parts")
        held["up"], held["across"], held["down"] = pass_on(added(up)), pass_on(across, 2), pass_on(down, -1)

    def owned(self):
        held = self.at.pop(self.name)
        own = added(held["own"], *[held[name] for name in ("up", "across", "down") if name in held])
        bit = SLICES
        while bit < lax.axis_size("dp"):
            own = added(own, swap(own, bit))
            bit *= 2
        return own


def on_device(
    tokens, images, segment_of_token, image_of_row, attention_in, query_value_bias, attention_out, output_bias,
    feed_in, feed_bias, feed_out, image_weight, image_bias, norm_gain, norm_bias, cotangent,
):
    mp = lax.axis_size("mp")
    slot = lax.axis_index("dp") % SLICES
    owner = lax.axis_index("mp")
    place = jnp.stack([slot, owner]).astype(jnp.int32)
    own_rows, seq, width = tokens.shape
    group_rows = segment_of_token.shape[0]
    patches, image_width = images.shape[1:]
    quarter = attention_in.shape[3]
    units = feed_in.shape[2]
    n_tokens = own_rows * seq
    inward = attention_in.transpose(0, 1, 3, 2)
    image = image_weight.T

    attention_rows = quarter // 4
    feed_rows = units // SLICES
    image_rows = quarter * image_width // width // SLICES // 2

    token_shape = shape((n_tokens, width))
    token_low = shape((n_tokens, width), BF16)
    row_low = shape((own_rows, seq, width), BF16)
    inner_shape = shape((mp, n_tokens, units))
    inner_low = shape((mp, n_tokens, units), BF16)
    padded = -(-patches // 16) * 16
    n_patches = own_rows * padded
    patch_low = shape((n_patches, width), BF16)
    small_shape = shape((8, width))
    attention_grad = shape((2, 4, mp, attention_rows, width), BF16)
    feed_grad = shape((2, 4, mp, feed_rows, width), BF16)
    image_grad = shape((2, 4, mp, image_rows, width), BF16)
    kept_square = shape((4, width, width), BF16)
    kept_wide = shape((2, mp, units, width), BF16)
    kept_tall = shape((width, image_width), BF16)
    square = pltpu.VMEM((4, width, width), BF16)
    wide = pltpu.VMEM((2, mp, units, width), BF16)
    tall = pltpu.VMEM((width, image_width), BF16)
    token_f32 = pltpu.VMEM((n_tokens, width), F32)
    token_bf16 = pltpu.VMEM((n_tokens, width), BF16)
    row_bf16 = pltpu.VMEM((own_rows, seq, width), BF16)
    inner_f32 = pltpu.VMEM((mp, n_tokens, units), F32)
    inner_bf16 = pltpu.VMEM((mp, n_tokens, units), BF16)
    dma = pltpu.SemaphoreType.DMA
    matmul = 2 * n_tokens * width * width
    patch_matmul = 2 * n_patches * width * width

    local_order = image_of_row % group_rows
    here = owner * own_rows + jnp.arange(own_rows, dtype=jnp.int32)
    chosen = (local_order[None, :] == here[:, None]).astype(jnp.int32)
    source_row = jnp.sum(chosen * jnp.arange(group_rows, dtype=jnp.int32)[None, :], axis=1)
    picks_in = ((owner - source_row // own_rows) % mp) * own_rows + source_row % own_rows
    mine = (jnp.arange(group_rows, dtype=jnp.int32)[None, :] == here[:, None]).astype(jnp.int32)
    image_row = jnp.sum(mine * local_order[None, :], axis=1)
    picks_out = ((owner - image_row // own_rows) % mp) * own_rows + image_row % own_rows
    segments = jnp.sum(chosen[:, :, None] * segment_of_token[None], axis=1)
    code = jnp.arange(own_rows, dtype=jnp.int32)[:, None] * seq + segments
    code_col = code.reshape(n_tokens, 1)
    code_row = code.reshape(own_rows // 2, 2 * seq)

    flat = jnp.concatenate([query_value_bias.reshape(-1), feed_bias.reshape(-1), image_bias])
    bias_rows = -(-flat.shape[0] // (32 * width)) * 16
    biases = jnp.pad(flat, (0, 2 * bias_rows * width - flat.shape[0])).reshape(2, bias_rows, width)
    first_rows = 2 * attention_rows + image_rows
    first, second, third = call(
        slice_kernel,
        [(place, SMEM), (biases, VMEM)] + [(v, ANY) for v in (inward, attention_out, feed_in, feed_out, image)],
        [
            (shape((2, rows, width), BF16), VMEM)
            for rows in (first_rows + bias_rows, feed_rows + attention_rows, feed_rows)
        ],
        [dma((3,))],
    )

    at = {}

    def step():
        done = lax.optimization_barrier(at)
        at.clear()
        at.update(done)

    rings = {
        name: Ring(at, name, own)
        for name, own in (
            ("first", first), ("second", second), ("third", third), (TOKENS, tokens), (COTANGENT, cotangent),
        )
    }

    def gathered(name, rows=None):
        parts = rings[name].take()[1:]
        return Widen(at, name, *[jnp.stack([part[half, :rows] for part in parts]) for half in range(2)])

    rings["first"].direct()
    step()

    parts = [part[:, first_rows:].reshape(-1) for part in at["first"].values()]
    ordered = jnp.stack(parts)[(owner - jnp.arange(mp)) % mp].astype(F32)
    cut0 = query_value_bias.size
    cut1 = cut0 + feed_bias.size
    bias = jnp.concatenate(
        [
            ordered[:, :cut0].reshape(mp, -1, quarter).transpose(1, 0, 2).reshape(-1, width),
            ordered[:, cut0:cut1].reshape(mp, 2, units).transpose(1, 0, 2).reshape(-1, width),
            ordered[:, cut1 : cut1 + quarter].reshape(1, width),
        ]
    )
    params = jnp.stack([output_bias, norm_gain, norm_bias], axis=1).astype(F32).reshape(-1, width)
    patch_rows = jnp.pad(images, ((0, 0), (0, padded - patches), (0, 0))).reshape(n_patches, image_width)
    at["tables"] = bias, params, code_col, code_row, picks_in, picks_out, image_row, patch_rows
    first_wide = gathered("first", first_rows)
    first_wide.one()
    rings["second"].up()
    rings["second"].down()
    rings[TOKENS].up()
    step()
    bias, params, code_col, code_row, picks_in, picks_out, image_row, patch_rows = at.pop("tables")
    first_wide.two()
    rings["second"].far()
    rings[TOKENS].down()
    rings["third"].up()
    step()
    second_wide = gathered("second")
    first_wide.core()
    second_wide.one()
    rings[TOKENS].far()
    rings["third"].down()
    step()

    attention_pieces = [None, None, None]
    attention_at = [0, feed_rows, attention_rows]
    feed_pieces = [None, None]
    feed_at = [0, 0]

    def attention_ins(layer):
        return [(inward, ANY), (attention_out, ANY)] + [(piece, ANY) for piece in attention_pieces[layer]]

    def feed_ins(layer):
        return [(feed_in, ANY), (feed_out, ANY)] + [(piece, ANY) for piece in feed_pieces[layer]]

    def self_forward(layer, norm, parts):
        picked = len(parts) > 1
        return call(
            partial(self_forward_kernel, layer, norm, attention_at[layer], len(parts), len(attention_pieces[layer])),
            [(place, SMEM), (picks_in, SMEM)]
            + [(part, ANY if picked else VMEM) for part in parts]
            + attention_ins(layer)
            + [(bias, VMEM), (params, VMEM), (code_col, VMEM), (code_row, VMEM)],
            [(token_shape, VMEM), (token_low, VMEM), (token_shape, VMEM)] + [(token_low, VMEM)] * 4 + [(kept_square, ANY)],
            [square, dma((4,)), dma] + ([row_bf16, token_f32, dma] if picked else []),
        )

    def self_backward(norm, grad, kept, leave, spot, rows, held):
        _, low, pre, query, keys, value, context, weights = kept
        grads = shape((2, 4, mp, rows, width), BF16)
        ins = [(place, SMEM)] + [(v, VMEM) for v in (grad, low, pre, query, keys, value, context)]
        ins += [(weights, ANY), (params, VMEM), (code_col, VMEM), (code_row, VMEM)]
        return call(
            partial(self_backward_kernel, leave, norm, spot, len(held)),
            ins + [(v, ANY) for v in held],
            [(row_low if leave else token_shape, VMEM), (small_shape, VMEM)] + [(grads, ANY)] * 2,
            [square, square] + [token_bf16] * 4 + [dma((4,)), dma],
            {len(ins) + i: 2 + i for i in range(len(held))},
        )

    def feed_forward(layer, norm, rows):
        return call(
            partial(feed_forward_kernel, layer, norm, feed_at[layer], len(feed_pieces[layer])),
            [(place, SMEM), (rows, VMEM)] + feed_ins(layer) + [(bias, VMEM), (params, VMEM)],
            [(token_shape, VMEM), (token_low, VMEM), (token_shape, VMEM)]
            + [(inner_shape, ANY), (inner_low, ANY), (kept_wide, ANY)],
            [wide, inner_f32, inner_bf16, dma((2, mp)), dma],
        )

    def feed_backward(norm, grad, kept):
        _, low, pre, slope, active, weights = kept
        return call(
            partial(feed_backward_kernel, norm),
            [(place, SMEM)] + [(v, ANY) for v in (grad, low, pre, slope, active, weights)] + [(params, VMEM)],
            [(token_shape, VMEM), (small_shape, VMEM)] + [(feed_grad, ANY)] * 2,
            [wide, wide, token_f32, token_bf16, token_f32, inner_f32, inner_bf16]
            + [dma((3 + 2 * mp,)), dma((2, mp)), dma],
        )

    def feed_both(layer, norm, rows, parts):
        return call(
            partial(feed_both_kernel, layer, norm, feed_at[layer], len(parts), len(feed_pieces[layer])),
            [(place, SMEM), (picks_in, SMEM), (rows, VMEM), (feed_in, ANY), (feed_out, ANY)]
            + [(v, ANY) for v in parts + list(feed_pieces[layer])]
            + [(bias, VMEM), (params, VMEM)],
            [(row_low, VMEM), (token_shape, VMEM), (small_shape, VMEM)] + [(feed_grad, ANY)] * 2,
            [wide, wide, inner_f32, inner_bf16, token_bf16, token_f32, token_f32, row_bf16]
            + [dma((2, mp)), dma, dma],
        )

    def pick_rows(parts):
        return call(
            pick_kernel,
            [(picks_out, SMEM)] + [(part, ANY) for part in parts],
            [(shape((own_rows, seq, width)), VMEM)],
            [row_bf16, dma],
        )[0]

    attention_pieces[0] = attention_pieces[2] = first_wide.take()
    second_wide.two_early()
    rings["third"].far()
    rings[COTANGENT].up()
    text_attention = self_forward(0, 0, rings[TOKENS].take())
    at["stream"] = text_attention[0]
    step()

    second_wide.core_late()
    third_wide = gathered("third")
    third_wide.one()
    rings[COTANGENT].down()
    projected, image_keys, image_value, kept_image = call(
        partial(image_forward_kernel, 2, attention_rows, 2 * attention_rows, image_rows, len(attention_pieces[2])),
        [(place, SMEM), (patch_rows, VMEM), (image, ANY)] + attention_ins(2) + [(bias, VMEM)],
        [(patch_low, VMEM)] * 3 + [(kept_tall, ANY)],
        [square, tall, dma((4,)), dma, dma],
    )
    at["keys"] = image_keys
    step()

    attention_pieces[1] = feed_pieces[0] = second_wide.take()
    third_wide.two()
    rings[COTANGENT].far()
    text_feed = feed_forward(0, 1, at.pop("stream"))
    joining_attention = self_forward(1, 2, [text_feed[0]])
    at["stream"] = joining_attention[0]
    step()

    third_wide.core()
    image_keys = at.pop("keys")
    cross_attention = call(
        partial(cross_forward_kernel, 2, 3, attention_rows, seq, patches, len(attention_pieces[2])),
        [(place, SMEM), (at.pop("stream"), VMEM), (image_keys, VMEM), (image_value, VMEM)]
        + attention_ins(2)
        + [(bias, VMEM), (params, VMEM)],
        [(token_shape, VMEM), (token_low, VMEM), (token_shape, VMEM), (token_shape, VMEM), (token_low, VMEM)]
        + [(kept_square, ANY)],
        [square, token_f32, dma((4,)), dma],
    )
    at["stream"] = cross_attention[0]
    step()

    feed_pieces[1] = third_wide.take()

    mixed, grad, small_joining_feed, keep, send = feed_both(1, 4, at.pop("stream"), rings[COTANGENT].take())
    mixed_ring = Ring(at, "mixed", mixed)
    at["grad"] = grad
    last_grads = Reduce(at, "last", keep, send)
    step()

    last_grads.core()
    mixed_ring.up()
    grad, small_cross, grad_keys, grad_value, cross_branch, cross_query = call(
        partial(cross_backward_kernel, 3, seq, patches),
        [(place, SMEM), (at.pop("grad"), VMEM)]
        + [(cross_attention[i], VMEM) for i in (1, 2, 3, 4)]
        + [(image_keys, VMEM), (image_value, VMEM), (cross_attention[5], ANY), (params, VMEM)],
        [(token_shape, VMEM), (small_shape, VMEM)] + [(patch_low, VMEM)] * 2 + [(token_low, VMEM)] * 2,
        [square, token_f32, token_f32, dma((4,))],
    )
    at["grad"] = grad
    step()

    last_grads.one()
    mixed_ring.down()
    middle_rows = 2 * attention_rows
    grad, small_joining, keep, send = self_backward(
        2, at.pop("grad"), joining_attention, False, attention_rows, middle_rows, ()
    )
    at["grad"] = grad
    cross_grads = (cross_attention[4], cross_branch, cross_query, cross_attention[1], grad_keys, grad_value, projected)
    keep, send = call(
        partial(cross_weights_kernel, 0),
        [(place, SMEM)] + [(v, VMEM) for v in cross_grads] + [(keep, ANY), (send, ANY)],
        [(shape(keep.shape, BF16), ANY)] * 2,
        [square, dma],
        {8: 0, 9: 1},
    )
    middle_grads = Reduce(at, "middle", keep, send)
    at["patch grads"] = grad_keys, grad_value
    step()

    last_grads.two()
    middle_grads.core()
    mixed_ring.far()
    grad, small_text_feed, keep, send = feed_backward(1, at.pop("grad"), text_feed)
    at["grad"] = grad
    first_grads = Reduce(at, "first", keep, send)
    step()

    mixed_parts = mixed_ring.take()
    middle_grads.one()
    first_grads.core()
    last_grads.combine()
    held = at["last"]
    down, across, up = held.pop("parts")
    held["up"], held["down"] = pass_on(up.astype(BF16)), pass_on(down, -1)
    held["across part"] = across
    rows_back, small_text, keep, send = self_backward(
        0, at.pop("grad"), text_attention, True, 0, attention_rows + image_rows, ()
    )
    back_ring = Ring(at, "back", rows_back)
    at["text"] = keep, send
    step()

    middle_grads.two()
    first_grads.one()
    at["last"]["across"] = pass_on(at["last"].pop("across part"), 2)
    grad_keys, grad_value = at.pop("patch grads")
    keep, send = at.pop("text")
    grad_images, small_image, keep, send = call(
        partial(image_backward_kernel, image_rows, attention_rows, 2),
        [(place, SMEM), (patch_rows, VMEM), (grad_keys, VMEM), (grad_value, VMEM), (cross_attention[5], ANY)]
        + [(kept_image, ANY), (keep, ANY), (send, ANY)],
        [(shape((patches, own_rows, image_width)), VMEM), (small_shape, VMEM)] + [(shape(keep.shape, BF16), ANY)] * 2,
        [square, tall, tall, pltpu.VMEM((n_patches, width), BF16), dma((4,)), dma, dma],
        {6: 2, 7: 3},
    )
    text_grads = Reduce(at, "text", keep, send)
    at[SMALL] = jnp.concatenate(
        [small_text, small_text_feed, small_joining, small_cross, small_joining_feed, small_image]
    )
    step()

    first_grads.two()
    text_grads.core()
    middle_grads.combine()
    middle_grads.far()
    back_ring.up()
    at["mixed"] = pick_rows(mixed_parts)
    step()

    text_grads.one()
    middle_grads.near()
    first_grads.combine()
    first_grads.far()
    at[SMALL] = at[SMALL] + swap(at[SMALL], 1)
    at["last own"] = last_grads.owned()
    step()

    early = Widen(at, "early", *jnp.concatenate([at.pop("last own"), middle_grads.owned()], axis=1))
    early.one()
    text_grads.two()
    first_grads.near()
    back_ring.down()
    at[SMALL] = at[SMALL] + swap(at[SMALL], 2)
    step()

    early.two()
    text_grads.combine()
    text_grads.direct()
    at["first own"] = first_grads.owned()
    at[SMALL] = at[SMALL] + swap(at[SMALL], 4)
    step()

    late = Widen(at, "late", *jnp.concatenate([at.pop("first own"), text_grads.owned()], axis=1))
    late.one()
    early.core()
    back_ring.far()
    at[SMALL] = at[SMALL] + swap_owner(at[SMALL], 1)
    step()

    late.two()
    at[TOKENS] = pick_rows(back_ring.take())
    early_pieces = early.take()
    smalls = at.pop(SMALL)
    smalls = smalls + swap_owner(smalls, 2)
    bit = SLICES
    while bit < lax.axis_size("dp"):
        smalls = smalls + swap(smalls, bit)
        bit *= 2
    at[SMALL] = smalls

    whole_shapes = {
        ATTENTION_IN: shape(inward.shape),
        ATTENTION_OUT: shape(attention_out.shape),
        FEED_IN: shape(feed_in.shape),
        FEED_OUT: shape(feed_out.shape),
        IMAGE: shape(image.shape),
    }
    block_of = {ATTENTION: (4, quarter, width), FEED: (2, units, width), IMAGE: (quarter, image_width)}
    names_of = {ATTENTION: [ATTENTION_IN, ATTENTION_OUT], FEED: [FEED_IN, FEED_OUT], IMAGE: [IMAGE]}
    written = {}

    def write_out(result, *blocks):
        names = list(dict.fromkeys(name for kind, _, _ in blocks for name in names_of[kind]))
        names = [name for name in names if name in written] + [name for name in names if name not in written]
        held = [name for name in names if name in written]
        scratch = [pltpu.VMEM(block_of[kind], form) for kind, _, _ in blocks for form in (BF16, F32)]
        results = call(
            partial(finish_kernel, blocks, quarter, names, len(held), len(result)),
            [(place, SMEM)] + [(v, ANY) for v in result] + [(written[name], ANY) for name in held],
            [(whole_shapes[name], ANY) for name in names],
            scratch + [dma((len(blocks),)), dma((len(blocks),))],
            {1 + len(result) + i: i for i in range(len(held))},
        )
        written.update(zip(names, results))

    write_out(
        early_pieces, (FEED, 0, 1), (ATTENTION, feed_rows, 2), (ATTENTION, feed_rows + attention_rows, 1)
    )
    at["written"] = written
    step()
    written = at.pop("written")
    late.core()
    smalls = at.pop(SMALL).reshape(6, 8, width)

    def own_part(values):
        return lax.dynamic_slice_in_dim(values, owner * quarter, quarter, axis=values.ndim - 1)

    grad_query_value_bias = own_part(jnp.stack([smalls[i, 3:5] for i in (0, 2, 3)]))
    grad_feed_bias = jnp.stack([smalls[i, 3 : 3 + mp].reshape(-1) for i in (1, 4)])
    grad_feed_bias = lax.dynamic_slice_in_dim(grad_feed_bias, owner * units, units, axis=1)
    vectors = (
        grad_query_value_bias, smalls[:5, 2], grad_feed_bias, own_part(smalls[5, 0]), smalls[:5, 0], smalls[:5, 1]
    )
    at["vectors"] = vectors
    step()
    vectors = at.pop("vectors")
    write_out(
        late.take(), (FEED, 0, 0), (ATTENTION, feed_rows, 0), (IMAGE, feed_rows + attention_rows, 0)
    )
    return (
        at["mixed"],
        at[TOKENS],
        grad_images.transpose(1, 0, 2),
        written[ATTENTION_IN].transpose(0, 1, 3, 2),
        vectors[0],
        written[ATTENTION_OUT],
        vectors[1],
        written[FEED_IN],
        vectors[2],
        written[FEED_OUT],
        written[IMAGE].T,
        vectors[3],
        vectors[4],
        vectors[5],
    )


def solution(mesh):
    rows = P(("dp", "mp"), None, None)
    return jax.shard_map(
        on_device,
        mesh=mesh,
        in_specs=(
            rows,
            rows,
            P("dp", None),
            P("dp"),
            P(None, None, None, "mp"),
            P(None, None, "mp"),
            P(None, "mp", None),
            P(),
            P(None, None, "mp"),
            P(None, "mp"),
            P(None, "mp", None),
            P(None, "mp"),
            P("mp"),
            P(),
            P(),
            rows,
        ),
        out_specs=(
            rows,
            rows,
            rows,
            P(None, None, None, "mp"),
            P(None, None, "mp"),
            P(None, "mp", None),
            P(),
            P(None, None, "mp"),
            P(None, "mp"),
            P(None, "mp", None),
            P(None, "mp"),
            P("mp"),
            P(),
            P(),
        ),
        check_vma=False,
    )
```

time: 708 us -> 573 us (0.81)
  local copies, waits for them, and re-layouts: 83.6 us -> 27 us
  starting transfers between devices: 144 us -> 99.6 us
  Pallas kernels: 213 us -> 199 us
  waiting for transfers between devices: 194 us -> 183 us
    unnamed x487 -> x122, local copies, waits for them, and re-layouts: 75 us -> 11.2 us
    ppermute x95 -> x49, waiting for transfers between devices: 83.4 us -> 44.2 us  [swap(): return lax.ppermute(values, 'dp', [(i, i ^ bit) for i in range(count)])]
    ppermute x95 -> x49, starting transfers between devices: 72.6 us -> 42.7 us  [swap(): return lax.ppermute(values, 'dp', [(i, i ^ bit) for i in range(count)])]
    ppermute x42 -> x33, waiting for transfers between devices: 105 us -> 124 us  [pass_on(): lax.ppermute(values, 'mp', [(i, (i + way) % count) for i in range(count)])]
    pallas_call x19 -> x21, Pallas kernels: 213 us -> 199 us  [call(): pl.pallas_call(kernel, in_specs=[spec for _, spec in ins], out_specs=[spe...]
    ppermute x42 -> x33, starting transfers between devices: 66.9 us -> 55.7 us  [pass_on(): lax.ppermute(values, 'mp', [(i, (i + way) % count) for i in range(count)])]
    ppermute x2, waiting for transfers between devices: 5.81 us -> 15.3 us  [swap_owner(): return lax.ppermute(values, 'mp', [(i, i ^ bit) for i in range(count)])]
    another operation x18 -> x8, other arithmetic: 10.7 us -> 2.59 us  [two(): near = (jnp.stack(both[:2]), jnp.stack(both[2:]))]
  transfers between devices with their start and end apart: 139 -> 84, of which waited for: 43 -> 28; matrix products, arithmetic and copies ran while one was open for 9% -> 9% of each run, Pallas kernels for 26% -> 30%
where the time goes in v3:
time: 573 us; the launch traced here: 566 us
  Pallas kernels  199 us (35%)
  waiting for transfers between devices  183 us (32%)
  starting transfers between devices  99.6 us (17%)
  other arithmetic  54.6 us (10%)
  local copies, waits for them, and re-layouts  27 us (5%)
    pallas_call x21, Pallas kernels, call(): pl.pallas_call(kernel, in_specs=[spec for _, spec in ins], out_specs=[spe...  199 us
    ppermute x33, waiting for transfers between devices, pass_on(): lax.ppermute(values, 'mp', [(i, (i + way) % count) for i in range(count)])  124 us
    ppermute x33, starting transfers between devices, pass_on(): lax.ppermute(values, 'mp', [(i, (i + way) % count) for i in range(count)])  55.7 us
    ppermute x49, waiting for transfers between devices, swap(): return lax.ppermute(values, 'dp', [(i, i ^ bit) for i in range(count)])  44.2 us
    ppermute x49, starting transfers between devices, swap(): return lax.ppermute(values, 'dp', [(i, i ^ bit) for i in range(count)])  42.7 us
    convert_element_type x15, other arithmetic, added(): return total.astype(BF16)  34.6 us
    ppermute x2, waiting for transfers between devices, swap_owner(): return lax.ppermute(values, 'mp', [(i, i ^ bit) for i in range(count)])  15.3 us
  transfers between devices with their start and end apart: 84, of which 28 were waited for; matrix products, arithmetic and copies ran while one was open for 9% of the time, Pallas kernels for 30%

profile of v3, /device:TPU:0, one launch (start us, length us, event | category | flops | bytes accessed | tf_op | source)
XLA Modules:
  0.0 565.7 jit_solution(14061381680782484448)
XLA Ops:
  22.7 16.1 %collective-permute-done.1 = bf16[2,128,768]{2,1,0:T(8,128)(2,1)} collective-permute-done((bf16[2,128,768]{2,1,0:T(8,128)(2,1)}, bf16[2,128,768]{2,1,0:T(8,128)(2,1)}, u32[]{:S(2)}, u32[]{:S(2)}) %collective-permute-start.1) | collective-permute-done | bytes 393248 | tf_op jit(solution)/shard_map/ppermute | solution.py:35
  40.7 8.8 %collective-permute-start.5 = (bf16[2,144,768]{2,1,0:T(8,128)(2,1)}, bf16[2,144,768]{2,1,0:T(8,128)(2,1)}, u32[]{:S(2)}, u32[]{:S(2)}) collective-permute-start(bf16[2,144,768]{2,1,0:T(8,128)(2,1)} %get-tuple-element.373), channel_id=1, source_target_pairs={{0,1},{1,2},{2,3},{3,0},{4,5},{5,6},{6,7},{7,4},{8,9},{9,10},{10,1... | collective-permute-start | bytes 1327112 | tf_op jit(solution)/shard_map/ppermute | solution.py:35
  62.1 9.4 %collective-permute-done.6 = bf16[2,144,768]{2,1,0:T(8,128)(2,1)} collective-permute-done((bf16[2,144,768]{2,1,0:T(8,128)(2,1)}, bf16[2,144,768]{2,1,0:T(8,128)(2,1)}, u32[]{:S(2)}, u32[]{:S(2)}) %collective-permute-start.6) | collective-permute-done | bytes 442400 | tf_op jit(solution)/shard_map/ppermute | solution.py:35
  71.6 8.8 %collective-permute-done.7.refs_1_ = bf16[8,40,768]{2,1,0:T(8,128)(2,1)} collective-permute-done((bf16[8,40,768]{2,1,0:T(8,128)(2,1)S(1)}, bf16[8,40,768]{2,1,0:T(8,128)(2,1)}, u32[]{:S(2)}, u32[]{:S(2)}) %collective-permute-start.7) | collective-permute-done | bytes 491552 | tf_op jit(solution)/shard_map/ppermute | solution.py:35
  87.4 25.0 %collective-permute-done.11 = bf16[2,96,768]{2,1,0:T(8,128)(2,1)} collective-permute-done((bf16[2,96,768]{2,1,0:T(8,128)(2,1)S(1)}, bf16[2,96,768]{2,1,0:T(8,128)(2,1)}, u32[]{:S(2)}, u32[]{:S(2)}) %collective-permute-start.11) | collective-permute-done | bytes 294944 | tf_op jit(solution)/shard_map/ppermute | solution.py:35
  122.0 15.0 %collective-permute-done.16 = bf16[2,96,768]{2,1,0:T(8,128)(2,1)S(1)} collective-permute-done((bf16[2,96,768]{2,1,0:T(8,128)(2,1)S(1)}, bf16[2,96,768]{2,1,0:T(8,128)(2,1)S(1)}, u32[]{:S(2)}, u32[]{:S(2)}) %collective-permute-start.16) | collective-permute-done | bytes 294944 | tf_op jit(solution)/shard_map/ppermute | solution.py:35
  149.5 11.4 %shard_map.264 = (f32[320,768]{1,0:T(8,128)}, bf16[320,768]{1,0:T(8,128)(2,1)}, f32[320,768]{1,0:T(8,128)}, bf16[320,768]{1,0:T(8,128)(2,1)}, bf16[320,768]{1,0:...) custom-call(s32[2]{0:T(128)} %pad_add_fusion.place, ...), custom_call_target="tpu_custom_call" | custom-call | tf_op jit(solution)/shard_map/pallas_call | solution.py:735
  166.3 7.4 %collective-permute-done.20 = bf16[2,3,144,768]{3,2,1,0:T(8,128)(2,1)} collective-permute-done((bf16[2,3,144,768]{3,2,1,0:T(8,128)(2,1)}, bf16[2,3,144,768]{3,2,1,0:T(8,128)(2,1)}, u32[]{:S(2)}, u32[]{:S(2)}) %collective-permute-start.20) | collective-permute-done | bytes 1327136 | tf_op jit(solution)/shard_map/ppermute | solution.py:30
  183.1 13.0 %shard_map.265 = (bf16[1280,768]{1,0:T(8,128)(2,1)}, bf16[1280,768]{1,0:T(8,128)(2,1)}, bf16[1280,768]{1,0:T(8,128)(2,1)}, bf16[768,1024]{1,0:T(8,128)(2,1)}) custom-call(s32[2]{0:T(128)} %pad_add_fusion.place, bf16[1280,1024]{1,0:T(8,128)(2,1)} %bitcast.145, bf16[192,1024]{1,0:T(8,128)(2,1)} %bitcast.155, bf16[3,3,192,768]{3,2,1,0:T(8,128)(2,1)} %bitcast.142, ...), custom_call_target="tpu_custom_call" | custom-call | tf_op jit(solution)/shard_map/pallas_call | solution.py:735
  200.6 10.9 %shard_map.266 = (f32[320,768]{1,0:T(8,128)}, bf16[320,768]{1,0:T(8,128)(2,1)}, f32[320,768]{1,0:T(8,128)}, f32[4,320,768]{2,1,0:T(8,128)}, bf16[4,320,768]{2,1,...) custom-call(s32[2]{0:T(128)} %pad_add_fusion.place, f32[320,768]{1,0:T(8,128)} %get-tuple-element.435.rows_ref, ...), custom_call_target="tpu_custom_call" | custom-call | tf_op jit(solution)/shard_map/pallas_call | solution.py:735
  211.4 11.3 %shard_map.267 = (f32[320,768]{1,0:T(8,128)}, bf16[320,768]{1,0:T(8,128)(2,1)}, f32[320,768]{1,0:T(8,128)}, bf16[320,768]{1,0:T(8,128)(2,1)}, bf16[320,768]{1,0:...) custom-call(s32[2]{0:T(128)} %pad_add_fusion.place, ...), custom_call_target="tpu_custom_call" | custom-call | tf_op jit(solution)/shard_map/pallas_call | solution.py:735
  223.6 11.7 %shard_map.268 = (f32[320,768]{1,0:T(8,128)}, bf16[320,768]{1,0:T(8,128)(2,1)}, f32[320,768]{1,0:T(8,128)}, f32[320,768]{1,0:T(8,128)}, bf16[320,768]{1,0:T(8,128)(2,1)}, /*index=5*/bf16[4,768,768]{2,1,0:T(8,128)(2,1)}) custom-call(s32[2]{0:T(128)} %pad_add_fusion.place, f32[320,768]{1,0:T(8,128)} %get-tuple-element.450.rows_ref, ...), custom_call_target="tpu_custom_call" | custom-call | tf_op jit(solution)/shard_map/pallas_call | solution.py:735
  235.3 19.3 %shard_map.269 = (bf16[8,40,768]{2,1,0:T(8,128)(2,1)}, f32[320,768]{1,0:T(8,128)}, f32[8,768]{1,0:T(8,128)}, bf16[2,4,4,96,768]{4,3,2,1,0:T(8,128)(2,1)}, bf16[2,4,4,96,768]{4,3,2,1,0:T(8,128)(2,1)}) custom-call(s32[2]{0:T(128)} %pad_add_fusion.place, s32[8]{0:T(128)} %get-tuple-element.377.picks, f32[320,768]{1,0:T(8,128)} %get-tuple-element.458.rows_ref, ...), custom_call_target="tpu_custom_call" | custom-call | tf_op jit(solution)/shard_map/pallas_call | solution.py:735
  255.6 13.4 %shard_map.270 = (f32[320,768]{1,0:T(8,128)}, f32[8,768]{1,0:T(8,128)}, bf16[1280,768]{1,0:T(8,128)(2,1)}, bf16[1280,768]{1,0:T(8,128)(2,1)}, bf16[320,768]{1,0:T(8,128)(2,1)}, /*index=5*/bf16[320,768]{1,0:T(8,128)(2,1)}) custom-call(s32[2]{0:T(128)} %pad_add_fusion.place, f32[320,768]{1,0:T(8,128)} %get-tuple-element.469.grad, ...), custom_call_target="tpu_custom_call" | custom-call | tf_op jit(solution)/shard_map/pallas_call | solution.py:735
  279.0 13.7 %shard_map.271 = (f32[320,768]{1,0:T(8,128)}, f32[8,768]{1,0:T(8,128)}, bf16[2,4,4,96,768]{4,3,2,1,0:T(8,128)(2,1)}, bf16[2,4,4,96,768]{4,3,2,1,0:T(8,128)(2,1)}) custom-call(s32[2]{0:T(128)} %pad_add_fusion.place, f32[320,768]{1,0:T(8,128)} %get-tuple-element.479.grad, bf16[320,768]{1,0:T(8,128)(2,1)} %get-tuple-element.480.low, ...), custom_call_target="tpu_custom_call" | custom-call | tf_op jit(solution)/shard_map/pallas_call | solution.py:735
  292.7 10.0 %shard_map.272 = (bf16[2,4,4,96,768]{4,3,2,1,0:T(8,128)(2,1)}, bf16[2,4,4,96,768]{4,3,2,1,0:T(8,128)(2,1)}) custom-call(s32[2]{0:T(128)} %pad_add_fusion.place, bf16[320,768]{1,0:T(8,128)(2,1)} %get-tuple-element.473.context, bf16[320,768]{1,0:T(8,128)(2,1)} %get-tuple-element.490.branch, ...), custom_call_target="tpu_custom_call", output_to_operand_aliasing={{0}: (8, {}), {1}: (9, {})} | custom-call | tf_op jit(solution)/shard_map/pallas_call | solution.py:735
  308.9 17.6 %shard_map.273 = (f32[320,768]{1,0:T(8,128)}, f32[8,768]{1,0:T(8,128)}, bf16[2,4,4,96,768]{4,3,2,1,0:T(8,128)(2,1)}, bf16[2,4,4,96,768]{4,3,2,1,0:T(8,128)(2,1)}) custom-call(s32[2]{0:T(128)} %pad_add_fusion.place, f32[320,768]{1,0:T(8,128)} %get-tuple-element.501.grad_in, bf16[320,768]{1,0:T(8,128)(2,1)} %get-tuple-element.502.low_in, ...), custom_call_target="tpu_custom_call" | custom-call | tf_op jit(solution)/shard_map/pallas_call | solution.py:735
  343.5 13.5 %shard_map.274 = (bf16[8,40,768]{2,1,0:T(8,128)(2,1)}, f32[8,768]{1,0:T(8,128)}, bf16[2,4,4,64,768]{4,3,2,1,0:T(8,128)(2,1)}, bf16[2,4,4,64,768]{4,3,2,1,0:T(8,128)(2,1)}) custom-call(s32[2]{0:T(128)} %pad_add_fusion.place, f32[320,768]{1,0:T(8,128)} %get-tuple-element.521.grad, bf16[320,768]{1,0:T(8,128)(2,1)} %get-tuple-element.522.low, ...), custom_call_target="tpu_custom_call" | custom-call | tf_op jit(solution)/shard_map/pallas_call | solution.py:735
  376.9 18.2 %shard_map.276 = (f32[145,8,1024]{2,1,0:T(8,128)}, f32[8,768]{1,0:T(8,128)}, bf16[2,4,4,64,768]{4,3,2,1,0:T(8,128)(2,1)}, bf16[2,4,4,64,768]{4,3,2,1,0:T(8,128)(2,1)}) custom-call(s32[2]{0:T(128)} %pad_add_fusion.place, bf16[1280,1024]{1,0:T(8,128)(2,1)} %bitcast.146, ...), custom_call_target="tpu_custom_call", output_to_operand_aliasing={{2}: (6, {}), {3}: (7, {})} | custom-call | tf_op jit(solution)/shard_map/pallas_call | solution.py:735
  396.4 9.1 %collective-permute-done.48.two0 = bf16[4,96,768]{2,1,0:T(8,128)(2,1)S(1)} collective-permute-done((bf16[4,96,768]{2,1,0:T(8,128)(2,1)}, bf16[4,96,768]{2,1,0:T(8,128)(2,1)S(1)}, u32[]{:S(2)}, u32[]{:S(2)}) %collective-permute-start.48) | collective-permute-done | bytes 589856 | tf_op jit(solution)/shard_map/ppermute | solution.py:30
  421.0 11.6 %collective-permute-done.53 = bf16[2,96,768]{2,1,0:T(8,128)(2,1)S(1)} collective-permute-done((bf16[2,96,768]{2,1,0:T(8,128)(2,1)}, bf16[2,96,768]{2,1,0:T(8,128)(2,1)S(1)}, u32[]{:S(2)}, u32[]{:S(2)}) %collective-permute-start.53) | collective-permute-done | bytes 294944 | tf_op jit(solution)/shard_map/ppermute | solution.py:35
  480.3 9.5 %collective-permute-done.63 = bf16[192,768]{1,0:T(8,128)(2,1)S(1)} collective-permute-done((bf16[192,768]{1,0:T(8,128)(2,1)S(1)}, bf16[192,768]{1,0:T(8,128)(2,1)S(1)}, u32[]{:S(2)}, u32[]{:S(2)}) %collective-permute-start.63) | collective-permute-done | bytes 294944 | tf_op jit(solution)/shard_map/ppermute | solution.py:30
  500.7 11.0 %collective-permute-done.71 = f32[48,768]{1,0:T(8,128)S(1)} collective-permute-done((f32[48,768]{1,0:T(8,128)S(1)}, f32[48,768]{1,0:T(8,128)S(1)}, u32[]{:S(2)}, u32[]{:S(2)}) %collective-permute-start.71) | collective-permute-done | bytes 147488 | tf_op jit(solution)/shard_map/ppermute | solution.py:30
  523.8 15.3 %collective-permute-done.79 = f32[48,768]{1,0:T(8,128)S(1)} collective-permute-done((f32[48,768]{1,0:T(8,128)S(1)}, f32[48,768]{1,0:T(8,128)S(1)}, u32[]{:S(2)}, u32[]{:S(2)}) %collective-permute-start.79) | collective-permute-done | bytes 147488 | tf_op jit(solution)/shard_map/ppermute | solution.py:40
  (401 shorter events, 252.4 us)
Async XLA Ops:
  10.4 28.4 %collective-permute-start.1 = (bf16[2,128,768]{2,1,0:T(8,128)(2,1)}, bf16[2,128,768]{2,1,0:T(8,128)(2,1)}, u32[]{:S(2)}, u32[]{:S(2)}) collective-permute-start(bf16[2,128,768]{2,1,0:T(8,128)(2,1)} %get-tuple-element.374), channel_id=1, source_target_pairs={{0,2},{1,3},{2,0},{3,1},{4,6},{5,7},{6,4},{7,5},{8,10},{9,11},{10,... | collective-permute-start | bytes 1179656 | tf_op jit(solution)/shard_map/ppermute | solution.py:35
  51.7 28.6 %collective-permute-start.4 = (bf16[3,112,768]{2,1,0:T(8,128)(2,1)S(1)}, bf16[3,112,768]{2,1,0:T(8,128)(2,1)S(1)}, u32[]{:S(2)}, u32[]{:S(2)}) collective-permute-start(bf16[3,112,768]{2,1,0:T(8,128)(2,1)S(1)} %pad_maximum_fusion.17), channel_id=1, source_target_pairs={{0,16},{4,20},{8,24},{12,28},{16,0},{20,4},{24,8},{28,12},{1,17},{... | collective-permute-start | bytes 1548296 | tf_op jit(solution)/shard_map/ppermute | solution.py:30
  53.4 27.0 %collective-permute-start.3 = (bf16[3,112,768]{2,1,0:T(8,128)(2,1)S(1)}, bf16[3,112,768]{2,1,0:T(8,128)(2,1)S(1)}, u32[]{:S(2)}, u32[]{:S(2)}) collective-permute-start(bf16[3,112,768]{2,1,0:T(8,128)(2,1)S(1)} %pad_maximum_fusion.16), channel_id=1, source_target_pairs={{0,8},{4,12},{8,0},{12,4},{16,24},{20,28},{24,16},{28,20},{1,9},{5... | collective-permute-start | bytes 1548296 | tf_op jit(solution)/shard_map/ppermute | solution.py:30
  80.5 32.0 %collective-permute-start.9 = (bf16[2,3,112,768]{3,2,1,0:T(8,128)(2,1)S(1)}, bf16[2,3,112,768]{3,2,1,0:T(8,128)(2,1)S(1)}, u32[]{:S(2)}, u32[]{:S(2)}) collective-permute-start(bf16[2,3,112,768]{3,2,1,0:T(8,128)(2,1)S(1)} %pad_maximum_fusion.9), channel_id=1, source_target_pairs={{0,8},{4,12},{8,0},{12,4},{16,24},{20,28},{24,16},{28,20},{1,9},{5... | collective-permute-start | bytes 3096584 | tf_op jit(solution)/shard_map/ppermute | solution.py:30
  82.1 31.2 %collective-permute-start.8 = (bf16[2,3,112,768]{3,2,1,0:T(8,128)(2,1)S(1)}, bf16[2,3,112,768]{3,2,1,0:T(8,128)(2,1)S(1)}, u32[]{:S(2)}, u32[]{:S(2)}) collective-permute-start(bf16[2,3,112,768]{3,2,1,0:T(8,128)(2,1)S(1)} %pad_maximum_fusion.8), channel_id=1, source_target_pairs={{0,16},{4,20},{8,24},{12,28},{16,0},{20,4},{24,8},{28,12},{1,17},{... | collective-permute-start | bytes 3096584 | tf_op jit(solution)/shard_map/ppermute | solution.py:30
  83.8 28.7 %collective-permute-start.12 = (bf16[8,40,768]{2,1,0:T(8,128)(2,1)S(1)}, bf16[8,40,768]{2,1,0:T(8,128)(2,1)S(1)}, u32[]{:S(2)}, u32[]{:S(2)}) collective-permute-start(bf16[8,40,768]{2,1,0:T(8,128)(2,1)S(1)} %copy-done.28), channel_id=1, source_target_pairs={{0,3},{1,0},{2,1},{3,2},{4,7},{5,4},{6,5},{7,6},{8,11},{9,8},{10,9... | collective-permute-start | bytes 1474568 | tf_op jit(solution)/shard_map/ppermute | solution.py:35
  85.5 27.0 %collective-permute-start.10 = (bf16[2,144,768]{2,1,0:T(8,128)(2,1)}, bf16[2,144,768]{2,1,0:T(8,128)(2,1)S(1)}, u32[]{:S(2)}, u32[]{:S(2)}) collective-permute-start(bf16[2,144,768]{2,1,0:T(8,128)(2,1)} %collective-permute-done.5), channel_id=1, source_target_pairs={{0,1},{1,2},{2,3},{3,0},{4,5},{5,6},{6,7},{7,4},{8,9},{9,10},{10,1... | collective-permute-start | bytes 1327112 | tf_op jit(solution)/shard_map/ppermute | solution.py:35
  85.8 26.7 %collective-permute-start.11 = (bf16[2,96,768]{2,1,0:T(8,128)(2,1)S(1)}, bf16[2,96,768]{2,1,0:T(8,128)(2,1)}, u32[]{:S(2)}, u32[]{:S(2)}) collective-permute-start(bf16[2,96,768]{2,1,0:T(8,128)(2,1)S(1)} %copy-done.52), channel_id=1, source_target_pairs={{0,1},{1,2},{2,3},{3,0},{4,5},{5,6},{6,7},{7,4},{8,9},{9,10},{10,1... | collective-permute-start | bytes 884744 | tf_op jit(solution)/shard_map/ppermute | solution.py:35
  141.8 33.2 %collective-permute-start.21 = (bf16[2,2,3,144,768]{4,3,2,1,0:T(8,128)(2,1)S(1)}, bf16[2,2,3,144,768]{4,3,2,1,0:T(8,128)(2,1)}, u32[]{:S(2)}, u32[]{:S(2)}) collective-permute-start(bf16[2,2,3,144,768]{4,3,2,1,0:T(8,128)(2,1)S(1)} %pad_maximum_fusion.2.refs_0_.refs_3_), channel_id=1, source_target_pairs={{0,4},{4,0},{8,12},{12,8},{16,20},{20,16},{24,28},{28,24},{1,5},{5... | collective-permute-start | bytes 7962632 | tf_op jit(solution)/shard_map/ppermute | solution.py:30
  141.9 31.9 %collective-permute-start.20 = (bf16[2,3,144,768]{3,2,1,0:T(8,128)(2,1)}, bf16[2,3,144,768]{3,2,1,0:T(8,128)(2,1)}, u32[]{:S(2)}, u32[]{:S(2)}) collective-permute-start(bf16[2,3,144,768]{3,2,1,0:T(8,128)(2,1)} %get-tuple-element.739), channel_id=1, source_target_pairs={{0,8},{4,12},{8,0},{12,4},{16,24},{20,28},{24,16},{28,20},{1,9},{5... | collective-permute-start | bytes 3981320 | tf_op jit(solution)/shard_map/ppermute | solution.py:30
  143.4 31.5 %collective-permute-start.19 = (bf16[2,3,144,768]{3,2,1,0:T(8,128)(2,1)}, bf16[2,3,144,768]{3,2,1,0:T(8,128)(2,1)}, u32[]{:S(2)}, u32[]{:S(2)}) collective-permute-start(bf16[2,3,144,768]{3,2,1,0:T(8,128)(2,1)} %get-tuple-element.737), channel_id=1, source_target_pairs={{0,16},{4,20},{8,24},{12,28},{16,0},{20,4},{24,8},{28,12},{1,17},{... | collective-permute-start | bytes 3981320 | tf_op jit(solution)/shard_map/ppermute | solution.py:30
  274.8 27.9 %collective-permute-start.33 = (bf16[2,4,96,768]{3,2,1,0:T(8,128)(2,1)}, bf16[2,4,96,768]{3,2,1,0:T(8,128)(2,1)S(1)}, u32[]{:S(2)}, u32[]{:S(2)}) collective-permute-start(bf16[2,4,96,768]{3,2,1,0:T(8,128)(2,1)} %get-tuple-element.731), channel_id=1, source_target_pairs={{0,16},{4,20},{8,24},{12,28},{16,0},{20,4},{24,8},{28,12},{1,17},{... | collective-permute-start | bytes 3538952 | tf_op jit(solution)/shard_map/ppermute | solution.py:30
  276.4 27.4 %collective-permute-start.34 = (bf16[2,4,96,768]{3,2,1,0:T(8,128)(2,1)S(1)}, bf16[2,4,96,768]{3,2,1,0:T(8,128)(2,1)S(1)}, u32[]{:S(2)}, u32[]{:S(2)}) collective-permute-start(bf16[2,4,96,768]{3,2,1,0:T(8,128)(2,1)S(1)} %get-tuple-element.730), channel_id=1, source_target_pairs={{0,8},{4,12},{8,0},{12,4},{16,24},{20,28},{24,16},{28,20},{1,9},{5... | collective-permute-start | bytes 3538952 | tf_op jit(solution)/shard_map/ppermute | solution.py:30
  326.6 33.4 %collective-permute-start.40 = (bf16[2,4,4,96,768]{4,3,2,1,0:T(8,128)(2,1)}, bf16[2,4,4,96,768]{4,3,2,1,0:T(8,128)(2,1)}, u32[]{:S(2)}, u32[]{:S(2)}) collective-permute-start(bf16[2,4,4,96,768]{4,3,2,1,0:T(8,128)(2,1)} %get-tuple-element.530), channel_id=1, source_target_pairs={{0,4},{4,0},{8,12},{12,8},{16,20},{20,16},{24,28},{28,24},{1,5},{5... | collective-permute-start | bytes 14155784 | tf_op jit(solution)/shard_map/ppermute | solution.py:30
  331.2 28.2 %collective-permute-start.43 = (bf16[2,4,96,768]{3,2,1,0:T(8,128)(2,1)}, bf16[2,4,96,768]{3,2,1,0:T(8,128)(2,1)S(1)}, u32[]{:S(2)}, u32[]{:S(2)}) collective-permute-start(bf16[2,4,96,768]{3,2,1,0:T(8,128)(2,1)} %get-tuple-element.727), channel_id=1, source_target_pairs={{0,16},{4,20},{8,24},{12,28},{16,0},{20,4},{24,8},{28,12},{1,17},{... | collective-permute-start | bytes 3538952 | tf_op jit(solution)/shard_map/ppermute | solution.py:30
  332.4 27.6 %collective-permute-start.44 = (bf16[2,4,96,768]{3,2,1,0:T(8,128)(2,1)S(1)}, bf16[2,4,96,768]{3,2,1,0:T(8,128)(2,1)S(1)}, u32[]{:S(2)}, u32[]{:S(2)}) collective-permute-start(bf16[2,4,96,768]{3,2,1,0:T(8,128)(2,1)S(1)} %get-tuple-element.726), channel_id=1, source_target_pairs={{0,8},{4,12},{8,0},{12,4},{16,24},{20,28},{24,16},{28,20},{1,9},{5... | collective-permute-start | bytes 3538952 | tf_op jit(solution)/shard_map/ppermute | solution.py:30
  364.9 40.6 %collective-permute-start.45 = (bf16[2,4,96,768]{3,2,1,0:T(8,128)(2,1)}, bf16[2,4,96,768]{3,2,1,0:T(8,128)(2,1)S(1)}, u32[]{:S(2)}, u32[]{:S(2)}) collective-permute-start(bf16[2,4,96,768]{3,2,1,0:T(8,128)(2,1)} %get-tuple-element.725), channel_id=1, source_target_pairs={{0,16},{4,20},{8,24},{12,28},{16,0},{20,4},{24,8},{28,12},{1,17},{... | collective-permute-start | bytes 3538952 | tf_op jit(solution)/shard_map/ppermute | solution.py:30
  365.8 39.7 %collective-permute-start.46 = (bf16[2,4,96,768]{3,2,1,0:T(8,128)(2,1)}, bf16[2,4,96,768]{3,2,1,0:T(8,128)(2,1)}, u32[]{:S(2)}, u32[]{:S(2)}) collective-permute-start(bf16[2,4,96,768]{3,2,1,0:T(8,128)(2,1)} %get-tuple-element.724), channel_id=1, source_target_pairs={{0,8},{4,12},{8,0},{12,4},{16,24},{20,28},{24,16},{28,20},{1,9},{5... | collective-permute-start | bytes 3538952 | tf_op jit(solution)/shard_map/ppermute | solution.py:30
  370.3 35.2 %collective-permute-start.48 = (bf16[4,96,768]{2,1,0:T(8,128)(2,1)}, bf16[4,96,768]{2,1,0:T(8,128)(2,1)S(1)}, u32[]{:S(2)}, u32[]{:S(2)}) collective-permute-start(bf16[4,96,768]{2,1,0:T(8,128)(2,1)} %get-tuple-element.723), channel_id=1, source_target_pairs={{0,8},{4,12},{8,0},{12,4},{16,24},{20,28},{24,16},{28,20},{1,9},{5... | collective-permute-start | bytes 1769480 | tf_op jit(solution)/shard_map/ppermute | solution.py:30
  371.0 34.6 %collective-permute-start.49 = (bf16[4,96,768]{2,1,0:T(8,128)(2,1)}, bf16[4,96,768]{2,1,0:T(8,128)(2,1)S(1)}, u32[]{:S(2)}, u32[]{:S(2)}) collective-permute-start(bf16[4,96,768]{2,1,0:T(8,128)(2,1)} %get-tuple-element.722), channel_id=1, source_target_pairs={{0,16},{4,20},{8,24},{12,28},{16,0},{20,4},{24,8},{28,12},{1,17},{... | collective-permute-start | bytes 1769480 | tf_op jit(solution)/shard_map/ppermute | solution.py:30
  405.6 27.1 %collective-permute-start.54 = (bf16[2,4,4,64,768]{4,3,2,1,0:T(8,128)(2,1)}, bf16[2,4,4,64,768]{4,3,2,1,0:T(8,128)(2,1)}, u32[]{:S(2)}, u32[]{:S(2)}) collective-permute-start(bf16[2,4,4,64,768]{4,3,2,1,0:T(8,128)(2,1)} %get-tuple-element.597), channel_id=1, source_target_pairs={{0,4},{4,0},{8,12},{12,8},{16,20},{20,16},{24,28},{28,24},{1,5},{5... | collective-permute-start | bytes 9437192 | tf_op jit(solution)/shard_map/ppermute | solution.py:30
  435.9 27.7 %collective-permute-start.59 = (bf16[2,4,64,768]{3,2,1,0:T(8,128)(2,1)}, bf16[2,4,64,768]{3,2,1,0:T(8,128)(2,1)S(1)}, u32[]{:S(2)}, u32[]{:S(2)}) collective-permute-start(bf16[2,4,64,768]{3,2,1,0:T(8,128)(2,1)} %get-tuple-element.735), channel_id=1, source_target_pairs={{0,16},{4,20},{8,24},{12,28},{16,0},{20,4},{24,8},{28,12},{1,17},{... | collective-permute-start | bytes 2359304 | tf_op jit(solution)/shard_map/ppermute | solution.py:30
  437.1 26.5 %collective-permute-start.60 = (bf16[2,4,64,768]{3,2,1,0:T(8,128)(2,1)}, bf16[2,4,64,768]{3,2,1,0:T(8,128)(2,1)}, u32[]{:S(2)}, u32[]{:S(2)}) collective-permute-start(bf16[2,4,64,768]{3,2,1,0:T(8,128)(2,1)} %get-tuple-element.734), channel_id=1, source_target_pairs={{0,8},{4,12},{8,0},{12,4},{16,24},{20,28},{24,16},{28,20},{1,9},{5... | collective-permute-start | bytes 2359304 | tf_op jit(solution)/shard_map/ppermute | solution.py:30
  492.6 27.2 %collective-permute-start.70 = (bf16[2,192,768]{2,1,0:T(8,128)(2,1)S(1)}, bf16[2,192,768]{2,1,0:T(8,128)(2,1)S(1)}, u32[]{:S(2)}, u32[]{:S(2)}) collective-permute-start(bf16[2,192,768]{2,1,0:T(8,128)(2,1)S(1)} %pad_maximum_fusion.15), channel_id=1, source_target_pairs={{0,8},{4,12},{8,0},{12,4},{16,24},{20,28},{24,16},{28,20},{1,9},{5... | collective-permute-start | bytes 1769480 | tf_op jit(solution)/shard_map/ppermute | solution.py:30
  (115 other events, 1557.1 us)

commit v4 on v3

--- a/solution.py
+++ b/solution.py
@@ -319,17 +319,28 @@
         target[row] = values[row * seq : (row + 1) * seq].astype(target.dtype)
 
 
-def slice_kernel(place, biases, inward, outward, feed_in, feed_out, image, first, second, third, sems):
+def slice_kernel(
+    place, head_bias, unit_bias, patch_bias, inward, outward, feed_in, feed_out, image, first, second, third, sems,
+):
     slot = place[0]
     quarter, width = inward.shape[2:]
     span = 4 * quarter // SLICES
     count = quarter // span
     rows = span // 2
     feed_rows = feed_in.shape[1] // SLICES
-    bias_rows = biases.shape[1]
-    image_rows = first.shape[1] - 2 * rows - bias_rows
+    image_rows = first.shape[1] - 2 * rows - 16
     weights = first.at[:, pl.ds(0, 2 * rows + image_rows)]
-    first[:, 2 * rows + image_rows :] = biases[...]
+    table = jnp.concatenate(
+        [
+            head_bias[...].astype(F32),
+            jnp.zeros((head_bias.shape[0], width - quarter), F32),
+        ],
+        axis=1,
+    )
+    patch = jnp.concatenate([patch_bias[...].astype(F32), jnp.zeros((1, width - quarter), F32)], axis=1)
+    table = jnp.concatenate([table, unit_bias[...].astype(F32), patch, jnp.zeros((7, width), F32)], axis=0)
+    first[0, 2 * rows + image_rows :] = table.astype(BF16)
+    first[1, 2 * rows + image_rows :] = jnp.zeros((16, width), BF16)
 
     def attention(layer, target, offset, sem):
         for half in range(2):
@@ -361,21 +372,10 @@
         finish(target, sems.at[number])
 
 
-def self_forward_kernel(
-    layer, norm, offset, n_parts, n_pieces, place, picks, *refs,
+def self_forward(
+    layer, norm, stream, bias, params, code_col, code_row, out, low, pre, query, keys, value, context, kept, whole, sems,
+    out_sem,
 ):
-    parts, (inward, outward), refs = refs[:n_parts], refs[n_parts : n_parts + 2], refs[n_parts + 2 :]
-    pieces, refs = refs[:n_pieces], refs[n_pieces:]
-    bias, params, code_col, code_row, out, low, pre, query, keys, value, context, kept, whole, sems, out_sem, *held = refs
-    if held:
-        pick_copies(picks, parts, held[0], held[2])
-    load_attention(place, (inward, outward), pieces, offset, layer, whole, sems)
-    if held:
-        finish(held[0], held[2])
-        flat_rows(held[0], held[1])
-        stream = held[1][...]
-    else:
-        stream = parts[0][...]
     hb = stream.astype(BF16)
     low[...] = hb
     finish(whole.at[0], sems.at[0])
@@ -395,6 +395,43 @@
     finish(whole, out_sem)
 
 
+def self_forward_kernel(
+    layer, norm, offset, n_parts, n_pieces, place, picks, *refs,
+):
+    parts, (inward, outward), refs = refs[:n_parts], refs[n_parts : n_parts + 2], refs[n_parts + 2 :]
+    pieces, refs = refs[:n_pieces], refs[n_pieces:]
+    held = refs[15:]
+    if held:
+        pick_copies(picks, parts, held[0], held[2])
+    load_attention(place, (inward, outward), pieces, offset, layer, refs[12], refs[13])
+    if held:
+        finish(held[0], held[2])
+        flat_rows(held[0], held[1])
+        stream = held[1][...]
+    else:
+        stream = parts[0][...]
+    self_forward(layer, norm, stream, *refs[:15])
+
+
+def feed_self_forward_kernel(
+    layer, norm, offset, next_layer, next_norm, next_offset, n_pieces, n_next, place, rows_ref, first_weight, second_weight,
+    inward, outward, *refs,
+):
+    pieces, following, refs = refs[:n_pieces], refs[n_pieces : n_pieces + n_next], refs[n_pieces + n_next :]
+    bias, params, code_col, code_row = refs[:4]
+    feed_outs, self_outs, scratch = refs[4:10], refs[10:18], refs[18:]
+    whole, slope, active, sems, out_sem, square, square_sems, square_out = scratch
+    feed_refs = (bias, params, *feed_outs, whole, slope, active, sems, out_sem)
+    for step in range(whole.shape[1]):
+        for half in range(2):
+            load_feed(place, (first_weight, second_weight), pieces, offset, layer, half, step, whole, sems)
+    load_attention(place, (inward, outward), following, next_offset, next_layer, square, square_sems)
+    feed_forward(layer, norm, place, rows_ref, *feed_refs)
+    self_forward(
+        next_layer, next_norm, feed_outs[0][...], bias, params, code_col, code_row, *self_outs, square, square_sems, square_out
+    )
+
+
 def load_kept(kept, whole, sems, order):
     for mat in order:
         start(kept.at[mat], whole.at[mat], sems.at[mat])
@@ -433,15 +470,10 @@
     finish(grads, out_sem)
 
 
-def feed_forward_kernel(
-    layer, norm, offset, n_pieces, place, rows_ref, first_weight, second_weight, *refs,
+def feed_forward(
+    layer, norm, place, rows_ref, bias, params, out, low, pre, slope_out, active_out, kept, whole, slope, active, sems, out_sem,
 ):
-    pieces, refs = refs[:n_pieces], refs[n_pieces:]
-    bias, params, out, low, pre, slope_out, active_out, kept, whole, slope, active, sems, out_sem = refs
     parts = whole.shape[1]
-    for step in range(parts):
-        for half in range(2):
-            load_feed(place, (first_weight, second_weight), pieces, offset, layer, half, step, whole, sems)
     stream = rows_ref[...]
     hb = stream.astype(BF16)
     low[...] = hb
@@ -952,16 +984,15 @@
     code_col = code.reshape(n_tokens, 1)
     code_row = code.reshape(own_rows // 2, 2 * seq)
 
-    flat = jnp.concatenate([query_value_bias.reshape(-1), feed_bias.reshape(-1), image_bias])
-    bias_rows = -(-flat.shape[0] // (32 * width)) * 16
-    biases = jnp.pad(flat, (0, 2 * bias_rows * width - flat.shape[0])).reshape(2, bias_rows, width)
     first_rows = 2 * attention_rows + image_rows
     first, second, third = call(
         slice_kernel,
-        [(place, SMEM), (biases, VMEM)] + [(v, ANY) for v in (inward, attention_out, feed_in, feed_out, image)],
+        [(place, SMEM)]
+        + [(v, VMEM) for v in (query_value_bias.reshape(6, quarter), feed_bias, image_bias.reshape(1, quarter))]
+        + [(v, ANY) for v in (inward, attention_out, feed_in, feed_out, image)],
         [
             (shape((2, rows, width), BF16), VMEM)
-            for rows in (first_rows + bias_rows, feed_rows + attention_rows, feed_rows)
+            for rows in (first_rows + 16, feed_rows + attention_rows, feed_rows)
         ],
         [dma((3,))],
     )
@@ -987,15 +1018,13 @@
     rings["first"].direct()
     step()
 
-    parts = [part[:, first_rows:].reshape(-1) for part in at["first"].values()]
+    parts = [part[0, first_rows:] for part in at["first"].values()]
     ordered = jnp.stack(parts)[(owner - jnp.arange(mp)) % mp].astype(F32)
-    cut0 = query_value_bias.size
-    cut1 = cut0 + feed_bias.size
     bias = jnp.concatenate(
         [
-            ordered[:, :cut0].reshape(mp, -1, quarter).transpose(1, 0, 2).reshape(-1, width),
-            ordered[:, cut0:cut1].reshape(mp, 2, units).transpose(1, 0, 2).reshape(-1, width),
-            ordered[:, cut1 : cut1 + quarter].reshape(1, width),
+            ordered[:, :6, :quarter].transpose(1, 0, 2).reshape(6, width),
+            ordered[:, 6:8].transpose(1, 0, 2).reshape(2 * mp, width),
+            ordered[:, 8, :quarter].reshape(1, width),
         ]
     )
     params = jnp.stack([output_bias, norm_gain, norm_bias], axis=1).astype(F32).reshape(-1, width)
@@ -1005,18 +1034,17 @@
     first_wide.one()
     rings["second"].up()
     rings["second"].down()
-    rings[TOKENS].up()
     step()
     bias, params, code_col, code_row, picks_in, picks_out, image_row, patch_rows = at.pop("tables")
     first_wide.two()
     rings["second"].far()
-    rings[TOKENS].down()
+    rings[TOKENS].up()
     rings["third"].up()
     step()
     second_wide = gathered("second")
     first_wide.core()
     second_wide.one()
-    rings[TOKENS].far()
+    rings[TOKENS].down()
     rings["third"].down()
     step()
 
@@ -1031,7 +1059,7 @@
     def feed_ins(layer):
         return [(feed_in, ANY), (feed_out, ANY)] + [(piece, ANY) for piece in feed_pieces[layer]]
 
-    def self_forward(layer, norm, parts):
+    def first_forward(layer, norm, parts):
         picked = len(parts) > 1
         return call(
             partial(self_forward_kernel, layer, norm, attention_at[layer], len(parts), len(attention_pieces[layer])),
@@ -1056,14 +1084,24 @@
             {len(ins) + i: 2 + i for i in range(len(held))},
         )
 
-    def feed_forward(layer, norm, rows):
-        return call(
-            partial(feed_forward_kernel, layer, norm, feed_at[layer], len(feed_pieces[layer])),
-            [(place, SMEM), (rows, VMEM)] + feed_ins(layer) + [(bias, VMEM), (params, VMEM)],
+    def feed_self_forward(layer, norm, next_layer, next_norm, rows):
+        pieces, following = feed_pieces[layer], attention_pieces[next_layer]
+        outs = call(
+            partial(
+                feed_self_forward_kernel, layer, norm, feed_at[layer], next_layer, next_norm, attention_at[next_layer],
+                len(pieces), len(following),
+            ),
+            [(place, SMEM), (rows, VMEM)]
+            + [(v, ANY) for v in (feed_in, feed_out, inward, attention_out, *pieces, *following)]
+            + [(bias, VMEM), (params, VMEM), (code_col, VMEM), (code_row, VMEM)],
             [(token_shape, VMEM), (token_low, VMEM), (token_shape, VMEM)]
-            + [(inner_shape, ANY), (inner_low, ANY), (kept_wide, ANY)],
-            [wide, inner_f32, inner_bf16, dma((2, mp)), dma],
+            + [(inner_shape, ANY), (inner_low, ANY), (kept_wide, ANY)]
+            + [(token_shape, VMEM), (token_low, VMEM), (token_shape, VMEM)]
+            + [(token_low, VMEM)] * 4
+            + [(kept_square, ANY)],
+            [wide, inner_f32, inner_bf16, dma((2, mp)), dma, square, dma((4,)), dma],
         )
+        return outs[:6], outs[6:]
 
     def feed_backward(norm, grad, kept):
         _, low, pre, slope, active, weights = kept
@@ -1096,16 +1134,8 @@
 
     attention_pieces[0] = attention_pieces[2] = first_wide.take()
     second_wide.two_early()
+    rings[TOKENS].far()
     rings["third"].far()
-    rings[COTANGENT].up()
-    text_attention = self_forward(0, 0, rings[TOKENS].take())
-    at["stream"] = text_attention[0]
-    step()
-
-    second_wide.core_late()
-    third_wide = gathered("third")
-    third_wide.one()
-    rings[COTANGENT].down()
     projected, image_keys, image_value, kept_image = call(
         partial(image_forward_kernel, 2, attention_rows, 2 * attention_rows, image_rows, len(attention_pieces[2])),
         [(place, SMEM), (patch_rows, VMEM), (image, ANY)] + attention_ins(2) + [(bias, VMEM)],
@@ -1115,15 +1145,23 @@
     at["keys"] = image_keys
     step()
 
+    text_attention = first_forward(0, 0, rings[TOKENS].take())
+    at["stream"] = text_attention[0]
+    second_wide.core_late()
+    third_wide = gathered("third")
+    third_wide.one()
+    rings[COTANGENT].up()
+    step()
+
     attention_pieces[1] = feed_pieces[0] = second_wide.take()
     third_wide.two()
+    rings[COTANGENT].down()
+    text_feed, joining_attention = feed_self_forward(0, 1, 1, 2, at.pop("stream"))
+    at["stream"] = joining_attention[0]
+    step()
+
+    third_wide.core()
     rings[COTANGENT].far()
-    text_feed = feed_forward(0, 1, at.pop("stream"))
-    joining_attention = self_forward(1, 2, [text_feed[0]])
-    at["stream"] = joining_attention[0]
-    step()
-
-    third_wide.core()
     image_keys = at.pop("keys")
     cross_attention = call(
         partial(cross_forward_kernel, 2, 3, attention_rows, seq, patches, len(attention_pieces[2])),
@@ -1224,7 +1262,6 @@
     middle_grads.combine()
     middle_grads.far()
     back_ring.up()
-    at["mixed"] = pick_rows(mixed_parts)
     step()
 
     text_grads.one()
@@ -1252,6 +1289,7 @@
 
     late = Widen(at, "late", *jnp.concatenate([at.pop("first own"), text_grads.owned()], axis=1))
     late.one()
+    at["mixed"] = pick_rows(mixed_parts)
     early.core()
     back_ring.far()
     at[SMALL] = at[SMALL] + swap_owner(at[SMALL], 1)

time: 573 us -> 562 us (0.981)
  waiting for transfers between devices: 183 us -> 191 us
  starting transfers between devices: 99.6 us -> 92.2 us
    ppermute x33, waiting for transfers between devices: 124 us -> 131 us  [pass_on(): lax.ppermute(values, 'mp', [(i, (i + way) % count) for i in range(count)])]
    ppermute x33, starting transfers between devices: 55.7 us -> 49.6 us  [pass_on(): lax.ppermute(values, 'mp', [(i, (i + way) % count) for i in range(count)])]
    pallas_call x21 -> x20, Pallas kernels: 199 us -> 197 us  [call(): pl.pallas_call(kernel, in_specs=[spec for _, spec in ins], out_specs=[spe...]
  transfers between devices with their start and end apart: 84 -> 84, of which waited for: 28 -> 30; matrix products, arithmetic and copies ran while one was open for 9% -> 8% of each run, Pallas kernels for 30% -> 30%
where the time goes in v4:
time: 562 us; the launch traced here: 555 us
  Pallas kernels  197 us (35%)
  waiting for transfers between devices  191 us (34%)
  starting transfers between devices  92.2 us (16%)
  other arithmetic  50.5 us (9%)
  local copies, waits for them, and re-layouts  22 us (4%)
    pallas_call x20, Pallas kernels, call(): pl.pallas_call(kernel, in_specs=[spec for _, spec in ins], out_specs=[spe...  197 us
    ppermute x33, waiting for transfers between devices, pass_on(): lax.ppermute(values, 'mp', [(i, (i + way) % count) for i in range(count)])  131 us
    ppermute x33, starting transfers between devices, pass_on(): lax.ppermute(values, 'mp', [(i, (i + way) % count) for i in range(count)])  49.6 us
    ppermute x49, waiting for transfers between devices, swap(): return lax.ppermute(values, 'dp', [(i, i ^ bit) for i in range(count)])  47.5 us
    ppermute x49, starting transfers between devices, swap(): return lax.ppermute(values, 'dp', [(i, i ^ bit) for i in range(count)])  41.5 us
    convert_element_type x15, other arithmetic, added(): return total.astype(BF16)  33.7 us
    ppermute x2, waiting for transfers between devices, swap_owner(): return lax.ppermute(values, 'mp', [(i, i ^ bit) for i in range(count)])  12.6 us
  transfers between devices with their start and end apart: 84, of which 30 were waited for; matrix products, arithmetic and copies ran while one was open for 8% of the time, Pallas kernels for 30%

profile of v4, /device:TPU:0, one launch (start us, length us, event | category | flops | bytes accessed | tf_op | source)
XLA Modules:
  0.0 554.8 jit_solution(6040850860027487002)
XLA Ops:
  22.4 16.1 %collective-permute-done.1 = bf16[2,128,768]{2,1,0:T(8,128)(2,1)} collective-permute-done((bf16[2,128,768]{2,1,0:T(8,128)(2,1)}, bf16[2,128,768]{2,1,0:T(8,128)(2,1)}, u32[]{:S(2)}, u32[]{:S(2)}) %collective-permute-start.1) | collective-permute-done | bytes 393248 | tf_op jit(solution)/shard_map/ppermute | solution.py:35
  40.4 8.8 %collective-permute-start.5 = (bf16[2,144,768]{2,1,0:T(8,128)(2,1)}, bf16[2,144,768]{2,1,0:T(8,128)(2,1)S(1)}, u32[]{:S(2)}, u32[]{:S(2)}) collective-permute-start(bf16[2,144,768]{2,1,0:T(8,128)(2,1)} %get-tuple-element.366), channel_id=1, source_target_pairs={{0,1},{1,2},{2,3},{3,0},{4,5},{5,6},{6,7},{7,4},{8,9},{9,10},{10,1... | collective-permute-start | bytes 1327112 | tf_op jit(solution)/shard_map/ppermute | solution.py:35
  61.7 7.7 %collective-permute-done.6 = bf16[2,144,768]{2,1,0:T(8,128)(2,1)S(1)} collective-permute-done((bf16[2,144,768]{2,1,0:T(8,128)(2,1)}, bf16[2,144,768]{2,1,0:T(8,128)(2,1)S(1)}, u32[]{:S(2)}, u32[]{:S(2)}) %collective-permute-start.6) | collective-permute-done | bytes 442400 | tf_op jit(solution)/shard_map/ppermute | solution.py:35
  77.3 25.7 %collective-permute-done.10 = bf16[2,96,768]{2,1,0:T(8,128)(2,1)} collective-permute-done((bf16[2,96,768]{2,1,0:T(8,128)(2,1)S(1)}, bf16[2,96,768]{2,1,0:T(8,128)(2,1)}, u32[]{:S(2)}, u32[]{:S(2)}) %collective-permute-start.10) | collective-permute-done | bytes 294944 | tf_op jit(solution)/shard_map/ppermute | solution.py:35
  106.4 18.5 %collective-permute-done.15 = bf16[2,96,768]{2,1,0:T(8,128)(2,1)S(1)} collective-permute-done((bf16[2,96,768]{2,1,0:T(8,128)(2,1)S(1)}, bf16[2,96,768]{2,1,0:T(8,128)(2,1)S(1)}, u32[]{:S(2)}, u32[]{:S(2)}) %collective-permute-start.15) | collective-permute-done | bytes 294944 | tf_op jit(solution)/shard_map/ppermute | solution.py:35
  132.3 13.0 %shard_map.264 = (bf16[1280,768]{1,0:T(8,128)(2,1)}, bf16[1280,768]{1,0:T(8,128)(2,1)}, bf16[1280,768]{1,0:T(8,128)(2,1)}, bf16[768,1024]{1,0:T(8,128)(2,1)}) custom-call(s32[2]{0:T(128)} %pad_add_fusion.place, bf16[1280,1024]{1,0:T(8,128)(2,1)} %bitcast.145, bf16[192,1024]{1,0:T(8,128)(2,1)} %bitcast.155, bf16[3,3,192,768]{3,2,1,0:T(8,128)(2,1)} %bitcast.141, ...), custom_call_target="tpu_custom_call" | custom-call | tf_op jit(solution)/shard_map/pallas_call | solution.py:767
  145.3 7.7 %collective-permute-done.20 = bf16[2,96,768]{2,1,0:T(8,128)(2,1)} collective-permute-done((bf16[2,96,768]{2,1,0:T(8,128)(2,1)}, bf16[2,96,768]{2,1,0:T(8,128)(2,1)}, u32[]{:S(2)}, u32[]{:S(2)}) %collective-permute-start.20) | collective-permute-done | bytes 294944 | tf_op jit(solution)/shard_map/ppermute | solution.py:35
  153.1 7.3 %collective-permute-done.18 = bf16[2,3,144,768]{3,2,1,0:T(8,128)(2,1)} collective-permute-done((bf16[2,3,144,768]{3,2,1,0:T(8,128)(2,1)S(1)}, bf16[2,3,144,768]{3,2,1,0:T(8,128)(2,1)}, u32[]{:S(2)}, u32[]{:S(2)}) %collective-permute-start.18) | collective-permute-done | bytes 1327136 | tf_op jit(solution)/shard_map/ppermute | solution.py:30
  169.2 11.3 %shard_map.265 = (f32[320,768]{1,0:T(8,128)}, bf16[320,768]{1,0:T(8,128)(2,1)}, f32[320,768]{1,0:T(8,128)}, bf16[320,768]{1,0:T(8,128)(2,1)}, bf16[320,768]{1,0:...) custom-call(s32[2]{0:T(128)} %pad_add_fusion.place, ...), custom_call_target="tpu_custom_call" | custom-call | tf_op jit(solution)/shard_map/pallas_call | solution.py:767
  188.9 20.7 %shard_map.266 = (f32[320,768]{1,0:T(8,128)}, bf16[320,768]{1,0:T(8,128)(2,1)}, f32[320,768]{1,0:T(8,128)}, f32[4,320,768]{2,1,0:T(8,128)}, bf16[4,320,768]{2,1,...) custom-call(s32[2]{0:T(128)} %pad_add_fusion.place, ...), custom_call_target="tpu_custom_call" | custom-call | tf_op jit(solution)/shard_map/pallas_call | solution.py:767
  211.1 11.1 %shard_map.267 = (f32[320,768]{1,0:T(8,128)}, bf16[320,768]{1,0:T(8,128)(2,1)}, f32[320,768]{1,0:T(8,128)}, f32[320,768]{1,0:T(8,128)}, bf16[320,768]{1,0:T(8,128)(2,1)}, /*index=5*/bf16[4,768,768]{2,1,0:T(8,128)(2,1)}) custom-call(s32[2]{0:T(128)} %pad_add_fusion.place, f32[320,768]{1,0:T(8,128)} %get-tuple-element.440.rows_ref, ...), custom_call_target="tpu_custom_call" | custom-call | tf_op jit(solution)/shard_map/pallas_call | solution.py:767
  227.4 19.3 %shard_map.268 = (bf16[8,40,768]{2,1,0:T(8,128)(2,1)}, f32[320,768]{1,0:T(8,128)}, f32[8,768]{1,0:T(8,128)}, bf16[2,4,4,96,768]{4,3,2,1,0:T(8,128)(2,1)}, bf16[2,4,4,96,768]{4,3,2,1,0:T(8,128)(2,1)}) custom-call(s32[2]{0:T(128)} %pad_add_fusion.place, s32[8]{0:T(128)} %get-tuple-element.370.picks, f32[320,768]{1,0:T(8,128)} %get-tuple-element.448.rows_ref, ...), custom_call_target="tpu_custom_call" | custom-call | tf_op jit(solution)/shard_map/pallas_call | solution.py:767
  246.9 13.4 %shard_map.269 = (f32[320,768]{1,0:T(8,128)}, f32[8,768]{1,0:T(8,128)}, bf16[1280,768]{1,0:T(8,128)(2,1)}, bf16[1280,768]{1,0:T(8,128)(2,1)}, bf16[320,768]{1,0:T(8,128)(2,1)}, /*index=5*/bf16[320,768]{1,0:T(8,128)(2,1)}) custom-call(s32[2]{0:T(128)} %pad_add_fusion.place, f32[320,768]{1,0:T(8,128)} %get-tuple-element.459.grad, ...), custom_call_target="tpu_custom_call" | custom-call | tf_op jit(solution)/shard_map/pallas_call | solution.py:767
  270.5 13.6 %shard_map.270 = (f32[320,768]{1,0:T(8,128)}, f32[8,768]{1,0:T(8,128)}, bf16[2,4,4,96,768]{4,3,2,1,0:T(8,128)(2,1)}, bf16[2,4,4,96,768]{4,3,2,1,0:T(8,128)(2,1)}) custom-call(s32[2]{0:T(128)} %pad_add_fusion.place, f32[320,768]{1,0:T(8,128)} %get-tuple-element.469.grad, bf16[320,768]{1,0:T(8,128)(2,1)} %get-tuple-element.470.low, ...), custom_call_target="tpu_custom_call" | custom-call | tf_op jit(solution)/shard_map/pallas_call | solution.py:767
  284.1 9.9 %shard_map.271 = (bf16[2,4,4,96,768]{4,3,2,1,0:T(8,128)(2,1)}, bf16[2,4,4,96,768]{4,3,2,1,0:T(8,128)(2,1)}) custom-call(s32[2]{0:T(128)} %pad_add_fusion.place, bf16[320,768]{1,0:T(8,128)(2,1)} %get-tuple-element.463.context, bf16[320,768]{1,0:T(8,128)(2,1)} %get-tuple-element.480.branch, ...), custom_call_target="tpu_custom_call", output_to_operand_aliasing={{0}: (8, {}), {1}: (9, {})} | custom-call | tf_op jit(solution)/shard_map/pallas_call | solution.py:767
  299.7 17.6 %shard_map.272 = (f32[320,768]{1,0:T(8,128)}, f32[8,768]{1,0:T(8,128)}, bf16[2,4,4,96,768]{4,3,2,1,0:T(8,128)(2,1)}, bf16[2,4,4,96,768]{4,3,2,1,0:T(8,128)(2,1)}) custom-call(s32[2]{0:T(128)} %pad_add_fusion.place, f32[320,768]{1,0:T(8,128)} %get-tuple-element.491.grad_in, bf16[320,768]{1,0:T(8,128)(2,1)} %get-tuple-element.492.low_in, ...), custom_call_target="tpu_custom_call" | custom-call | tf_op jit(solution)/shard_map/pallas_call | solution.py:767
  334.6 13.4 %shard_map.273 = (bf16[8,40,768]{2,1,0:T(8,128)(2,1)}, f32[8,768]{1,0:T(8,128)}, bf16[2,4,4,64,768]{4,3,2,1,0:T(8,128)(2,1)}, bf16[2,4,4,64,768]{4,3,2,1,0:T(8,128)(2,1)}) custom-call(s32[2]{0:T(128)} %pad_add_fusion.place, f32[320,768]{1,0:T(8,128)} %get-tuple-element.511.grad, bf16[320,768]{1,0:T(8,128)(2,1)} %get-tuple-element.512.low, ...), custom_call_target="tpu_custom_call" | custom-call | tf_op jit(solution)/shard_map/pallas_call | solution.py:767
  365.8 18.2 %shard_map.275 = (f32[145,8,1024]{2,1,0:T(8,128)}, f32[8,768]{1,0:T(8,128)}, bf16[2,4,4,64,768]{4,3,2,1,0:T(8,128)(2,1)}, bf16[2,4,4,64,768]{4,3,2,1,0:T(8,128)(2,1)}) custom-call(s32[2]{0:T(128)} %pad_add_fusion.place, bf16[1280,1024]{1,0:T(8,128)(2,1)} %bitcast.146, ...), custom_call_target="tpu_custom_call", output_to_operand_aliasing={{2}: (6, {}), {3}: (7, {})} | custom-call | tf_op jit(solution)/shard_map/pallas_call | solution.py:767
  384.8 12.1 %collective-permute-done.48.two0 = bf16[4,96,768]{2,1,0:T(8,128)(2,1)S(1)} collective-permute-done((bf16[4,96,768]{2,1,0:T(8,128)(2,1)}, bf16[4,96,768]{2,1,0:T(8,128)(2,1)S(1)}, u32[]{:S(2)}, u32[]{:S(2)}) %collective-permute-start.48) | collective-permute-done | bytes 589856 | tf_op jit(solution)/shard_map/ppermute | solution.py:30
  410.1 13.9 %collective-permute-done.53 = bf16[2,96,768]{2,1,0:T(8,128)(2,1)S(1)} collective-permute-done((bf16[2,96,768]{2,1,0:T(8,128)(2,1)}, bf16[2,96,768]{2,1,0:T(8,128)(2,1)S(1)}, u32[]{:S(2)}, u32[]{:S(2)}) %collective-permute-start.53) | collective-permute-done | bytes 294944 | tf_op jit(solution)/shard_map/ppermute | solution.py:35
  470.5 9.6 %collective-permute-done.63 = bf16[192,768]{1,0:T(8,128)(2,1)S(1)} collective-permute-done((bf16[192,768]{1,0:T(8,128)(2,1)S(1)}, bf16[192,768]{1,0:T(8,128)(2,1)S(1)}, u32[]{:S(2)}, u32[]{:S(2)}) %collective-permute-start.63) | collective-permute-done | bytes 294944 | tf_op jit(solution)/shard_map/ppermute | solution.py:30
  491.2 10.8 %collective-permute-done.71 = f32[48,768]{1,0:T(8,128)S(1)} collective-permute-done((f32[48,768]{1,0:T(8,128)S(1)}, f32[48,768]{1,0:T(8,128)S(1)}, u32[]{:S(2)}, u32[]{:S(2)}) %collective-permute-start.71) | collective-permute-done | bytes 147488 | tf_op jit(solution)/shard_map/ppermute | solution.py:30
  517.0 12.6 %collective-permute-done.79 = f32[48,768]{1,0:T(8,128)} collective-permute-done((f32[48,768]{1,0:T(8,128)S(1)}, f32[48,768]{1,0:T(8,128)}, u32[]{:S(2)}, u32[]{:S(2)}) %collective-permute-start.79) | collective-permute-done | bytes 147488 | tf_op jit(solution)/shard_map/ppermute | solution.py:40
  533.5 6.3 %shard_map.281 = (f32[2,768,768]{2,1,0:T(8,128)}, f32[2,768,768]{2,1,0:T(8,128)}, f32[3,3,192,768]{3,2,1,0:T(8,128)}, f32[3,192,768]{2,1,0:T(8,128)}) custom-call(s32[2]{0:T(128)} %pad_add_fusion.place, bf16[2,4,192,768]{3,2,1,0:T(8,128)(2,1)} %copy-done.6, bf16[2,4,192,768]{3,2,1,0:T(8,128)(2,1)} %collective-permute-done.76.refs_1_), custom_call_target="tpu_custom_call" | custom-call | tf_op jit(solution)/shard_map/pallas_call | solution.py:767
  (395 shorter events, 233.7 us)
Async XLA Ops:
  10.1 28.4 %collective-permute-start.1 = (bf16[2,128,768]{2,1,0:T(8,128)(2,1)}, bf16[2,128,768]{2,1,0:T(8,128)(2,1)}, u32[]{:S(2)}, u32[]{:S(2)}) collective-permute-start(bf16[2,128,768]{2,1,0:T(8,128)(2,1)} %get-tuple-element.367), channel_id=1, source_target_pairs={{0,2},{1,3},{2,0},{3,1},{4,6},{5,7},{6,4},{7,5},{8,10},{9,11},{10,... | collective-permute-start | bytes 1179656 | tf_op jit(solution)/shard_map/ppermute | solution.py:35
  12.7 25.9 %collective-permute-start.2 = (bf16[2,128,768]{2,1,0:T(8,128)(2,1)}, bf16[2,128,768]{2,1,0:T(8,128)(2,1)S(1)}, u32[]{:S(2)}, u32[]{:S(2)}) collective-permute-start(bf16[2,128,768]{2,1,0:T(8,128)(2,1)} %get-tuple-element.367), channel_id=1, source_target_pairs={{0,3},{1,0},{2,1},{3,2},{4,7},{5,4},{6,5},{7,6},{8,11},{9,8},{10,9... | collective-permute-start | bytes 1179656 | tf_op jit(solution)/shard_map/ppermute | solution.py:35
  69.5 33.5 %collective-permute-start.8 = (bf16[2,3,112,768]{3,2,1,0:T(8,128)(2,1)S(1)}, bf16[2,3,112,768]{3,2,1,0:T(8,128)(2,1)S(1)}, u32[]{:S(2)}, u32[]{:S(2)}) collective-permute-start(bf16[2,3,112,768]{3,2,1,0:T(8,128)(2,1)S(1)} %pad_maximum_fusion.9), channel_id=1, source_target_pairs={{0,8},{4,12},{8,0},{12,4},{16,24},{20,28},{24,16},{28,20},{1,9},{5... | collective-permute-start | bytes 3096584 | tf_op jit(solution)/shard_map/ppermute | solution.py:30
  71.1 31.9 %collective-permute-start.7 = (bf16[2,3,112,768]{3,2,1,0:T(8,128)(2,1)S(1)}, bf16[2,3,112,768]{3,2,1,0:T(8,128)(2,1)S(1)}, u32[]{:S(2)}, u32[]{:S(2)}) collective-permute-start(bf16[2,3,112,768]{3,2,1,0:T(8,128)(2,1)S(1)} %pad_maximum_fusion.8), channel_id=1, source_target_pairs={{0,16},{4,20},{8,24},{12,28},{16,0},{20,4},{24,8},{28,12},{1,17},{... | collective-permute-start | bytes 3096584 | tf_op jit(solution)/shard_map/ppermute | solution.py:30
  72.7 30.3 %collective-permute-start.11 = (bf16[8,40,768]{2,1,0:T(8,128)(2,1)S(1)}, bf16[8,40,768]{2,1,0:T(8,128)(2,1)}, u32[]{:S(2)}, u32[]{:S(2)}) collective-permute-start(bf16[8,40,768]{2,1,0:T(8,128)(2,1)S(1)} %copy-done.27), channel_id=1, source_target_pairs={{0,1},{1,2},{2,3},{3,0},{4,5},{5,6},{6,7},{7,4},{8,9},{9,10},{10,1... | collective-permute-start | bytes 1474568 | tf_op jit(solution)/shard_map/ppermute | solution.py:35
  73.3 29.7 %collective-permute-start.9 = (bf16[2,144,768]{2,1,0:T(8,128)(2,1)S(1)}, bf16[2,144,768]{2,1,0:T(8,128)(2,1)S(1)}, u32[]{:S(2)}, u32[]{:S(2)}) collective-permute-start(bf16[2,144,768]{2,1,0:T(8,128)(2,1)S(1)} %collective-permute-done.5), channel_id=1, source_target_pairs={{0,1},{1,2},{2,3},{3,0},{4,5},{5,6},{6,7},{7,4},{8,9},{9,10},{10,1... | collective-permute-start | bytes 1327112 | tf_op jit(solution)/shard_map/ppermute | solution.py:35
  73.9 29.1 %collective-permute-start.10 = (bf16[2,96,768]{2,1,0:T(8,128)(2,1)S(1)}, bf16[2,96,768]{2,1,0:T(8,128)(2,1)}, u32[]{:S(2)}, u32[]{:S(2)}) collective-permute-start(bf16[2,96,768]{2,1,0:T(8,128)(2,1)S(1)} %copy-done.52), channel_id=1, source_target_pairs={{0,1},{1,2},{2,3},{3,0},{4,5},{5,6},{6,7},{7,4},{8,9},{9,10},{10,1... | collective-permute-start | bytes 884744 | tf_op jit(solution)/shard_map/ppermute | solution.py:35
  128.7 32.9 %collective-permute-start.19 = (bf16[2,2,3,144,768]{4,3,2,1,0:T(8,128)(2,1)S(1)}, bf16[2,2,3,144,768]{4,3,2,1,0:T(8,128)(2,1)}, u32[]{:S(2)}, u32[]{:S(2)}) collective-permute-start(bf16[2,2,3,144,768]{4,3,2,1,0:T(8,128)(2,1)S(1)} %pad_maximum_fusion.2.refs_0_.refs_4_), channel_id=1, source_target_pairs={{0,4},{4,0},{8,12},{12,8},{16,20},{20,16},{24,28},{28,24},{1,5},{5... | collective-permute-start | bytes 7962632 | tf_op jit(solution)/shard_map/ppermute | solution.py:30
  128.7 31.6 %collective-permute-start.18 = (bf16[2,3,144,768]{3,2,1,0:T(8,128)(2,1)S(1)}, bf16[2,3,144,768]{3,2,1,0:T(8,128)(2,1)}, u32[]{:S(2)}, u32[]{:S(2)}) collective-permute-start(bf16[2,3,144,768]{3,2,1,0:T(8,128)(2,1)S(1)} %get-tuple-element.725), channel_id=1, source_target_pairs={{0,8},{4,12},{8,0},{12,4},{16,24},{20,28},{24,16},{28,20},{1,9},{5... | collective-permute-start | bytes 3981320 | tf_op jit(solution)/shard_map/ppermute | solution.py:30
  130.1 31.5 %collective-permute-start.17 = (bf16[2,3,144,768]{3,2,1,0:T(8,128)(2,1)}, bf16[2,3,144,768]{3,2,1,0:T(8,128)(2,1)}, u32[]{:S(2)}, u32[]{:S(2)}) collective-permute-start(bf16[2,3,144,768]{3,2,1,0:T(8,128)(2,1)} %get-tuple-element.723), channel_id=1, source_target_pairs={{0,16},{4,20},{8,24},{12,28},{16,0},{20,4},{24,8},{28,12},{1,17},{... | collective-permute-start | bytes 3981320 | tf_op jit(solution)/shard_map/ppermute | solution.py:30
  184.0 25.6 %collective-permute-start.28 = (bf16[2,3,96,768]{3,2,1,0:T(8,128)(2,1)S(1)}, bf16[2,3,96,768]{3,2,1,0:T(8,128)(2,1)S(1)}, u32[]{:S(2)}, u32[]{:S(2)}) collective-permute-start(bf16[2,3,96,768]{3,2,1,0:T(8,128)(2,1)S(1)} %pad_maximum_fusion.11), channel_id=1, source_target_pairs={{0,8},{4,12},{8,0},{12,4},{16,24},{20,28},{24,16},{28,20},{1,9},{5... | collective-permute-start | bytes 2654216 | tf_op jit(solution)/shard_map/ppermute | solution.py:30
  266.7 27.7 %collective-permute-start.33 = (bf16[2,4,96,768]{3,2,1,0:T(8,128)(2,1)}, bf16[2,4,96,768]{3,2,1,0:T(8,128)(2,1)S(1)}, u32[]{:S(2)}, u32[]{:S(2)}) collective-permute-start(bf16[2,4,96,768]{3,2,1,0:T(8,128)(2,1)} %get-tuple-element.717), channel_id=1, source_target_pairs={{0,16},{4,20},{8,24},{12,28},{16,0},{20,4},{24,8},{28,12},{1,17},{... | collective-permute-start | bytes 3538952 | tf_op jit(solution)/shard_map/ppermute | solution.py:30
  268.3 27.2 %collective-permute-start.34 = (bf16[2,4,96,768]{3,2,1,0:T(8,128)(2,1)S(1)}, bf16[2,4,96,768]{3,2,1,0:T(8,128)(2,1)S(1)}, u32[]{:S(2)}, u32[]{:S(2)}) collective-permute-start(bf16[2,4,96,768]{3,2,1,0:T(8,128)(2,1)S(1)} %get-tuple-element.716), channel_id=1, source_target_pairs={{0,8},{4,12},{8,0},{12,4},{16,24},{20,28},{24,16},{28,20},{1,9},{5... | collective-permute-start | bytes 3538952 | tf_op jit(solution)/shard_map/ppermute | solution.py:30
  317.4 33.9 %collective-permute-start.40 = (bf16[2,4,4,96,768]{4,3,2,1,0:T(8,128)(2,1)}, bf16[2,4,4,96,768]{4,3,2,1,0:T(8,128)(2,1)}, u32[]{:S(2)}, u32[]{:S(2)}) collective-permute-start(bf16[2,4,4,96,768]{4,3,2,1,0:T(8,128)(2,1)} %get-tuple-element.520), channel_id=1, source_target_pairs={{0,4},{4,0},{8,12},{12,8},{16,20},{20,16},{24,28},{28,24},{1,5},{5... | collective-permute-start | bytes 14155784 | tf_op jit(solution)/shard_map/ppermute | solution.py:30
  322.1 28.2 %collective-permute-start.43 = (bf16[2,4,96,768]{3,2,1,0:T(8,128)(2,1)}, bf16[2,4,96,768]{3,2,1,0:T(8,128)(2,1)S(1)}, u32[]{:S(2)}, u32[]{:S(2)}) collective-permute-start(bf16[2,4,96,768]{3,2,1,0:T(8,128)(2,1)} %get-tuple-element.713), channel_id=1, source_target_pairs={{0,16},{4,20},{8,24},{12,28},{16,0},{20,4},{24,8},{28,12},{1,17},{... | collective-permute-start | bytes 3538952 | tf_op jit(solution)/shard_map/ppermute | solution.py:30
  323.7 27.6 %collective-permute-start.44 = (bf16[2,4,96,768]{3,2,1,0:T(8,128)(2,1)S(1)}, bf16[2,4,96,768]{3,2,1,0:T(8,128)(2,1)S(1)}, u32[]{:S(2)}, u32[]{:S(2)}) collective-permute-start(bf16[2,4,96,768]{3,2,1,0:T(8,128)(2,1)S(1)} %get-tuple-element.712), channel_id=1, source_target_pairs={{0,8},{4,12},{8,0},{12,4},{16,24},{20,28},{24,16},{28,20},{1,9},{5... | collective-permute-start | bytes 3538952 | tf_op jit(solution)/shard_map/ppermute | solution.py:30
  356.3 40.6 %collective-permute-start.45 = (bf16[2,4,96,768]{3,2,1,0:T(8,128)(2,1)}, bf16[2,4,96,768]{3,2,1,0:T(8,128)(2,1)S(1)}, u32[]{:S(2)}, u32[]{:S(2)}) collective-permute-start(bf16[2,4,96,768]{3,2,1,0:T(8,128)(2,1)} %get-tuple-element.711), channel_id=1, source_target_pairs={{0,16},{4,20},{8,24},{12,28},{16,0},{20,4},{24,8},{28,12},{1,17},{... | collective-permute-start | bytes 3538952 | tf_op jit(solution)/shard_map/ppermute | solution.py:30
  357.2 39.7 %collective-permute-start.46 = (bf16[2,4,96,768]{3,2,1,0:T(8,128)(2,1)}, bf16[2,4,96,768]{3,2,1,0:T(8,128)(2,1)}, u32[]{:S(2)}, u32[]{:S(2)}) collective-permute-start(bf16[2,4,96,768]{3,2,1,0:T(8,128)(2,1)} %get-tuple-element.710), channel_id=1, source_target_pairs={{0,8},{4,12},{8,0},{12,4},{16,24},{20,28},{24,16},{28,20},{1,9},{5... | collective-permute-start | bytes 3538952 | tf_op jit(solution)/shard_map/ppermute | solution.py:30
  361.4 35.5 %collective-permute-start.48 = (bf16[4,96,768]{2,1,0:T(8,128)(2,1)}, bf16[4,96,768]{2,1,0:T(8,128)(2,1)S(1)}, u32[]{:S(2)}, u32[]{:S(2)}) collective-permute-start(bf16[4,96,768]{2,1,0:T(8,128)(2,1)} %get-tuple-element.709), channel_id=1, source_target_pairs={{0,8},{4,12},{8,0},{12,4},{16,24},{20,28},{24,16},{28,20},{1,9},{5... | collective-permute-start | bytes 1769480 | tf_op jit(solution)/shard_map/ppermute | solution.py:30
  362.4 34.5 %collective-permute-start.49 = (bf16[4,96,768]{2,1,0:T(8,128)(2,1)}, bf16[4,96,768]{2,1,0:T(8,128)(2,1)S(1)}, u32[]{:S(2)}, u32[]{:S(2)}) collective-permute-start(bf16[4,96,768]{2,1,0:T(8,128)(2,1)} %get-tuple-element.708), channel_id=1, source_target_pairs={{0,16},{4,20},{8,24},{12,28},{16,0},{20,4},{24,8},{28,12},{1,17},{... | collective-permute-start | bytes 1769480 | tf_op jit(solution)/shard_map/ppermute | solution.py:30
  396.9 27.1 %collective-permute-start.54 = (bf16[2,4,4,64,768]{4,3,2,1,0:T(8,128)(2,1)}, bf16[2,4,4,64,768]{4,3,2,1,0:T(8,128)(2,1)}, u32[]{:S(2)}, u32[]{:S(2)}) collective-permute-start(bf16[2,4,4,64,768]{4,3,2,1,0:T(8,128)(2,1)} %get-tuple-element.582), channel_id=1, source_target_pairs={{0,4},{4,0},{8,12},{12,8},{16,20},{20,16},{24,28},{28,24},{1,5},{5... | collective-permute-start | bytes 9437192 | tf_op jit(solution)/shard_map/ppermute | solution.py:30
  427.3 26.6 %collective-permute-start.59 = (bf16[2,4,64,768]{3,2,1,0:T(8,128)(2,1)}, bf16[2,4,64,768]{3,2,1,0:T(8,128)(2,1)S(1)}, u32[]{:S(2)}, u32[]{:S(2)}) collective-permute-start(bf16[2,4,64,768]{3,2,1,0:T(8,128)(2,1)} %get-tuple-element.721), channel_id=1, source_target_pairs={{0,16},{4,20},{8,24},{12,28},{16,0},{20,4},{24,8},{28,12},{1,17},{... | collective-permute-start | bytes 2359304 | tf_op jit(solution)/shard_map/ppermute | solution.py:30
  482.9 27.4 %collective-permute-start.70 = (bf16[2,192,768]{2,1,0:T(8,128)(2,1)S(1)}, bf16[2,192,768]{2,1,0:T(8,128)(2,1)S(1)}, u32[]{:S(2)}, u32[]{:S(2)}) collective-permute-start(bf16[2,192,768]{2,1,0:T(8,128)(2,1)S(1)} %pad_maximum_fusion.15), channel_id=1, source_target_pairs={{0,8},{4,12},{8,0},{12,4},{16,24},{20,28},{24,16},{28,20},{1,9},{5... | collective-permute-start | bytes 1769480 | tf_op jit(solution)/shard_map/ppermute | solution.py:30
  483.7 26.6 %collective-permute-start.69 = (bf16[2,192,768]{2,1,0:T(8,128)(2,1)S(1)}, bf16[2,192,768]{2,1,0:T(8,128)(2,1)S(1)}, u32[]{:S(2)}, u32[]{:S(2)}) collective-permute-start(bf16[2,192,768]{2,1,0:T(8,128)(2,1)S(1)} %pad_maximum_fusion.14), channel_id=1, source_target_pairs={{0,16},{4,20},{8,24},{12,28},{16,0},{20,4},{24,8},{28,12},{1,17},{... | collective-permute-start | bytes 1769480 | tf_op jit(solution)/shard_map/ppermute | solution.py:30
  (115 other events, 1479.6 us)

commit v5 on v4

--- a/solution.py
+++ b/solution.py
@@ -763,7 +763,7 @@
     return jax.ShapeDtypeStruct(tuple(dims), kind)
 
 
-def call(kernel, ins, outs, scratch, aliases=None):
+def call(kernel, ins, outs, scratch, aliases=None, megabytes=60):
     return pl.pallas_call(
         kernel,
         in_specs=[spec for _, spec in ins],
@@ -771,7 +771,7 @@
         out_shape=[s for s, _ in outs],
         scratch_shapes=scratch,
         input_output_aliases=aliases or {},
-        compiler_params=pltpu.CompilerParams(vmem_limit_bytes=60 << 20),
+        compiler_params=pltpu.CompilerParams(vmem_limit_bytes=megabytes << 20),
         cost_estimate=pl.CostEstimate(flops=0, bytes_accessed=0, transcendentals=0),
     )(*[v for v, _ in ins])
 
@@ -889,6 +889,7 @@
             [(v, ANY) for v in arrays],
             [(v, VMEM) for v in outs],
             [pltpu.VMEM((2, mp, rows, width), BF16)] * 4 + [pltpu.SemaphoreType.DMA((4,))],
+            megabytes=12,
         )
         self.at[self.name] = {"own": parts[0], "parts": parts[1:]}
 

time: 562 us -> 553 us (0.984)
  local copies, waits for them, and re-layouts: 22 us -> 34.4 us
  other arithmetic: 50.5 us -> 39 us
    unnamed x122 -> x98, local copies, waits for them, and re-layouts: 8.57 us -> 20.4 us
    convert_element_type x15, other arithmetic: 33.7 us -> 23.8 us  [added(): return total.astype(BF16)]
  transfers between devices with their start and end apart: 84 -> 84, of which waited for: 30 -> 30; matrix products, arithmetic and copies ran while one was open for 8% -> 7% of each run, Pallas kernels for 30% -> 30%
where the time goes in v5:
time: 553 us; the launch traced here: 547 us
  Pallas kernels  192 us (35%)
  waiting for transfers between devices  186 us (34%)
  starting transfers between devices  93.5 us (17%)
  other arithmetic  39 us (7%)
  local copies, waits for them, and re-layouts  34.4 us (6%)
    pallas_call x20, Pallas kernels, call(): pl.pallas_call(kernel, in_specs=[spec for _, spec in ins], out_specs=[spe...  192 us
    ppermute x33, waiting for transfers between devices, pass_on(): lax.ppermute(values, 'mp', [(i, (i + way) % count) for i in range(count)])  131 us
    ppermute x33, starting transfers between devices, pass_on(): lax.ppermute(values, 'mp', [(i, (i + way) % count) for i in range(count)])  48.3 us
    ppermute x49, starting transfers between devices, swap(): return lax.ppermute(values, 'dp', [(i, i ^ bit) for i in range(count)])  43.7 us
    ppermute x49, waiting for transfers between devices, swap(): return lax.ppermute(values, 'dp', [(i, i ^ bit) for i in range(count)])  42.4 us
    convert_element_type x15, other arithmetic, added(): return total.astype(BF16)  23.8 us
    unnamed x98, local copies, waits for them, and re-layouts  20.4 us
    ppermute x2, waiting for transfers between devices, swap_owner(): return lax.ppermute(values, 'mp', [(i, i ^ bit) for i in range(count)])  12.4 us
  transfers between devices with their start and end apart: 84, of which 30 were waited for; matrix products, arithmetic and copies ran while one was open for 7% of the time, Pallas kernels for 30%

profile of v5, /device:TPU:0, one launch (start us, length us, event | category | flops | bytes accessed | tf_op | source)
XLA Modules:
  0.0 546.7 jit_solution(4852844006656446876)
XLA Ops:
  22.4 16.1 %collective-permute-done.1 = bf16[2,128,768]{2,1,0:T(8,128)(2,1)} collective-permute-done((bf16[2,128,768]{2,1,0:T(8,128)(2,1)}, bf16[2,128,768]{2,1,0:T(8,128)(2,1)}, u32[]{:S(2)}, u32[]{:S(2)}) %collective-permute-start.1) | collective-permute-done | bytes 393248 | tf_op jit(solution)/shard_map/ppermute | solution.py:35
  40.4 8.8 %collective-permute-start.5 = (bf16[2,144,768]{2,1,0:T(8,128)(2,1)}, bf16[2,144,768]{2,1,0:T(8,128)(2,1)S(1)}, u32[]{:S(2)}, u32[]{:S(2)}) collective-permute-start(bf16[2,144,768]{2,1,0:T(8,128)(2,1)} %get-tuple-element.366), channel_id=1, source_target_pairs={{0,1},{1,2},{2,3},{3,0},{4,5},{5,6},{6,7},{7,4},{8,9},{9,10},{10,1... | collective-permute-start | bytes 1327112 | tf_op jit(solution)/shard_map/ppermute | solution.py:35
  61.7 7.7 %collective-permute-done.6 = bf16[2,144,768]{2,1,0:T(8,128)(2,1)S(1)} collective-permute-done((bf16[2,144,768]{2,1,0:T(8,128)(2,1)}, bf16[2,144,768]{2,1,0:T(8,128)(2,1)S(1)}, u32[]{:S(2)}, u32[]{:S(2)}) %collective-permute-start.6) | collective-permute-done | bytes 442400 | tf_op jit(solution)/shard_map/ppermute | solution.py:35
  77.3 25.7 %collective-permute-done.10 = bf16[2,96,768]{2,1,0:T(8,128)(2,1)} collective-permute-done((bf16[2,96,768]{2,1,0:T(8,128)(2,1)S(1)}, bf16[2,96,768]{2,1,0:T(8,128)(2,1)}, u32[]{:S(2)}, u32[]{:S(2)}) %collective-permute-start.10) | collective-permute-done | bytes 294944 | tf_op jit(solution)/shard_map/ppermute | solution.py:35
  106.4 18.5 %collective-permute-done.15 = bf16[2,96,768]{2,1,0:T(8,128)(2,1)S(1)} collective-permute-done((bf16[2,96,768]{2,1,0:T(8,128)(2,1)S(1)}, bf16[2,96,768]{2,1,0:T(8,128)(2,1)S(1)}, u32[]{:S(2)}, u32[]{:S(2)}) %collective-permute-start.15) | collective-permute-done | bytes 294944 | tf_op jit(solution)/shard_map/ppermute | solution.py:35
  132.3 12.9 %shard_map.264 = (bf16[1280,768]{1,0:T(8,128)(2,1)}, bf16[1280,768]{1,0:T(8,128)(2,1)}, bf16[1280,768]{1,0:T(8,128)(2,1)}, bf16[768,1024]{1,0:T(8,128)(2,1)}) custom-call(s32[2]{0:T(128)} %pad_add_fusion.place, bf16[1280,1024]{1,0:T(8,128)(2,1)} %bitcast.145, bf16[192,1024]{1,0:T(8,128)(2,1)} %bitcast.155, bf16[3,3,192,768]{3,2,1,0:T(8,128)(2,1)} %bitcast.141, ...), custom_call_target="tpu_custom_call" | custom-call | tf_op jit(solution)/shard_map/pallas_call | solution.py:767
  145.3 7.8 %collective-permute-done.20 = bf16[2,96,768]{2,1,0:T(8,128)(2,1)} collective-permute-done((bf16[2,96,768]{2,1,0:T(8,128)(2,1)}, bf16[2,96,768]{2,1,0:T(8,128)(2,1)}, u32[]{:S(2)}, u32[]{:S(2)}) %collective-permute-start.20) | collective-permute-done | bytes 294944 | tf_op jit(solution)/shard_map/ppermute | solution.py:35
  153.1 7.3 %collective-permute-done.18 = bf16[2,3,144,768]{3,2,1,0:T(8,128)(2,1)} collective-permute-done((bf16[2,3,144,768]{3,2,1,0:T(8,128)(2,1)S(1)}, bf16[2,3,144,768]{3,2,1,0:T(8,128)(2,1)}, u32[]{:S(2)}, u32[]{:S(2)}) %collective-permute-start.18) | collective-permute-done | bytes 1327136 | tf_op jit(solution)/shard_map/ppermute | solution.py:30
  169.2 11.3 %shard_map.265 = (f32[320,768]{1,0:T(8,128)}, bf16[320,768]{1,0:T(8,128)(2,1)}, f32[320,768]{1,0:T(8,128)}, bf16[320,768]{1,0:T(8,128)(2,1)}, bf16[320,768]{1,0:...) custom-call(s32[2]{0:T(128)} %pad_add_fusion.place, ...), custom_call_target="tpu_custom_call" | custom-call | tf_op jit(solution)/shard_map/pallas_call | solution.py:767
  188.9 20.7 %shard_map.266 = (f32[320,768]{1,0:T(8,128)}, bf16[320,768]{1,0:T(8,128)(2,1)}, f32[320,768]{1,0:T(8,128)}, f32[4,320,768]{2,1,0:T(8,128)}, bf16[4,320,768]{2,1,...) custom-call(s32[2]{0:T(128)} %pad_add_fusion.place, ...), custom_call_target="tpu_custom_call" | custom-call | tf_op jit(solution)/shard_map/pallas_call | solution.py:767
  211.1 11.1 %shard_map.267 = (f32[320,768]{1,0:T(8,128)}, bf16[320,768]{1,0:T(8,128)(2,1)}, f32[320,768]{1,0:T(8,128)}, f32[320,768]{1,0:T(8,128)}, bf16[320,768]{1,0:T(8,128)(2,1)}, /*index=5*/bf16[4,768,768]{2,1,0:T(8,128)(2,1)}) custom-call(s32[2]{0:T(128)} %pad_add_fusion.place, f32[320,768]{1,0:T(8,128)} %get-tuple-element.440.rows_ref, ...), custom_call_target="tpu_custom_call" | custom-call | tf_op jit(solution)/shard_map/pallas_call | solution.py:767
  227.4 19.4 %shard_map.268 = (bf16[8,40,768]{2,1,0:T(8,128)(2,1)}, f32[320,768]{1,0:T(8,128)}, f32[8,768]{1,0:T(8,128)}, bf16[2,4,4,96,768]{4,3,2,1,0:T(8,128)(2,1)}, bf16[2,4,4,96,768]{4,3,2,1,0:T(8,128)(2,1)}) custom-call(s32[2]{0:T(128)} %pad_add_fusion.place, s32[8]{0:T(128)} %get-tuple-element.370.picks, f32[320,768]{1,0:T(8,128)} %get-tuple-element.448.rows_ref, ...), custom_call_target="tpu_custom_call" | custom-call | tf_op jit(solution)/shard_map/pallas_call | solution.py:767
  247.0 13.4 %shard_map.269 = (f32[320,768]{1,0:T(8,128)}, f32[8,768]{1,0:T(8,128)}, bf16[1280,768]{1,0:T(8,128)(2,1)}, bf16[1280,768]{1,0:T(8,128)(2,1)}, bf16[320,768]{1,0:T(8,128)(2,1)}, /*index=5*/bf16[320,768]{1,0:T(8,128)(2,1)}) custom-call(s32[2]{0:T(128)} %pad_add_fusion.place, f32[320,768]{1,0:T(8,128)} %get-tuple-element.459.grad, ...), custom_call_target="tpu_custom_call" | custom-call | tf_op jit(solution)/shard_map/pallas_call | solution.py:767
  270.6 13.5 %shard_map.270 = (f32[320,768]{1,0:T(8,128)}, f32[8,768]{1,0:T(8,128)}, bf16[2,4,4,96,768]{4,3,2,1,0:T(8,128)(2,1)}, bf16[2,4,4,96,768]{4,3,2,1,0:T(8,128)(2,1)}) custom-call(s32[2]{0:T(128)} %pad_add_fusion.place, f32[320,768]{1,0:T(8,128)} %get-tuple-element.469.grad, bf16[320,768]{1,0:T(8,128)(2,1)} %get-tuple-element.470.low, ...), custom_call_target="tpu_custom_call" | custom-call | tf_op jit(solution)/shard_map/pallas_call | solution.py:767
  284.1 10.0 %shard_map.271 = (bf16[2,4,4,96,768]{4,3,2,1,0:T(8,128)(2,1)}, bf16[2,4,4,96,768]{4,3,2,1,0:T(8,128)(2,1)}) custom-call(s32[2]{0:T(128)} %pad_add_fusion.place, bf16[320,768]{1,0:T(8,128)(2,1)} %get-tuple-element.463.context, bf16[320,768]{1,0:T(8,128)(2,1)} %get-tuple-element.480.branch, ...), custom_call_target="tpu_custom_call", output_to_operand_aliasing={{0}: (8, {}), {1}: (9, {})} | custom-call | tf_op jit(solution)/shard_map/pallas_call | solution.py:767
  299.6 17.6 %shard_map.272 = (f32[320,768]{1,0:T(8,128)}, f32[8,768]{1,0:T(8,128)}, bf16[2,4,4,96,768]{4,3,2,1,0:T(8,128)(2,1)}, bf16[2,4,4,96,768]{4,3,2,1,0:T(8,128)(2,1)}) custom-call(s32[2]{0:T(128)} %pad_add_fusion.place, f32[320,768]{1,0:T(8,128)} %get-tuple-element.491.grad_in, bf16[320,768]{1,0:T(8,128)(2,1)} %get-tuple-element.492.low_in, ...), custom_call_target="tpu_custom_call" | custom-call | tf_op jit(solution)/shard_map/pallas_call | solution.py:767
  336.5 13.3 %shard_map.273 = (bf16[8,40,768]{2,1,0:T(8,128)(2,1)}, f32[8,768]{1,0:T(8,128)}, bf16[2,4,4,64,768]{4,3,2,1,0:T(8,128)(2,1)}, bf16[2,4,4,64,768]{4,3,2,1,0:T(8,128)(2,1)}) custom-call(s32[2]{0:T(128)} %pad_add_fusion.place, f32[320,768]{1,0:T(8,128)} %get-tuple-element.511.grad, bf16[320,768]{1,0:T(8,128)(2,1)} %get-tuple-element.512.low, ...), custom_call_target="tpu_custom_call" | custom-call | tf_op jit(solution)/shard_map/pallas_call | solution.py:767
  368.7 18.2 %shard_map.275 = (f32[145,8,1024]{2,1,0:T(8,128)}, f32[8,768]{1,0:T(8,128)}, bf16[2,4,4,64,768]{4,3,2,1,0:T(8,128)(2,1)}, bf16[2,4,4,64,768]{4,3,2,1,0:T(8,128)(2,1)}) custom-call(s32[2]{0:T(128)} %pad_add_fusion.place, bf16[1280,1024]{1,0:T(8,128)(2,1)} %bitcast.146, ...), custom_call_target="tpu_custom_call", output_to_operand_aliasing={{2}: (6, {}), {3}: (7, {})} | custom-call | tf_op jit(solution)/shard_map/pallas_call | solution.py:767
  388.3 7.8 %collective-permute-done.48.two0 = bf16[4,96,768]{2,1,0:T(8,128)(2,1)S(1)} collective-permute-done((bf16[4,96,768]{2,1,0:T(8,128)(2,1)}, bf16[4,96,768]{2,1,0:T(8,128)(2,1)S(1)}, u32[]{:S(2)}, u32[]{:S(2)}) %collective-permute-start.48) | collective-permute-done | bytes 589856 | tf_op jit(solution)/shard_map/ppermute | solution.py:30
  409.4 13.4 %collective-permute-done.53 = bf16[2,96,768]{2,1,0:T(8,128)(2,1)S(1)} collective-permute-done((bf16[2,96,768]{2,1,0:T(8,128)(2,1)S(1)}, bf16[2,96,768]{2,1,0:T(8,128)(2,1)S(1)}, u32[]{:S(2)}, u32[]{:S(2)}) %collective-permute-start.53) | collective-permute-done | bytes 294944 | tf_op jit(solution)/shard_map/ppermute | solution.py:35
  464.4 8.2 %collective-permute-done.63 = bf16[192,768]{1,0:T(8,128)(2,1)S(1)} collective-permute-done((bf16[192,768]{1,0:T(8,128)(2,1)S(1)}, bf16[192,768]{1,0:T(8,128)(2,1)S(1)}, u32[]{:S(2)}, u32[]{:S(2)}) %collective-permute-start.63) | collective-permute-done | bytes 294944 | tf_op jit(solution)/shard_map/ppermute | solution.py:30
  483.5 12.8 %collective-permute-done.71 = f32[48,768]{1,0:T(8,128)S(1)} collective-permute-done((f32[48,768]{1,0:T(8,128)S(1)}, f32[48,768]{1,0:T(8,128)S(1)}, u32[]{:S(2)}, u32[]{:S(2)}) %collective-permute-start.71) | collective-permute-done | bytes 147488 | tf_op jit(solution)/shard_map/ppermute | solution.py:30
  508.6 12.4 %collective-permute-done.79 = f32[48,768]{1,0:T(8,128)} collective-permute-done((f32[48,768]{1,0:T(8,128)S(1)}, f32[48,768]{1,0:T(8,128)}, u32[]{:S(2)}, u32[]{:S(2)}) %collective-permute-start.79) | collective-permute-done | bytes 147488 | tf_op jit(solution)/shard_map/ppermute | solution.py:40
  525.1 6.3 %shard_map.281 = (f32[2,768,768]{2,1,0:T(8,128)}, f32[2,768,768]{2,1,0:T(8,128)}, f32[3,3,192,768]{3,2,1,0:T(8,128)}, f32[3,192,768]{2,1,0:T(8,128)}) custom-call(s32[2]{0:T(128)} %pad_add_fusion.place, bf16[2,4,192,768]{3,2,1,0:T(8,128)(2,1)} %copy-done.15, bf16[2,4,192,768]{3,2,1,0:T(8,128)(2,1)} %collective-permute-done.76.refs_1_), custom_call_target="tpu_custom_call" | custom-call | tf_op jit(solution)/shard_map/pallas_call | solution.py:767
  (371 shorter events, 230.2 us)
Async XLA Ops:
  10.1 28.4 %collective-permute-start.1 = (bf16[2,128,768]{2,1,0:T(8,128)(2,1)}, bf16[2,128,768]{2,1,0:T(8,128)(2,1)}, u32[]{:S(2)}, u32[]{:S(2)}) collective-permute-start(bf16[2,128,768]{2,1,0:T(8,128)(2,1)} %get-tuple-element.367), channel_id=1, source_target_pairs={{0,2},{1,3},{2,0},{3,1},{4,6},{5,7},{6,4},{7,5},{8,10},{9,11},{10,... | collective-permute-start | bytes 1179656 | tf_op jit(solution)/shard_map/ppermute | solution.py:35
  12.7 25.9 %collective-permute-start.2 = (bf16[2,128,768]{2,1,0:T(8,128)(2,1)}, bf16[2,128,768]{2,1,0:T(8,128)(2,1)S(1)}, u32[]{:S(2)}, u32[]{:S(2)}) collective-permute-start(bf16[2,128,768]{2,1,0:T(8,128)(2,1)} %get-tuple-element.367), channel_id=1, source_target_pairs={{0,3},{1,0},{2,1},{3,2},{4,7},{5,4},{6,5},{7,6},{8,11},{9,8},{10,9... | collective-permute-start | bytes 1179656 | tf_op jit(solution)/shard_map/ppermute | solution.py:35
  69.5 33.5 %collective-permute-start.8 = (bf16[2,3,112,768]{3,2,1,0:T(8,128)(2,1)S(1)}, bf16[2,3,112,768]{3,2,1,0:T(8,128)(2,1)S(1)}, u32[]{:S(2)}, u32[]{:S(2)}) collective-permute-start(bf16[2,3,112,768]{3,2,1,0:T(8,128)(2,1)S(1)} %pad_maximum_fusion.9), channel_id=1, source_target_pairs={{0,8},{4,12},{8,0},{12,4},{16,24},{20,28},{24,16},{28,20},{1,9},{5... | collective-permute-start | bytes 3096584 | tf_op jit(solution)/shard_map/ppermute | solution.py:30
  71.1 31.9 %collective-permute-start.7 = (bf16[2,3,112,768]{3,2,1,0:T(8,128)(2,1)S(1)}, bf16[2,3,112,768]{3,2,1,0:T(8,128)(2,1)S(1)}, u32[]{:S(2)}, u32[]{:S(2)}) collective-permute-start(bf16[2,3,112,768]{3,2,1,0:T(8,128)(2,1)S(1)} %pad_maximum_fusion.8), channel_id=1, source_target_pairs={{0,16},{4,20},{8,24},{12,28},{16,0},{20,4},{24,8},{28,12},{1,17},{... | collective-permute-start | bytes 3096584 | tf_op jit(solution)/shard_map/ppermute | solution.py:30
  72.7 30.3 %collective-permute-start.11 = (bf16[8,40,768]{2,1,0:T(8,128)(2,1)S(1)}, bf16[8,40,768]{2,1,0:T(8,128)(2,1)}, u32[]{:S(2)}, u32[]{:S(2)}) collective-permute-start(bf16[8,40,768]{2,1,0:T(8,128)(2,1)S(1)} %copy-done.22), channel_id=1, source_target_pairs={{0,1},{1,2},{2,3},{3,0},{4,5},{5,6},{6,7},{7,4},{8,9},{9,10},{10,1... | collective-permute-start | bytes 1474568 | tf_op jit(solution)/shard_map/ppermute | solution.py:35
  73.3 29.7 %collective-permute-start.9 = (bf16[2,144,768]{2,1,0:T(8,128)(2,1)S(1)}, bf16[2,144,768]{2,1,0:T(8,128)(2,1)S(1)}, u32[]{:S(2)}, u32[]{:S(2)}) collective-permute-start(bf16[2,144,768]{2,1,0:T(8,128)(2,1)S(1)} %collective-permute-done.5), channel_id=1, source_target_pairs={{0,1},{1,2},{2,3},{3,0},{4,5},{5,6},{6,7},{7,4},{8,9},{9,10},{10,1... | collective-permute-start | bytes 1327112 | tf_op jit(solution)/shard_map/ppermute | solution.py:35
  73.9 29.1 %collective-permute-start.10 = (bf16[2,96,768]{2,1,0:T(8,128)(2,1)S(1)}, bf16[2,96,768]{2,1,0:T(8,128)(2,1)}, u32[]{:S(2)}, u32[]{:S(2)}) collective-permute-start(bf16[2,96,768]{2,1,0:T(8,128)(2,1)S(1)} %copy-done.41), channel_id=1, source_target_pairs={{0,1},{1,2},{2,3},{3,0},{4,5},{5,6},{6,7},{7,4},{8,9},{9,10},{10,1... | collective-permute-start | bytes 884744 | tf_op jit(solution)/shard_map/ppermute | solution.py:35
  128.7 32.9 %collective-permute-start.19 = (bf16[2,2,3,144,768]{4,3,2,1,0:T(8,128)(2,1)S(1)}, bf16[2,2,3,144,768]{4,3,2,1,0:T(8,128)(2,1)}, u32[]{:S(2)}, u32[]{:S(2)}) collective-permute-start(bf16[2,2,3,144,768]{4,3,2,1,0:T(8,128)(2,1)S(1)} %pad_maximum_fusion.2.refs_0_.refs_4_), channel_id=1, source_target_pairs={{0,4},{4,0},{8,12},{12,8},{16,20},{20,16},{24,28},{28,24},{1,5},{5... | collective-permute-start | bytes 7962632 | tf_op jit(solution)/shard_map/ppermute | solution.py:30
  128.7 31.6 %collective-permute-start.18 = (bf16[2,3,144,768]{3,2,1,0:T(8,128)(2,1)S(1)}, bf16[2,3,144,768]{3,2,1,0:T(8,128)(2,1)}, u32[]{:S(2)}, u32[]{:S(2)}) collective-permute-start(bf16[2,3,144,768]{3,2,1,0:T(8,128)(2,1)S(1)} %get-tuple-element.725), channel_id=1, source_target_pairs={{0,8},{4,12},{8,0},{12,4},{16,24},{20,28},{24,16},{28,20},{1,9},{5... | collective-permute-start | bytes 3981320 | tf_op jit(solution)/shard_map/ppermute | solution.py:30
  130.1 31.5 %collective-permute-start.17 = (bf16[2,3,144,768]{3,2,1,0:T(8,128)(2,1)}, bf16[2,3,144,768]{3,2,1,0:T(8,128)(2,1)}, u32[]{:S(2)}, u32[]{:S(2)}) collective-permute-start(bf16[2,3,144,768]{3,2,1,0:T(8,128)(2,1)} %get-tuple-element.723), channel_id=1, source_target_pairs={{0,16},{4,20},{8,24},{12,28},{16,0},{20,4},{24,8},{28,12},{1,17},{... | collective-permute-start | bytes 3981320 | tf_op jit(solution)/shard_map/ppermute | solution.py:30
  184.0 25.6 %collective-permute-start.28 = (bf16[2,3,96,768]{3,2,1,0:T(8,128)(2,1)S(1)}, bf16[2,3,96,768]{3,2,1,0:T(8,128)(2,1)S(1)}, u32[]{:S(2)}, u32[]{:S(2)}) collective-permute-start(bf16[2,3,96,768]{3,2,1,0:T(8,128)(2,1)S(1)} %pad_maximum_fusion.11), channel_id=1, source_target_pairs={{0,8},{4,12},{8,0},{12,4},{16,24},{20,28},{24,16},{28,20},{1,9},{5... | collective-permute-start | bytes 2654216 | tf_op jit(solution)/shard_map/ppermute | solution.py:30
  266.8 27.7 %collective-permute-start.33 = (bf16[2,4,96,768]{3,2,1,0:T(8,128)(2,1)}, bf16[2,4,96,768]{3,2,1,0:T(8,128)(2,1)S(1)}, u32[]{:S(2)}, u32[]{:S(2)}) collective-permute-start(bf16[2,4,96,768]{3,2,1,0:T(8,128)(2,1)} %get-tuple-element.717), channel_id=1, source_target_pairs={{0,16},{4,20},{8,24},{12,28},{16,0},{20,4},{24,8},{28,12},{1,17},{... | collective-permute-start | bytes 3538952 | tf_op jit(solution)/shard_map/ppermute | solution.py:30
  268.5 27.2 %collective-permute-start.34 = (bf16[2,4,96,768]{3,2,1,0:T(8,128)(2,1)S(1)}, bf16[2,4,96,768]{3,2,1,0:T(8,128)(2,1)S(1)}, u32[]{:S(2)}, u32[]{:S(2)}) collective-permute-start(bf16[2,4,96,768]{3,2,1,0:T(8,128)(2,1)S(1)} %get-tuple-element.716), channel_id=1, source_target_pairs={{0,8},{4,12},{8,0},{12,4},{16,24},{20,28},{24,16},{28,20},{1,9},{5... | collective-permute-start | bytes 3538952 | tf_op jit(solution)/shard_map/ppermute | solution.py:30
  268.9 25.2 %collective-permute-start.35 = (bf16[8,40,768]{2,1,0:T(8,128)(2,1)S(1)}, bf16[8,40,768]{2,1,0:T(8,128)(2,1)}, u32[]{:S(2)}, u32[]{:S(2)}) collective-permute-start(bf16[8,40,768]{2,1,0:T(8,128)(2,1)S(1)} %copy-done.17), channel_id=1, source_target_pairs={{0,3},{1,0},{2,1},{3,2},{4,7},{5,4},{6,5},{7,6},{8,11},{9,8},{10,9... | collective-permute-start | bytes 1474568 | tf_op jit(solution)/shard_map/ppermute | solution.py:35
  317.3 34.2 %collective-permute-start.40 = (bf16[2,4,4,96,768]{4,3,2,1,0:T(8,128)(2,1)}, bf16[2,4,4,96,768]{4,3,2,1,0:T(8,128)(2,1)}, u32[]{:S(2)}, u32[]{:S(2)}) collective-permute-start(bf16[2,4,4,96,768]{4,3,2,1,0:T(8,128)(2,1)} %get-tuple-element.520), channel_id=1, source_target_pairs={{0,4},{4,0},{8,12},{12,8},{16,20},{20,16},{24,28},{28,24},{1,5},{5... | collective-permute-start | bytes 14155784 | tf_op jit(solution)/shard_map/ppermute | solution.py:30
  322.2 28.2 %collective-permute-start.43 = (bf16[2,4,96,768]{3,2,1,0:T(8,128)(2,1)}, bf16[2,4,96,768]{3,2,1,0:T(8,128)(2,1)S(1)}, u32[]{:S(2)}, u32[]{:S(2)}) collective-permute-start(bf16[2,4,96,768]{3,2,1,0:T(8,128)(2,1)} %get-tuple-element.713), channel_id=1, source_target_pairs={{0,16},{4,20},{8,24},{12,28},{16,0},{20,4},{24,8},{28,12},{1,17},{... | collective-permute-start | bytes 3538952 | tf_op jit(solution)/shard_map/ppermute | solution.py:30
  323.6 27.9 %collective-permute-start.44 = (bf16[2,4,96,768]{3,2,1,0:T(8,128)(2,1)}, bf16[2,4,96,768]{3,2,1,0:T(8,128)(2,1)S(1)}, u32[]{:S(2)}, u32[]{:S(2)}) collective-permute-start(bf16[2,4,96,768]{3,2,1,0:T(8,128)(2,1)} %get-tuple-element.712), channel_id=1, source_target_pairs={{0,8},{4,12},{8,0},{12,4},{16,24},{20,28},{24,16},{28,20},{1,9},{5... | collective-permute-start | bytes 3538952 | tf_op jit(solution)/shard_map/ppermute | solution.py:30
  355.9 40.1 %collective-permute-start.45 = (bf16[2,4,96,768]{3,2,1,0:T(8,128)(2,1)}, bf16[2,4,96,768]{3,2,1,0:T(8,128)(2,1)S(1)}, u32[]{:S(2)}, u32[]{:S(2)}) collective-permute-start(bf16[2,4,96,768]{3,2,1,0:T(8,128)(2,1)} %get-tuple-element.711), channel_id=1, source_target_pairs={{0,16},{4,20},{8,24},{12,28},{16,0},{20,4},{24,8},{28,12},{1,17},{... | collective-permute-start | bytes 3538952 | tf_op jit(solution)/shard_map/ppermute | solution.py:30
  356.6 39.4 %collective-permute-start.46 = (bf16[2,4,96,768]{3,2,1,0:T(8,128)(2,1)}, bf16[2,4,96,768]{3,2,1,0:T(8,128)(2,1)}, u32[]{:S(2)}, u32[]{:S(2)}) collective-permute-start(bf16[2,4,96,768]{3,2,1,0:T(8,128)(2,1)} %get-tuple-element.710), channel_id=1, source_target_pairs={{0,8},{4,12},{8,0},{12,4},{16,24},{20,28},{24,16},{28,20},{1,9},{5... | collective-permute-start | bytes 3538952 | tf_op jit(solution)/shard_map/ppermute | solution.py:30
  361.1 34.9 %collective-permute-start.48 = (bf16[4,96,768]{2,1,0:T(8,128)(2,1)}, bf16[4,96,768]{2,1,0:T(8,128)(2,1)S(1)}, u32[]{:S(2)}, u32[]{:S(2)}) collective-permute-start(bf16[4,96,768]{2,1,0:T(8,128)(2,1)} %get-tuple-element.709), channel_id=1, source_target_pairs={{0,8},{4,12},{8,0},{12,4},{16,24},{20,28},{24,16},{28,20},{1,9},{5... | collective-permute-start | bytes 1769480 | tf_op jit(solution)/shard_map/ppermute | solution.py:30
  361.8 34.3 %collective-permute-start.49 = (bf16[4,96,768]{2,1,0:T(8,128)(2,1)}, bf16[4,96,768]{2,1,0:T(8,128)(2,1)}, u32[]{:S(2)}, u32[]{:S(2)}) collective-permute-start(bf16[4,96,768]{2,1,0:T(8,128)(2,1)} %get-tuple-element.708), channel_id=1, source_target_pairs={{0,16},{4,20},{8,24},{12,28},{16,0},{20,4},{24,8},{28,12},{1,17},{... | collective-permute-start | bytes 1769480 | tf_op jit(solution)/shard_map/ppermute | solution.py:30
  396.1 26.8 %collective-permute-start.54 = (bf16[2,4,4,64,768]{4,3,2,1,0:T(8,128)(2,1)}, bf16[2,4,4,64,768]{4,3,2,1,0:T(8,128)(2,1)S(1)}, u32[]{:S(2)}, u32[]{:S(2)}) collective-permute-start(bf16[2,4,4,64,768]{4,3,2,1,0:T(8,128)(2,1)} %get-tuple-element.582), channel_id=1, source_target_pairs={{0,4},{4,0},{8,12},{12,8},{16,20},{20,16},{24,28},{28,24},{1,5},{5... | collective-permute-start | bytes 9437192 | tf_op jit(solution)/shard_map/ppermute | solution.py:30
  423.4 25.2 %collective-permute-start.59 = (bf16[2,4,64,768]{3,2,1,0:T(8,128)(2,1)S(1)}, bf16[2,4,64,768]{3,2,1,0:T(8,128)(2,1)S(1)}, u32[]{:S(2)}, u32[]{:S(2)}) collective-permute-start(bf16[2,4,64,768]{3,2,1,0:T(8,128)(2,1)S(1)} %get-tuple-element.721), channel_id=1, source_target_pairs={{0,16},{4,20},{8,24},{12,28},{16,0},{20,4},{24,8},{28,12},{1,17},{... | collective-permute-start | bytes 2359304 | tf_op jit(solution)/shard_map/ppermute | solution.py:30
  476.6 25.6 %collective-permute-start.70 = (bf16[2,192,768]{2,1,0:T(8,128)(2,1)S(1)}, bf16[2,192,768]{2,1,0:T(8,128)(2,1)S(1)}, u32[]{:S(2)}, u32[]{:S(2)}) collective-permute-start(bf16[2,192,768]{2,1,0:T(8,128)(2,1)S(1)} %pad_maximum_fusion.15), channel_id=1, source_target_pairs={{0,8},{4,12},{8,0},{12,4},{16,24},{20,28},{24,16},{28,20},{1,9},{5... | collective-permute-start | bytes 1769480 | tf_op jit(solution)/shard_map/ppermute | solution.py:30
  (103 other events, 1332.0 us)

commit v6 on v5

--- a/solution.py
+++ b/solution.py
@@ -332,8 +332,8 @@
     weights = first.at[:, pl.ds(0, 2 * rows + image_rows)]
     table = jnp.concatenate(
         [
-            head_bias[...].astype(F32),
-            jnp.zeros((head_bias.shape[0], width - quarter), F32),
+            jnp.concatenate([head_bias[i].astype(F32) for i in range(head_bias.shape[0])], axis=0),
+            jnp.zeros((6, width - quarter), F32),
         ],
         axis=1,
     )
@@ -989,7 +989,7 @@
     first, second, third = call(
         slice_kernel,
         [(place, SMEM)]
-        + [(v, VMEM) for v in (query_value_bias.reshape(6, quarter), feed_bias, image_bias.reshape(1, quarter))]
+        + [(v, VMEM) for v in (query_value_bias, feed_bias, image_bias.reshape(1, quarter))]
         + [(v, ANY) for v in (inward, attention_out, feed_in, feed_out, image)],
         [
             (shape((2, rows, width), BF16), VMEM)

time: 553 us -> 552 us (level)
  no operation moved by 1% of the time
where the time goes in v6:
time: 552 us; the launch traced here: 545 us
  Pallas kernels  192 us (35%)
  waiting for transfers between devices  186 us (34%)
  starting transfers between devices  93.5 us (17%)
  other arithmetic  39 us (7%)
  local copies, waits for them, and re-layouts  33.1 us (6%)
    pallas_call x20, Pallas kernels, call(): pl.pallas_call(kernel, in_specs=[spec for _, spec in ins], out_specs=[spe...  192 us
    ppermute x33, waiting for transfers between devices, pass_on(): lax.ppermute(values, 'mp', [(i, (i + way) % count) for i in range(count)])  131 us
    ppermute x33, starting transfers between devices, pass_on(): lax.ppermute(values, 'mp', [(i, (i + way) % count) for i in range(count)])  48.5 us
    ppermute x49, starting transfers between devices, swap(): return lax.ppermute(values, 'dp', [(i, i ^ bit) for i in range(count)])  43.4 us
    ppermute x49, waiting for transfers between devices, swap(): return lax.ppermute(values, 'dp', [(i, i ^ bit) for i in range(count)])  41.8 us
    convert_element_type x15, other arithmetic, added(): return total.astype(BF16)  23.8 us
    unnamed x98, local copies, waits for them, and re-layouts  20.4 us
    ppermute x2, waiting for transfers between devices, swap_owner(): return lax.ppermute(values, 'mp', [(i, i ^ bit) for i in range(count)])  12.4 us
  transfers between devices with their start and end apart: 84, of which 30 were waited for; matrix products, arithmetic and copies ran while one was open for 7% of the time, Pallas kernels for 30%

profile of v6, /device:TPU:0, one launch (start us, length us, event | category | flops | bytes accessed | tf_op | source)
XLA Modules:
  0.0 545.1 jit_solution(3748297150981529767)
XLA Ops:
  21.1 16.1 %collective-permute-done.1 = bf16[2,128,768]{2,1,0:T(8,128)(2,1)} collective-permute-done((bf16[2,128,768]{2,1,0:T(8,128)(2,1)}, bf16[2,128,768]{2,1,0:T(8,128)(2,1)}, u32[]{:S(2)}, u32[]{:S(2)}) %collective-permute-start.1) | collective-permute-done | bytes 393248 | tf_op jit(solution)/shard_map/ppermute | solution.py:35
  39.1 8.8 %collective-permute-start.5 = (bf16[2,144,768]{2,1,0:T(8,128)(2,1)}, bf16[2,144,768]{2,1,0:T(8,128)(2,1)S(1)}, u32[]{:S(2)}, u32[]{:S(2)}) collective-permute-start(bf16[2,144,768]{2,1,0:T(8,128)(2,1)} %get-tuple-element.366), channel_id=1, source_target_pairs={{0,1},{1,2},{2,3},{3,0},{4,5},{5,6},{6,7},{7,4},{8,9},{9,10},{10,1... | collective-permute-start | bytes 1327112 | tf_op jit(solution)/shard_map/ppermute | solution.py:35
  60.4 7.7 %collective-permute-done.6 = bf16[2,144,768]{2,1,0:T(8,128)(2,1)S(1)} collective-permute-done((bf16[2,144,768]{2,1,0:T(8,128)(2,1)}, bf16[2,144,768]{2,1,0:T(8,128)(2,1)S(1)}, u32[]{:S(2)}, u32[]{:S(2)}) %collective-permute-start.6) | collective-permute-done | bytes 442400 | tf_op jit(solution)/shard_map/ppermute | solution.py:35
  76.0 25.7 %collective-permute-done.10 = bf16[2,96,768]{2,1,0:T(8,128)(2,1)} collective-permute-done((bf16[2,96,768]{2,1,0:T(8,128)(2,1)S(1)}, bf16[2,96,768]{2,1,0:T(8,128)(2,1)}, u32[]{:S(2)}, u32[]{:S(2)}) %collective-permute-start.10) | collective-permute-done | bytes 294944 | tf_op jit(solution)/shard_map/ppermute | solution.py:35
  105.1 18.5 %collective-permute-done.15 = bf16[2,96,768]{2,1,0:T(8,128)(2,1)S(1)} collective-permute-done((bf16[2,96,768]{2,1,0:T(8,128)(2,1)S(1)}, bf16[2,96,768]{2,1,0:T(8,128)(2,1)S(1)}, u32[]{:S(2)}, u32[]{:S(2)}) %collective-permute-start.15) | collective-permute-done | bytes 294944 | tf_op jit(solution)/shard_map/ppermute | solution.py:35
  131.1 12.9 %shard_map.264 = (bf16[1280,768]{1,0:T(8,128)(2,1)}, bf16[1280,768]{1,0:T(8,128)(2,1)}, bf16[1280,768]{1,0:T(8,128)(2,1)}, bf16[768,1024]{1,0:T(8,128)(2,1)}) custom-call(s32[2]{0:T(128)} %pad_add_fusion.place, bf16[1280,1024]{1,0:T(8,128)(2,1)} %bitcast.145, bf16[192,1024]{1,0:T(8,128)(2,1)} %bitcast.155, bf16[3,3,192,768]{3,2,1,0:T(8,128)(2,1)} %bitcast.141, ...), custom_call_target="tpu_custom_call" | custom-call | tf_op jit(solution)/shard_map/pallas_call | solution.py:767
  144.0 7.8 %collective-permute-done.20 = bf16[2,96,768]{2,1,0:T(8,128)(2,1)} collective-permute-done((bf16[2,96,768]{2,1,0:T(8,128)(2,1)}, bf16[2,96,768]{2,1,0:T(8,128)(2,1)}, u32[]{:S(2)}, u32[]{:S(2)}) %collective-permute-start.20) | collective-permute-done | bytes 294944 | tf_op jit(solution)/shard_map/ppermute | solution.py:35
  151.8 7.3 %collective-permute-done.18 = bf16[2,3,144,768]{3,2,1,0:T(8,128)(2,1)} collective-permute-done((bf16[2,3,144,768]{3,2,1,0:T(8,128)(2,1)S(1)}, bf16[2,3,144,768]{3,2,1,0:T(8,128)(2,1)}, u32[]{:S(2)}, u32[]{:S(2)}) %collective-permute-start.18) | collective-permute-done | bytes 1327136 | tf_op jit(solution)/shard_map/ppermute | solution.py:30
  167.9 11.3 %shard_map.265 = (f32[320,768]{1,0:T(8,128)}, bf16[320,768]{1,0:T(8,128)(2,1)}, f32[320,768]{1,0:T(8,128)}, bf16[320,768]{1,0:T(8,128)(2,1)}, bf16[320,768]{1,0:...) custom-call(s32[2]{0:T(128)} %pad_add_fusion.place, ...), custom_call_target="tpu_custom_call" | custom-call | tf_op jit(solution)/shard_map/pallas_call | solution.py:767
  187.6 20.7 %shard_map.266 = (f32[320,768]{1,0:T(8,128)}, bf16[320,768]{1,0:T(8,128)(2,1)}, f32[320,768]{1,0:T(8,128)}, f32[4,320,768]{2,1,0:T(8,128)}, bf16[4,320,768]{2,1,...) custom-call(s32[2]{0:T(128)} %pad_add_fusion.place, ...), custom_call_target="tpu_custom_call" | custom-call | tf_op jit(solution)/shard_map/pallas_call | solution.py:767
  209.8 11.1 %shard_map.267 = (f32[320,768]{1,0:T(8,128)}, bf16[320,768]{1,0:T(8,128)(2,1)}, f32[320,768]{1,0:T(8,128)}, f32[320,768]{1,0:T(8,128)}, bf16[320,768]{1,0:T(8,128)(2,1)}, /*index=5*/bf16[4,768,768]{2,1,0:T(8,128)(2,1)}) custom-call(s32[2]{0:T(128)} %pad_add_fusion.place, f32[320,768]{1,0:T(8,128)} %get-tuple-element.440.rows_ref, ...), custom_call_target="tpu_custom_call" | custom-call | tf_op jit(solution)/shard_map/pallas_call | solution.py:767
  226.1 19.4 %shard_map.268 = (bf16[8,40,768]{2,1,0:T(8,128)(2,1)}, f32[320,768]{1,0:T(8,128)}, f32[8,768]{1,0:T(8,128)}, bf16[2,4,4,96,768]{4,3,2,1,0:T(8,128)(2,1)}, bf16[2,4,4,96,768]{4,3,2,1,0:T(8,128)(2,1)}) custom-call(s32[2]{0:T(128)} %pad_add_fusion.place, s32[8]{0:T(128)} %get-tuple-element.370.picks, f32[320,768]{1,0:T(8,128)} %get-tuple-element.448.rows_ref, ...), custom_call_target="tpu_custom_call" | custom-call | tf_op jit(solution)/shard_map/pallas_call | solution.py:767
  245.7 13.4 %shard_map.269 = (f32[320,768]{1,0:T(8,128)}, f32[8,768]{1,0:T(8,128)}, bf16[1280,768]{1,0:T(8,128)(2,1)}, bf16[1280,768]{1,0:T(8,128)(2,1)}, bf16[320,768]{1,0:T(8,128)(2,1)}, /*index=5*/bf16[320,768]{1,0:T(8,128)(2,1)}) custom-call(s32[2]{0:T(128)} %pad_add_fusion.place, f32[320,768]{1,0:T(8,128)} %get-tuple-element.459.grad, ...), custom_call_target="tpu_custom_call" | custom-call | tf_op jit(solution)/shard_map/pallas_call | solution.py:767
  269.3 13.5 %shard_map.270 = (f32[320,768]{1,0:T(8,128)}, f32[8,768]{1,0:T(8,128)}, bf16[2,4,4,96,768]{4,3,2,1,0:T(8,128)(2,1)}, bf16[2,4,4,96,768]{4,3,2,1,0:T(8,128)(2,1)}) custom-call(s32[2]{0:T(128)} %pad_add_fusion.place, f32[320,768]{1,0:T(8,128)} %get-tuple-element.469.grad, bf16[320,768]{1,0:T(8,128)(2,1)} %get-tuple-element.470.low, ...), custom_call_target="tpu_custom_call" | custom-call | tf_op jit(solution)/shard_map/pallas_call | solution.py:767
  282.8 10.0 %shard_map.271 = (bf16[2,4,4,96,768]{4,3,2,1,0:T(8,128)(2,1)}, bf16[2,4,4,96,768]{4,3,2,1,0:T(8,128)(2,1)}) custom-call(s32[2]{0:T(128)} %pad_add_fusion.place, bf16[320,768]{1,0:T(8,128)(2,1)} %get-tuple-element.463.context, bf16[320,768]{1,0:T(8,128)(2,1)} %get-tuple-element.480.branch, ...), custom_call_target="tpu_custom_call", output_to_operand_aliasing={{0}: (8, {}), {1}: (9, {})} | custom-call | tf_op jit(solution)/shard_map/pallas_call | solution.py:767
  298.3 17.6 %shard_map.272 = (f32[320,768]{1,0:T(8,128)}, f32[8,768]{1,0:T(8,128)}, bf16[2,4,4,96,768]{4,3,2,1,0:T(8,128)(2,1)}, bf16[2,4,4,96,768]{4,3,2,1,0:T(8,128)(2,1)}) custom-call(s32[2]{0:T(128)} %pad_add_fusion.place, f32[320,768]{1,0:T(8,128)} %get-tuple-element.491.grad_in, bf16[320,768]{1,0:T(8,128)(2,1)} %get-tuple-element.492.low_in, ...), custom_call_target="tpu_custom_call" | custom-call | tf_op jit(solution)/shard_map/pallas_call | solution.py:767
  335.1 13.3 %shard_map.273 = (bf16[8,40,768]{2,1,0:T(8,128)(2,1)}, f32[8,768]{1,0:T(8,128)}, bf16[2,4,4,64,768]{4,3,2,1,0:T(8,128)(2,1)}, bf16[2,4,4,64,768]{4,3,2,1,0:T(8,128)(2,1)}) custom-call(s32[2]{0:T(128)} %pad_add_fusion.place, f32[320,768]{1,0:T(8,128)} %get-tuple-element.511.grad, bf16[320,768]{1,0:T(8,128)(2,1)} %get-tuple-element.512.low, ...), custom_call_target="tpu_custom_call" | custom-call | tf_op jit(solution)/shard_map/pallas_call | solution.py:767
  367.5 18.2 %shard_map.275 = (f32[145,8,1024]{2,1,0:T(8,128)}, f32[8,768]{1,0:T(8,128)}, bf16[2,4,4,64,768]{4,3,2,1,0:T(8,128)(2,1)}, bf16[2,4,4,64,768]{4,3,2,1,0:T(8,128)(2,1)}) custom-call(s32[2]{0:T(128)} %pad_add_fusion.place, bf16[1280,1024]{1,0:T(8,128)(2,1)} %bitcast.146, ...), custom_call_target="tpu_custom_call", output_to_operand_aliasing={{2}: (6, {}), {3}: (7, {})} | custom-call | tf_op jit(solution)/shard_map/pallas_call | solution.py:767
  387.0 7.8 %collective-permute-done.48.two0 = bf16[4,96,768]{2,1,0:T(8,128)(2,1)S(1)} collective-permute-done((bf16[4,96,768]{2,1,0:T(8,128)(2,1)}, bf16[4,96,768]{2,1,0:T(8,128)(2,1)S(1)}, u32[]{:S(2)}, u32[]{:S(2)}) %collective-permute-start.48) | collective-permute-done | bytes 589856 | tf_op jit(solution)/shard_map/ppermute | solution.py:30
  408.0 13.4 %collective-permute-done.53 = bf16[2,96,768]{2,1,0:T(8,128)(2,1)S(1)} collective-permute-done((bf16[2,96,768]{2,1,0:T(8,128)(2,1)S(1)}, bf16[2,96,768]{2,1,0:T(8,128)(2,1)S(1)}, u32[]{:S(2)}, u32[]{:S(2)}) %collective-permute-start.53) | collective-permute-done | bytes 294944 | tf_op jit(solution)/shard_map/ppermute | solution.py:35
  463.0 8.2 %collective-permute-done.63 = bf16[192,768]{1,0:T(8,128)(2,1)S(1)} collective-permute-done((bf16[192,768]{1,0:T(8,128)(2,1)S(1)}, bf16[192,768]{1,0:T(8,128)(2,1)S(1)}, u32[]{:S(2)}, u32[]{:S(2)}) %collective-permute-start.63) | collective-permute-done | bytes 294944 | tf_op jit(solution)/shard_map/ppermute | solution.py:30
  482.2 12.6 %collective-permute-done.71 = f32[48,768]{1,0:T(8,128)S(1)} collective-permute-done((f32[48,768]{1,0:T(8,128)S(1)}, f32[48,768]{1,0:T(8,128)S(1)}, u32[]{:S(2)}, u32[]{:S(2)}) %collective-permute-start.71) | collective-permute-done | bytes 147488 | tf_op jit(solution)/shard_map/ppermute | solution.py:30
  507.2 12.4 %collective-permute-done.79 = f32[48,768]{1,0:T(8,128)} collective-permute-done((f32[48,768]{1,0:T(8,128)S(1)}, f32[48,768]{1,0:T(8,128)}, u32[]{:S(2)}, u32[]{:S(2)}) %collective-permute-start.79) | collective-permute-done | bytes 147488 | tf_op jit(solution)/shard_map/ppermute | solution.py:40
  523.7 6.3 %shard_map.281 = (f32[2,768,768]{2,1,0:T(8,128)}, f32[2,768,768]{2,1,0:T(8,128)}, f32[3,3,192,768]{3,2,1,0:T(8,128)}, f32[3,192,768]{2,1,0:T(8,128)}) custom-call(s32[2]{0:T(128)} %pad_add_fusion.place, bf16[2,4,192,768]{3,2,1,0:T(8,128)(2,1)} %copy-done.15, bf16[2,4,192,768]{3,2,1,0:T(8,128)(2,1)} %collective-permute-done.76.refs_1_), custom_call_target="tpu_custom_call" | custom-call | tf_op jit(solution)/shard_map/pallas_call | solution.py:767
  (370 shorter events, 228.8 us)
Async XLA Ops:
  8.8 28.4 %collective-permute-start.1 = (bf16[2,128,768]{2,1,0:T(8,128)(2,1)}, bf16[2,128,768]{2,1,0:T(8,128)(2,1)}, u32[]{:S(2)}, u32[]{:S(2)}) collective-permute-start(bf16[2,128,768]{2,1,0:T(8,128)(2,1)} %get-tuple-element.367), channel_id=1, source_target_pairs={{0,2},{1,3},{2,0},{3,1},{4,6},{5,7},{6,4},{7,5},{8,10},{9,11},{10,... | collective-permute-start | bytes 1179656 | tf_op jit(solution)/shard_map/ppermute | solution.py:35
  11.4 25.9 %collective-permute-start.2 = (bf16[2,128,768]{2,1,0:T(8,128)(2,1)}, bf16[2,128,768]{2,1,0:T(8,128)(2,1)S(1)}, u32[]{:S(2)}, u32[]{:S(2)}) collective-permute-start(bf16[2,128,768]{2,1,0:T(8,128)(2,1)} %get-tuple-element.367), channel_id=1, source_target_pairs={{0,3},{1,0},{2,1},{3,2},{4,7},{5,4},{6,5},{7,6},{8,11},{9,8},{10,9... | collective-permute-start | bytes 1179656 | tf_op jit(solution)/shard_map/ppermute | solution.py:35
  68.2 33.5 %collective-permute-start.8 = (bf16[2,3,112,768]{3,2,1,0:T(8,128)(2,1)S(1)}, bf16[2,3,112,768]{3,2,1,0:T(8,128)(2,1)S(1)}, u32[]{:S(2)}, u32[]{:S(2)}) collective-permute-start(bf16[2,3,112,768]{3,2,1,0:T(8,128)(2,1)S(1)} %pad_maximum_fusion.9), channel_id=1, source_target_pairs={{0,8},{4,12},{8,0},{12,4},{16,24},{20,28},{24,16},{28,20},{1,9},{5... | collective-permute-start | bytes 3096584 | tf_op jit(solution)/shard_map/ppermute | solution.py:30
  69.8 31.9 %collective-permute-start.7 = (bf16[2,3,112,768]{3,2,1,0:T(8,128)(2,1)S(1)}, bf16[2,3,112,768]{3,2,1,0:T(8,128)(2,1)S(1)}, u32[]{:S(2)}, u32[]{:S(2)}) collective-permute-start(bf16[2,3,112,768]{3,2,1,0:T(8,128)(2,1)S(1)} %pad_maximum_fusion.8), channel_id=1, source_target_pairs={{0,16},{4,20},{8,24},{12,28},{16,0},{20,4},{24,8},{28,12},{1,17},{... | collective-permute-start | bytes 3096584 | tf_op jit(solution)/shard_map/ppermute | solution.py:30
  71.5 30.3 %collective-permute-start.11 = (bf16[8,40,768]{2,1,0:T(8,128)(2,1)S(1)}, bf16[8,40,768]{2,1,0:T(8,128)(2,1)}, u32[]{:S(2)}, u32[]{:S(2)}) collective-permute-start(bf16[8,40,768]{2,1,0:T(8,128)(2,1)S(1)} %copy-done.22), channel_id=1, source_target_pairs={{0,1},{1,2},{2,3},{3,0},{4,5},{5,6},{6,7},{7,4},{8,9},{9,10},{10,1... | collective-permute-start | bytes 1474568 | tf_op jit(solution)/shard_map/ppermute | solution.py:35
  72.0 29.7 %collective-permute-start.9 = (bf16[2,144,768]{2,1,0:T(8,128)(2,1)S(1)}, bf16[2,144,768]{2,1,0:T(8,128)(2,1)S(1)}, u32[]{:S(2)}, u32[]{:S(2)}) collective-permute-start(bf16[2,144,768]{2,1,0:T(8,128)(2,1)S(1)} %collective-permute-done.5), channel_id=1, source_target_pairs={{0,1},{1,2},{2,3},{3,0},{4,5},{5,6},{6,7},{7,4},{8,9},{9,10},{10,1... | collective-permute-start | bytes 1327112 | tf_op jit(solution)/shard_map/ppermute | solution.py:35
  72.6 29.1 %collective-permute-start.10 = (bf16[2,96,768]{2,1,0:T(8,128)(2,1)S(1)}, bf16[2,96,768]{2,1,0:T(8,128)(2,1)}, u32[]{:S(2)}, u32[]{:S(2)}) collective-permute-start(bf16[2,96,768]{2,1,0:T(8,128)(2,1)S(1)} %copy-done.41), channel_id=1, source_target_pairs={{0,1},{1,2},{2,3},{3,0},{4,5},{5,6},{6,7},{7,4},{8,9},{9,10},{10,1... | collective-permute-start | bytes 884744 | tf_op jit(solution)/shard_map/ppermute | solution.py:35
  127.4 32.9 %collective-permute-start.19 = (bf16[2,2,3,144,768]{4,3,2,1,0:T(8,128)(2,1)S(1)}, bf16[2,2,3,144,768]{4,3,2,1,0:T(8,128)(2,1)}, u32[]{:S(2)}, u32[]{:S(2)}) collective-permute-start(bf16[2,2,3,144,768]{4,3,2,1,0:T(8,128)(2,1)S(1)} %pad_maximum_fusion.2.refs_0_.refs_4_), channel_id=1, source_target_pairs={{0,4},{4,0},{8,12},{12,8},{16,20},{20,16},{24,28},{28,24},{1,5},{5... | collective-permute-start | bytes 7962632 | tf_op jit(solution)/shard_map/ppermute | solution.py:30
  127.4 31.6 %collective-permute-start.18 = (bf16[2,3,144,768]{3,2,1,0:T(8,128)(2,1)S(1)}, bf16[2,3,144,768]{3,2,1,0:T(8,128)(2,1)}, u32[]{:S(2)}, u32[]{:S(2)}) collective-permute-start(bf16[2,3,144,768]{3,2,1,0:T(8,128)(2,1)S(1)} %get-tuple-element.725), channel_id=1, source_target_pairs={{0,8},{4,12},{8,0},{12,4},{16,24},{20,28},{24,16},{28,20},{1,9},{5... | collective-permute-start | bytes 3981320 | tf_op jit(solution)/shard_map/ppermute | solution.py:30
  128.8 31.5 %collective-permute-start.17 = (bf16[2,3,144,768]{3,2,1,0:T(8,128)(2,1)}, bf16[2,3,144,768]{3,2,1,0:T(8,128)(2,1)}, u32[]{:S(2)}, u32[]{:S(2)}) collective-permute-start(bf16[2,3,144,768]{3,2,1,0:T(8,128)(2,1)} %get-tuple-element.723), channel_id=1, source_target_pairs={{0,16},{4,20},{8,24},{12,28},{16,0},{20,4},{24,8},{28,12},{1,17},{... | collective-permute-start | bytes 3981320 | tf_op jit(solution)/shard_map/ppermute | solution.py:30
  182.7 25.6 %collective-permute-start.28 = (bf16[2,3,96,768]{3,2,1,0:T(8,128)(2,1)S(1)}, bf16[2,3,96,768]{3,2,1,0:T(8,128)(2,1)S(1)}, u32[]{:S(2)}, u32[]{:S(2)}) collective-permute-start(bf16[2,3,96,768]{3,2,1,0:T(8,128)(2,1)S(1)} %pad_maximum_fusion.11), channel_id=1, source_target_pairs={{0,8},{4,12},{8,0},{12,4},{16,24},{20,28},{24,16},{28,20},{1,9},{5... | collective-permute-start | bytes 2654216 | tf_op jit(solution)/shard_map/ppermute | solution.py:30
  265.5 27.7 %collective-permute-start.33 = (bf16[2,4,96,768]{3,2,1,0:T(8,128)(2,1)}, bf16[2,4,96,768]{3,2,1,0:T(8,128)(2,1)S(1)}, u32[]{:S(2)}, u32[]{:S(2)}) collective-permute-start(bf16[2,4,96,768]{3,2,1,0:T(8,128)(2,1)} %get-tuple-element.717), channel_id=1, source_target_pairs={{0,16},{4,20},{8,24},{12,28},{16,0},{20,4},{24,8},{28,12},{1,17},{... | collective-permute-start | bytes 3538952 | tf_op jit(solution)/shard_map/ppermute | solution.py:30
  267.1 27.2 %collective-permute-start.34 = (bf16[2,4,96,768]{3,2,1,0:T(8,128)(2,1)S(1)}, bf16[2,4,96,768]{3,2,1,0:T(8,128)(2,1)S(1)}, u32[]{:S(2)}, u32[]{:S(2)}) collective-permute-start(bf16[2,4,96,768]{3,2,1,0:T(8,128)(2,1)S(1)} %get-tuple-element.716), channel_id=1, source_target_pairs={{0,8},{4,12},{8,0},{12,4},{16,24},{20,28},{24,16},{28,20},{1,9},{5... | collective-permute-start | bytes 3538952 | tf_op jit(solution)/shard_map/ppermute | solution.py:30
  267.6 25.2 %collective-permute-start.35 = (bf16[8,40,768]{2,1,0:T(8,128)(2,1)S(1)}, bf16[8,40,768]{2,1,0:T(8,128)(2,1)}, u32[]{:S(2)}, u32[]{:S(2)}) collective-permute-start(bf16[8,40,768]{2,1,0:T(8,128)(2,1)S(1)} %copy-done.17), channel_id=1, source_target_pairs={{0,3},{1,0},{2,1},{3,2},{4,7},{5,4},{6,5},{7,6},{8,11},{9,8},{10,9... | collective-permute-start | bytes 1474568 | tf_op jit(solution)/shard_map/ppermute | solution.py:35
  316.0 34.1 %collective-permute-start.40 = (bf16[2,4,4,96,768]{4,3,2,1,0:T(8,128)(2,1)}, bf16[2,4,4,96,768]{4,3,2,1,0:T(8,128)(2,1)}, u32[]{:S(2)}, u32[]{:S(2)}) collective-permute-start(bf16[2,4,4,96,768]{4,3,2,1,0:T(8,128)(2,1)} %get-tuple-element.520), channel_id=1, source_target_pairs={{0,4},{4,0},{8,12},{12,8},{16,20},{20,16},{24,28},{28,24},{1,5},{5... | collective-permute-start | bytes 14155784 | tf_op jit(solution)/shard_map/ppermute | solution.py:30
  321.0 28.2 %collective-permute-start.43 = (bf16[2,4,96,768]{3,2,1,0:T(8,128)(2,1)}, bf16[2,4,96,768]{3,2,1,0:T(8,128)(2,1)S(1)}, u32[]{:S(2)}, u32[]{:S(2)}) collective-permute-start(bf16[2,4,96,768]{3,2,1,0:T(8,128)(2,1)} %get-tuple-element.713), channel_id=1, source_target_pairs={{0,16},{4,20},{8,24},{12,28},{16,0},{20,4},{24,8},{28,12},{1,17},{... | collective-permute-start | bytes 3538952 | tf_op jit(solution)/shard_map/ppermute | solution.py:30
  322.2 27.9 %collective-permute-start.44 = (bf16[2,4,96,768]{3,2,1,0:T(8,128)(2,1)}, bf16[2,4,96,768]{3,2,1,0:T(8,128)(2,1)S(1)}, u32[]{:S(2)}, u32[]{:S(2)}) collective-permute-start(bf16[2,4,96,768]{3,2,1,0:T(8,128)(2,1)} %get-tuple-element.712), channel_id=1, source_target_pairs={{0,8},{4,12},{8,0},{12,4},{16,24},{20,28},{24,16},{28,20},{1,9},{5... | collective-permute-start | bytes 3538952 | tf_op jit(solution)/shard_map/ppermute | solution.py:30
  354.6 40.2 %collective-permute-start.45 = (bf16[2,4,96,768]{3,2,1,0:T(8,128)(2,1)}, bf16[2,4,96,768]{3,2,1,0:T(8,128)(2,1)S(1)}, u32[]{:S(2)}, u32[]{:S(2)}) collective-permute-start(bf16[2,4,96,768]{3,2,1,0:T(8,128)(2,1)} %get-tuple-element.711), channel_id=1, source_target_pairs={{0,16},{4,20},{8,24},{12,28},{16,0},{20,4},{24,8},{28,12},{1,17},{... | collective-permute-start | bytes 3538952 | tf_op jit(solution)/shard_map/ppermute | solution.py:30
  355.3 39.4 %collective-permute-start.46 = (bf16[2,4,96,768]{3,2,1,0:T(8,128)(2,1)}, bf16[2,4,96,768]{3,2,1,0:T(8,128)(2,1)}, u32[]{:S(2)}, u32[]{:S(2)}) collective-permute-start(bf16[2,4,96,768]{3,2,1,0:T(8,128)(2,1)} %get-tuple-element.710), channel_id=1, source_target_pairs={{0,8},{4,12},{8,0},{12,4},{16,24},{20,28},{24,16},{28,20},{1,9},{5... | collective-permute-start | bytes 3538952 | tf_op jit(solution)/shard_map/ppermute | solution.py:30
  359.7 35.0 %collective-permute-start.48 = (bf16[4,96,768]{2,1,0:T(8,128)(2,1)}, bf16[4,96,768]{2,1,0:T(8,128)(2,1)S(1)}, u32[]{:S(2)}, u32[]{:S(2)}) collective-permute-start(bf16[4,96,768]{2,1,0:T(8,128)(2,1)} %get-tuple-element.709), channel_id=1, source_target_pairs={{0,8},{4,12},{8,0},{12,4},{16,24},{20,28},{24,16},{28,20},{1,9},{5... | collective-permute-start | bytes 1769480 | tf_op jit(solution)/shard_map/ppermute | solution.py:30
  360.5 34.3 %collective-permute-start.49 = (bf16[4,96,768]{2,1,0:T(8,128)(2,1)}, bf16[4,96,768]{2,1,0:T(8,128)(2,1)}, u32[]{:S(2)}, u32[]{:S(2)}) collective-permute-start(bf16[4,96,768]{2,1,0:T(8,128)(2,1)} %get-tuple-element.708), channel_id=1, source_target_pairs={{0,16},{4,20},{8,24},{12,28},{16,0},{20,4},{24,8},{28,12},{1,17},{... | collective-permute-start | bytes 1769480 | tf_op jit(solution)/shard_map/ppermute | solution.py:30
  394.8 26.6 %collective-permute-start.54 = (bf16[2,4,4,64,768]{4,3,2,1,0:T(8,128)(2,1)}, bf16[2,4,4,64,768]{4,3,2,1,0:T(8,128)(2,1)S(1)}, u32[]{:S(2)}, u32[]{:S(2)}) collective-permute-start(bf16[2,4,4,64,768]{4,3,2,1,0:T(8,128)(2,1)} %get-tuple-element.582), channel_id=1, source_target_pairs={{0,4},{4,0},{8,12},{12,8},{16,20},{20,16},{24,28},{28,24},{1,5},{5... | collective-permute-start | bytes 9437192 | tf_op jit(solution)/shard_map/ppermute | solution.py:30
  422.0 25.3 %collective-permute-start.59 = (bf16[2,4,64,768]{3,2,1,0:T(8,128)(2,1)S(1)}, bf16[2,4,64,768]{3,2,1,0:T(8,128)(2,1)S(1)}, u32[]{:S(2)}, u32[]{:S(2)}) collective-permute-start(bf16[2,4,64,768]{3,2,1,0:T(8,128)(2,1)S(1)} %get-tuple-element.721), channel_id=1, source_target_pairs={{0,16},{4,20},{8,24},{12,28},{16,0},{20,4},{24,8},{28,12},{1,17},{... | collective-permute-start | bytes 2359304 | tf_op jit(solution)/shard_map/ppermute | solution.py:30
  475.3 25.3 %collective-permute-start.70 = (bf16[2,192,768]{2,1,0:T(8,128)(2,1)S(1)}, bf16[2,192,768]{2,1,0:T(8,128)(2,1)S(1)}, u32[]{:S(2)}, u32[]{:S(2)}) collective-permute-start(bf16[2,192,768]{2,1,0:T(8,128)(2,1)S(1)} %pad_maximum_fusion.15), channel_id=1, source_target_pairs={{0,8},{4,12},{8,0},{12,4},{16,24},{20,28},{24,16},{28,20},{1,9},{5... | collective-permute-start | bytes 1769480 | tf_op jit(solution)/shard_map/ppermute | solution.py:30
  (103 other events, 1332.8 us)
